TPU v7x, 32 devices: a whole 2x2x4 slice. The times are simulated.
32 devices in a mesh: grp: 2 (over y), col: 8 (over z, x), row: 2 (over core).
Axes of the slice: x: 2, y: 2, z: 4, core: 2. Of those that a mesh axis runs over, the one named last changes fastest.
Arguments:
- left_bounds: bfloat16 [4, 8, 128, 8, 128], P(('grp', 'row'), 'col'), parts along dimension 0, may hold values from -0.1875 to 0.1875
- right_bounds: bfloat16 [4, 8, 128, 8, 128], P(('grp', 'row'), 'col'), parts along dimension 0, may hold values from -0.1875 to 0.1875
- site_tensors: bfloat16 [4, 8, 2, 4096], P(('grp', 'row'), 'col'), parts along dimension 0, may hold values from -2 to 2
- configuration: int32 [4, 8], P(('grp', 'row'), 'col'), parts along dimension 0, may hold values from 0 to 1
- top_env: bfloat16 [16, 128, 8, 128], P(('grp', 'col')), parts along dimension 0, may hold values from -6 to 6
- bottom_env: bfloat16 [16, 128, 8, 128], P(('grp', 'col')), parts along dimension 0, may hold values from -6 to 6
- sketch: bfloat16 [1024, 128], replicated, may hold values from -0.1875 to 0.1875
Outputs:
- gradient: float32 [4, 8, 2, 4096], P(('grp', 'row'), 'col'), parts along dimension 0
- left_updated: bfloat16 [4, 8, 128, 8, 128], P(('grp', 'row'), 'col'), parts along dimension 0
- right_updated: bfloat16 [4, 8, 128, 8, 128], P(('grp', 'row'), 'col'), parts along dimension 0
There are 2 independent parts, one for each index of `grp`. A program takes and returns all parts, laid end to end along the dimension named above; an argument that names none is the same for every part. Nothing has to cross between parts.
All inputs are finite; a program needn't handle non-finite values.
Results may differ from a plain program's by a relative error of at most 0.015.
Values may be sent and summed in bfloat16 or wider, within the bound.
No kernel may reach another device: no remote copies, remote signals or barrier semaphores. Data moves between devices by JAX's collectives and lax.ppermute only.
A program may use at most 64 MiB of HBM per device.

v0:
```python
import functools

import jax
import jax.numpy as jnp
from jax import lax
from jax.experimental import pallas as pl
from jax.experimental.pallas import tpu as pltpu
from jax.sharding import PartitionSpec as P

F32 = jnp.float32
BF16 = jnp.bfloat16
VMEM_BYTES = 48 * 1024 * 1024


def nn(a, b):
    return jnp.dot(a, b, preferred_element_type=F32)


def nt(a, b):
    return lax.dot_general(a, b, (((1,), (1,)), ((), ())), preferred_element_type=F32)


def split(x):
    high = x.astype(BF16)
    return high, (x - high.astype(F32)).astype(BF16)


def iota(shape, axis):
    return lax.broadcasted_iota(jnp.int32, shape, axis)


def chol_inverse(grams):
    n = grams[0].shape[0]
    blocks = n // 8
    count = len(grams)
    lane = iota((8, n), 1)
    sub = iota((8, n), 0)
    at = [sub == j for j in range(8)]
    after = [sub > j for j in range(8)]
    tiles = [[g[8 * i : 8 * i + 8, :] for i in range(blocks)] for g in grams]

    def over_lanes(x, j):
        return jnp.broadcast_to(x[:, j : j + 1], (8, n))

    def over_rows(x, j):
        return jnp.broadcast_to(x[j : j + 1, :], (8, n))

    for b in range(blocks):
        own = (lane >= 8 * b) & (lane < 8 * b + 8)
        eye = jnp.where(lane - 8 * b == sub, 1.0, 0.0)
        diag = [[over_lanes(tiles[q][b], 8 * b + j) for j in range(8)] for q in range(count)]
        below = [
            [[over_lanes(tiles[q][i], 8 * b + j) for j in range(8)] for i in range(b + 1, blocks)]
            for q in range(count)
        ]
        forward = [jnp.where(own, eye, tiles[q][b]) for q in range(count)]
        full = list(forward)
        pivots = [jnp.ones((8, n), F32) for _ in range(count)]
        for j in range(8):
            for q in range(count):
                c = diag[q]
                pivot = over_rows(c[j], j)
                inverse = 1.0 / pivot
                pivots[q] = jnp.where(at[j], pivot, pivots[q])
                for k in range(j + 1, 8):
                    m = over_rows(c[k], j) * inverse
                    c[k] = jnp.where(at[j], m, c[k] - c[j] * m)
                row = over_rows(forward[q], j) * inverse
                forward[q] = jnp.where(after[j], forward[q] - c[j] * row, forward[q])
                full[q] = jnp.where(at[j], row, full[q] - c[j] * row)
        for q in range(count):
            rows = [over_rows(full[q], j) for j in range(8)]
            for i in range(b + 1, blocks):
                terms = [below[q][i - b - 1][j] * rows[j] for j in range(8)]
                while len(terms) > 1:
                    terms = [x + y for x, y in zip(terms[::2], terms[1::2])]
                tiles[q][i] = jnp.where(own, 0.0, tiles[q][i]) - terms[0]
            tiles[q][b] = jnp.where(lane <= sub + 8 * b, forward[q] * lax.rsqrt(pivots[q]), 0.0)
    return [jnp.concatenate(t, axis=0) for t in tiles]


def leg(scratch, j):
    chi = scratch.shape[1]
    return scratch[pl.ds(j, chi, stride=scratch.shape[0] // chi), :]


def to_kron(lhs, rhs, x_ref, transposed):
    chi = lhs.shape[1]
    bond = lhs.shape[0] // chi
    groups = chi // 8
    for t in range(0, bond, 2):
        if transposed:
            product = nt(lhs[...], rhs[t * chi : (t + 2) * chi, :])
        else:
            product = nn(lhs[...], rhs[:, t * chi : (t + 2) * chi])
        for s in range(bond):
            at = (s * bond + t) * 8
            for g in range(groups):
                rows = product[s * chi + g * 8 : s * chi + g * 8 + 8, :]
                x_ref[at : at + 16, g * chi : (g + 1) * chi] = jnp.concatenate(
                    [rows[:, :chi], rows[:, chi:]], axis=0
                ).astype(BF16)


def absorb(kron, x_ref, m_ref, bond):
    chi = m_ref.shape[0] // bond
    for g in range(0, chi // 8, 2):
        out = nn(kron, x_ref[:, g * chi : (g + 2) * chi])
        for o in range(bond):
            for d in range(bond):
                rows = out[(o * bond + d) * 8 : (o * bond + d) * 8 + 8, :]
                at = o * chi + g * 8
                m_ref[at : at + 16, d * chi : (d + 1) * chi] = jnp.concatenate(
                    [rows[:, :chi], rows[:, chi:]], axis=0
                ).astype(BF16)


def square_core(flat):
    half = flat.shape[1] // 2
    size = flat.shape[0] * 2
    i = iota((size, flat.shape[0]), 0)
    j = iota((size, flat.shape[0]), 1)
    even = jnp.where(i == 2 * j, 1.0, 0.0).astype(BF16)
    odd = jnp.where(i == 2 * j + 1, 1.0, 0.0).astype(BF16)
    return (nn(even, flat[:, :half]) + nn(odd, flat[:, half:])).astype(BF16)


def swap_order(size, bond):
    i = iota((size, size), 0)
    j = iota((size, size), 1)
    hit = (i // bond == j % bond) & (i % bond == j // bond)
    return jnp.where(hit, 1.0, 0.0).astype(BF16)


def spread(size):
    i = iota((size * 8, size), 0)
    j = iota((size * 8, size), 1)
    return jnp.where(i // 8 == j, 1.0, 0.0).astype(BF16)


def kron_of(spread_rows, size):
    wide = nt(spread_rows.astype(BF16), spread(size))
    i = iota(wide.shape, 0)
    j = iota(wide.shape, 1)
    return jnp.where(i % 8 == j % 8, wide, 0.0).astype(BF16)


def kron_ahead(core, bond):
    size = core.shape[0]
    permuted = nn(swap_order(size, bond), core).astype(BF16)
    return kron_of(nt(spread(size), permuted), size)


def kron_back(core, bond):
    size = core.shape[0]
    permuted = nn(core, swap_order(size, bond)).astype(BF16)
    return kron_of(nn(spread(size), permuted), size)


def kron_mirrored(core, bond):
    size = core.shape[0]
    i = iota((size, size), 0)
    j = iota((size, size), 1)
    total = jnp.zeros((size, size), F32)
    for u in range(bond):
        pick = jnp.where(j == (i // bond) * bond + u, 1.0, 0.0).astype(BF16)
        picked = jnp.where(i % bond == j % bond, nn(pick, core), 0.0).astype(BF16)
        place = jnp.where(j == u * bond + i // bond, 1.0, 0.0).astype(BF16)
        total = total + nn(picked, place)
    return kron_of(nn(spread(size), total.astype(BF16)), size)


def edges_kernel(
    top, bottom, sketch, sites, choice, basis, edge, first, sketch_t, core, wide, legs_top, legs_bottom
):
    side = lax.axis_index("row")
    chi = top.shape[1]
    bond = top.shape[0] // chi
    for env, legs, mine in ((top, legs_top, 0), (bottom, legs_bottom, 1)):
        wide[...] = env[...].astype(F32)

        @pl.when(side == 0)
        def _():
            for u in range(bond):
                block = leg(wide, u).T.astype(BF16)
                legs[:, u * chi : (u + 1) * chi] = block
                if mine == 0:
                    first[u * chi : (u + 1) * chi, :] = block

        @pl.when(side == 1)
        def _():
            for u in range(bond):
                block = leg(wide, u).astype(BF16)
                legs[:, u * chi : (u + 1) * chi] = block
                if mine == 1:
                    first[u * chi : (u + 1) * chi, :] = block

    wide[...] = sketch[...].astype(F32)
    for o in range(bond):
        sketch_t[:, o * chi : (o + 1) * chi] = leg(wide, o).T.astype(BF16)
    phys = sites.shape[0]
    chosen = jnp.zeros((1, sites.shape[1]), F32)
    for p in range(phys):
        chosen = chosen + jnp.where(choice[0, 0] == p, sites[p : p + 1, :].astype(F32), 0.0)
    lanes = core.shape[1]
    core[...] = jnp.concatenate(
        [chosen[:, i * lanes : (i + 1) * lanes] for i in range(core.shape[0])], axis=0
    ).astype(BF16)
    inverse_top, inverse_bottom = chol_inverse(
        [nt(legs_top[...], legs_top[...]), nt(legs_bottom[...], legs_bottom[...])]
    )
    high, low = split(inverse_top)
    ortho = (nn(high, legs_top[...]) + nn(low, legs_top[...])).astype(BF16)
    for u in range(bond):
        basis[u * chi : (u + 1) * chi, :] = ortho[:, u * chi : (u + 1) * chi]
    high, low = split(inverse_bottom)
    edge[...] = (nn(high, legs_bottom[...]) + nn(low, legs_bottom[...])).astype(BF16)


def begin_kernel(
    first, western, eastern, core, x_out, back, carried, wide_w, wide_e, ahead, behind, kron, middle
):
    side = lax.axis_index("row")
    chi = first.shape[1]
    bond = first.shape[0] // chi
    wide_w[...] = western[...].astype(F32)
    wide_e[...] = eastern[...].astype(F32)

    @pl.when(side == 0)
    def _():
        for j in range(bond):
            at = slice(j * chi, (j + 1) * chi)
            east = leg(wide_e, j)
            ahead[:, at] = leg(wide_w, j).astype(BF16)
            behind[:, at] = east.T.astype(BF16)
            back[at, :] = east.astype(BF16)
        kron[...] = kron_ahead(square_core(core[...]), bond)

    @pl.when(side == 1)
    def _():
        for j in range(bond):
            at = slice(j * chi, (j + 1) * chi)
            west = leg(wide_w, j)
            ahead[:, at] = leg(wide_e, j).T.astype(BF16)
            behind[:, at] = west.astype(BF16)
            back[at, :] = west.T.astype(BF16)
        kron[...] = kron_back(square_core(core[...]), bond)

    to_kron(first, ahead, x_out, False)
    absorb(kron[...], x_out, middle, bond)
    state = nn(behind[...], middle[...]).astype(BF16)
    for s in range(bond):
        carried[s * chi : (s + 1) * chi, :] = state[:, s * chi : (s + 1) * chi]


def rows_kernel(
    basis,
    edge,
    sketch_t,
    western,
    eastern,
    swapped,
    core_own,
    core_other,
    keep,
    send,
    wide_0,
    wide_1,
    lanes,
    kron,
    x,
    absorbed,
    next_basis,
):
    side = lax.axis_index("row")
    chi = basis.shape[1]
    bond = basis.shape[0] // chi

    @pl.when(side == 0)
    def _():
        wide_0[...] = western[...].astype(F32)
        wide_1[...] = swapped[...].astype(F32)
        kron[0] = kron_ahead(square_core(core_own[...]), bond)
        kron[1] = kron_ahead(square_core(core_other[...]), bond)

    @pl.when(side == 1)
    def _():
        wide_0[...] = swapped[...].astype(F32)
        wide_1[...] = eastern[...].astype(F32)
        kron[0] = kron_mirrored(square_core(core_other[...]), bond)
        kron[1] = kron_mirrored(square_core(core_own[...]), bond)

    def project(frame, wide, row):
        for k in range(bond):
            lanes[:, k * chi : (k + 1) * chi] = leg(wide, k).astype(BF16)
        to_kron(frame, lanes, x, False)
        absorb(kron[row], x, absorbed, bond)

    def finish(closing, wide, row):
        unscaled = nt(absorbed[...], closing)
        mean = jnp.sum(unscaled * unscaled) * (1.0 / (unscaled.shape[0] * unscaled.shape[1]))
        scaled = unscaled * lax.rsqrt(mean + 1e-06)
        for o in range(bond):
            wide[pl.ds(o, chi, stride=bond), :] = scaled[o * chi : (o + 1) * chi, :]
        new = wide[...].astype(BF16)

        @pl.when(side == row)
        def _():
            keep[...] = new

        @pl.when(side != row)
        def _():
            send[...] = new

    project(basis, wide_0, 0)
    sketched = nn(sketch_t[...], absorbed[...])
    high, low = split(sketched)
    gram = nt(high, high) + (nt(high, low) + nt(low, high))
    (inverse,) = chol_inverse([gram])
    inverse_high, inverse_low = split(inverse)
    closing = (
        nn(inverse_high, high) + (nn(inverse_high, low) + nn(inverse_low, high))
    ).astype(BF16)
    for d in range(bond):
        next_basis[d * chi : (d + 1) * chi, :] = closing[:, d * chi : (d + 1) * chi]
    finish(closing, wide_0, 0)
    project(next_basis, wide_1, 1)
    finish(edge[...], wide_1, 1)


def gradient_kernel(x_first, back, carried, choice, gradient, x_second):
    side = lax.axis_index("row")
    chi = back.shape[1]
    bond = back.shape[0] // chi
    size = bond * bond
    to_kron(back, carried, x_second, True)
    product = nt(x_first[...], x_second[...])
    i = iota(product.shape, 0)
    j = iota(product.shape, 1)
    product = jnp.where(i % 8 == j % 8, product, 0.0)
    gather = spread(size)
    high, low = split(product)
    half = nn(high, gather) + nn(low, gather)
    i = iota((size, size * 8), 0)
    j = iota((size, size * 8), 1) // 8
    ordered = jnp.where((i // bond == j % bond) & (i % bond == j // bond), 1.0, 0.0).astype(BF16)
    high, low = split(half)
    env = nn(ordered, high) + nn(ordered, low)
    env = jnp.where(side == 0, env, env.T) * (bond / chi)
    for p in range(gradient.shape[0]):
        kept = jnp.where(choice[0, 0] == p, env, 0.0)
        for r in range(size):
            gradient[p : p + 1, r * size : (r + 1) * size] = kept[r : r + 1, :]


def call(kernel, out_shapes, scratch, inputs, flops):
    vmem = pl.BlockSpec(memory_space=pltpu.VMEM)
    smem = pl.BlockSpec(memory_space=pltpu.SMEM)
    return pl.pallas_call(
        kernel,
        out_shape=[jax.ShapeDtypeStruct(s, t) for s, t in out_shapes],
        in_specs=[smem if x.dtype == jnp.int32 else vmem for x in inputs],
        out_specs=[vmem for _ in out_shapes],
        scratch_shapes=[pltpu.VMEM(s, t) for s, t in scratch],
        compiler_params=pltpu.CompilerParams(vmem_limit_bytes=VMEM_BYTES),
        cost_estimate=pl.CostEstimate(flops=flops, bytes_accessed=2**21, transcendentals=0),
    )(*inputs)


def shifted(block, axis, steps):
    count = lax.axis_size(axis)
    return lax.ppermute(block, axis, [(i, (i + steps) % count) for i in range(count)])


def exchanged(block, axis):
    return lax.ppermute(block, axis, [(0, 1), (1, 0)])


def local(left_bounds, right_bounds, site_tensors, configuration, top_env, bottom_env, sketch):
    chi = left_bounds.shape[2]
    bond = left_bounds.shape[3]
    rows = chi * bond
    size = bond * bond
    tall = (rows, chi)
    flat = (chi, rows)
    kron = (size * 8, size * 8)
    stack = (size * 8, chi // 8 * chi)
    square = (rows, rows)
    western = shifted(left_bounds, "col", 1).reshape(tall)
    eastern = shifted(right_bounds, "col", -1).reshape(tall)
    is_upper = lax.axis_index("row") == 0
    basis, edge, first, sketch_t, core = call(
        edges_kernel,
        [(tall, BF16), (flat, BF16), (tall, BF16), (flat, BF16), ((size // 2, size * 2), BF16)],
        [(tall, F32), (flat, BF16), (flat, BF16)],
        [
            top_env.reshape(tall),
            bottom_env.reshape(tall),
            sketch,
            site_tensors.reshape(site_tensors.shape[2:]),
            configuration,
        ],
        2**31,
    )
    swapped = exchanged(jnp.where(is_upper, eastern, western), "row")
    core_other = exchanged(core, "row")
    x_first, back, carried = call(
        begin_kernel,
        [(stack, BF16), (tall, BF16), (tall, BF16)],
        [(tall, F32), (tall, F32), (flat, BF16), (flat, BF16), (kron, BF16), (square, BF16)],
        [first, western, eastern, core],
        2**31,
    )
    carried = exchanged(carried, "row")
    keep, send = call(
        rows_kernel,
        [(tall, BF16), (tall, BF16)],
        [
            (tall, F32),
            (tall, F32),
            (flat, BF16),
            ((2,) + kron, BF16),
            (stack, BF16),
            (square, BF16),
            (tall, BF16),
        ],
        [basis, edge, sketch_t, western, eastern, swapped, core, core_other],
        2**33,
    )
    received = exchanged(send, "row")
    (gradient,) = call(
        gradient_kernel,
        [(site_tensors.shape[2:], F32)],
        [(stack, BF16)],
        [x_first, back, carried, configuration],
        2**31,
    )
    left_new = jnp.where(is_upper, keep, received)
    right_new = jnp.where(is_upper, received, keep)
    return (
        gradient.reshape(site_tensors.shape),
        left_new.reshape(left_bounds.shape),
        right_new.reshape(right_bounds.shape),
    )


def solution(mesh):
    return jax.shard_map(
        local,
        mesh=mesh,
        in_specs=(
            P(("grp", "row"), "col", None, None, None),
            P(("grp", "row"), "col", None, None, None),
            P(("grp", "row"), "col", None, None),
            P(("grp", "row"), "col"),
            P(("grp", "col"), None, None, None),
            P(("grp", "col"), None, None, None),
            P(),
        ),
        out_specs=(
            P(("grp", "row"), "col", None, None),
            P(("grp", "row"), "col", None, None, None),
            P(("grp", "row"), "col", None, None, None),
        ),
        check_vma=False,
    )
```

profile of v0, /device:TPU:0, one launch (start us, length us, event | category | flops | bytes accessed | tf_op | source)
XLA Modules:
  0.0 52.0 jit_solution(11982823753699377010)
XLA Ops:
  0.6 3.0 %collective-permute-start = (bf16[1,1,128,8,128]{4,3,2,1,0:T(8,128)(2,1)}, bf16[1,1,128,8,128]{4,3,2,1,0:T(8,128)(2,1)S(1)}, u32[]{:S(2)}, u32[]{:S(2)}) collective-permute-start(bf16[1,1,128,8,128]{4,3,2,1,0:T(8,128)(2,1)} %param.7), channel_id=1, source_target_pairs={{0,2},{2,4},{4,6},{6,8},{8,10},{10,12},{12,14},{14,0},{1,3},{3,5},... | collective-permute-start | bytes 786440 | tf_op jit(solution)/shard_map/ppermute | solution.py:372
  3.6 3.1 %collective-permute-start.1 = (bf16[1,1,128,8,128]{4,3,2,1,0:T(8,128)(2,1)}, bf16[1,1,128,8,128]{4,3,2,1,0:T(8,128)(2,1)S(1)}, u32[]{:S(2)}, u32[]{:S(2)}) collective-permute-start(bf16[1,1,128,8,128]{4,3,2,1,0:T(8,128)(2,1)} %param.8), channel_id=1, source_target_pairs={{0,14},{2,0},{4,2},{6,4},{8,6},{10,8},{12,10},{14,12},{1,15},{3,1}... | collective-permute-start | bytes 786440 | tf_op jit(solution)/shard_map/ppermute | solution.py:372
  7.4 7.7 %collective-permute-done = bf16[1,1,128,8,128]{4,3,2,1,0:T(8,128)(2,1)S(1)} collective-permute-done((bf16[1,1,128,8,128]{4,3,2,1,0:T(8,128)(2,1)}, bf16[1,1,128,8,128]{4,3,2,1,0:T(8,128)(2,1)S(1)}, u32[]{:S(2)}, u32[]{:S(2)}) %collective-permute-start) | collective-permute-done | bytes 262176 | tf_op jit(solution)/shard_map/ppermute | solution.py:372
  15.1 2.1 %collective-permute-done.1 = bf16[1,1,128,8,128]{4,3,2,1,0:T(8,128)(2,1)S(1)} collective-permute-done((bf16[1,1,128,8,128]{4,3,2,1,0:T(8,128)(2,1)}, bf16[1,1,128,8,128]{4,3,2,1,0:T(8,128)(2,1)S(1)}, u32[]{:S(2)}, u32[]{:S(2)}) %collective-permute-start.1) | collective-permute-done | bytes 262176 | tf_op jit(solution)/shard_map/ppermute | solution.py:372
  17.2 0.1 collective-permute-start.3
  17.3 0.0 copy-start
  17.3 0.9 %copy-done = bf16[1,128,8,128]{3,2,1,0:T(8,128)(2,1)S(1)} copy-done((bf16[1,128,8,128]{3,2,1,0:T(8,128)(2,1)S(1)}, bf16[1,128,8,128]{3,2,1,0:T(8,128)(2,1)}, u32[]{:S(2)}) %copy-start) | copy-done | bytes 262168
  18.3 0.0 copy-start.1
  18.3 0.9 %copy-done.1 = bf16[1,128,8,128]{3,2,1,0:T(8,128)(2,1)S(1)} copy-done((bf16[1,128,8,128]{3,2,1,0:T(8,128)(2,1)S(1)}, bf16[1,128,8,128]{3,2,1,0:T(8,128)(2,1)}, u32[]{:S(2)}) %copy-start.1) | copy-done | bytes 262168
  19.2 0.0 copy-start.2
  19.2 0.9 %copy-done.2 = bf16[1024,128]{1,0:T(8,128)(2,1)S(1)} copy-done((bf16[1024,128]{1,0:T(8,128)(2,1)S(1)}, bf16[1024,128]{1,0:T(8,128)(2,1)}, u32[]{:S(2)}) %copy-start.2) | copy-done | bytes 262168
  20.2 0.0 copy-start.3
  20.2 0.7 %copy-done.3 = bf16[1,1,2,4096]{3,2,1,0:T(2,128)(2,1)S(1)} copy-done((bf16[1,1,2,4096]{3,2,1,0:T(2,128)(2,1)S(1)}, bf16[1,1,2,4096]{3,2,1,0:T(2,128)(2,1)}, u32[]{:S(2)}) %copy-start.3) | copy-done | bytes 16408
  20.9 7.8 %shard_map.94 = (bf16[1024,128]{1,0:T(8,128)(2,1)S(1)}, bf16[128,1024]{1,0:T(8,128)(2,1)S(1)}, bf16[1024,128]{1,0:T(8,128)(2,1)S(1)}, bf16[128,1024]{1,0:T(8,128)(2,1)S(1)}, bf16[32,128]{1,0:T(8,128)(2,1)S(1)}) custom-call(bf16[1024,128]{1,0:T(8,128)(2,1)S(1)} %bitcast.16, bf16[1024,128]{1,0:T(8,128)(2,1)S(1)} %bitcast.17, bf16[1024,128]{1,0:T(8,128)(2,1)S(1)} %copy-done.2, ...), custom_call_target="tpu_custom_call" | custom-call | flops 2147483648 | bytes 2097152 | tf_op jit(solution)/shard_map/pallas_call | solution.py:359
  28.7 0.5 collective-permute-start.4
  29.2 2.9 %shard_map.95 = (bf16[512,2048]{1,0:T(8,128)(2,1)S(1)}, bf16[1024,128]{1,0:T(8,128)(2,1)S(1)}, bf16[1024,128]{1,0:T(8,128)(2,1)S(1)}) custom-call(bf16[1024,128]{1,0:T(8,128)(2,1)S(1)} %get-tuple-element.13.first, bf16[1024,128]{1,0:T(8,128)(2,1)S(1)} %bitcast.12, bf16[1024,128]{1,0:T(8,128)(2,1)S(1)} %bitcast.14, ...), custom_call_target="tpu_custom_call" | custom-call | flops 2147483648 | bytes 2097152 | tf_op jit(solution)/shard_map/pallas_call | solution.py:359
  32.2 0.1 collective-permute-start.2
  32.3 0.0 collective-permute-done.4.core_other
  32.3 0.0 collective-permute-done.3.swapped
  32.3 14.5 %shard_map.97 = (bf16[1024,128]{1,0:T(8,128)(2,1)S(1)}, bf16[1024,128]{1,0:T(8,128)(2,1)S(1)}) custom-call(bf16[1024,128]{1,0:T(8,128)(2,1)S(1)} %get-tuple-element.18.basis, bf16[128,1024]{1,0:T(8,128)(2,1)S(1)} %get-tuple-element.19.edge, bf16[128,1024]{1,0:T(8,128)(2,1)S(1)} %get-tuple-element.20.sketch_t, bf16[1024,128]{1,0:T(8,128)(2,1)S(1)} %bitcast.13, ...), custom_call_target="tpu_custom_call" | custom-call | flops 8589934592 | bytes 2097152 | tf_op jit(solution)/shard_map/pallas_call | solution.py:359
  46.7 0.8 %collective-permute-start.5 = (bf16[1024,128]{1,0:T(8,128)(2,1)S(1)}, bf16[1024,128]{1,0:T(8,128)(2,1)S(1)}, u32[]{:S(2)}, u32[]{:S(2)}) collective-permute-start(bf16[1024,128]{1,0:T(8,128)(2,1)S(1)} %get-tuple-element.22), channel_id=1, source_target_pairs={{0,1},{1,0},{2,3},{3,2},{4,5},{5,4},{6,7},{7,6},{8,9},{9,8},{10,11... | collective-permute-start | bytes 786440 | tf_op jit(solution)/shard_map/ppermute | solution.py:376
  47.6 0.0 collective-permute-done.2.carried
  47.6 3.5 %shard_map.96 = f32[2,4096]{1,0:T(2,128)} custom-call(bf16[512,2048]{1,0:T(8,128)(2,1)S(1)} %get-tuple-element.15.x_first, bf16[1024,128]{1,0:T(8,128)(2,1)S(1)} %get-tuple-element.16.back, bf16[1024,128]{1,0:T(8,128)(2,1)S(1)} %collective-permute-done.2.carried, s32[1,1]{1,0:T(1,128)S(6)} %copy.10.choice), custom_call_target="tpu_custom_call" | custom-call | flops 2147483648 | bytes 2097152 | tf_op jit(solution)/shard_map/pallas_call | solution.py:359
  51.1 0.0 collective-permute-done.5
  51.1 0.8 %select_bitcast_fusion = (bf16[1,1,128,8,128]{4,3,2,1,0:T(8,128)(2,1)}, bf16[1,1,128,8,128]{4,3,2,1,0:T(8,128)(2,1)}) fusion(bf16[1024,128]{1,0:T(8,128)(2,1)S(1)} %collective-permute-done.5, bf16[1024,128]{1,0:T(8,128)(2,1)S(1)} %get-tuple-element.21, pred[]{:T(512)S(6)} %eq.3), kind=kLoop, calls=%fused_computation | loop fusion | flops 262144 | bytes 1048577 | tf_op jit(solution)/shard_map/reshape | solution.py:443
  (1 shorter events, 0.0 us)
Async XLA Ops:
  0.6 14.5 %collective-permute-start = (bf16[1,1,128,8,128]{4,3,2,1,0:T(8,128)(2,1)}, bf16[1,1,128,8,128]{4,3,2,1,0:T(8,128)(2,1)S(1)}, u32[]{:S(2)}, u32[]{:S(2)}) collective-permute-start(bf16[1,1,128,8,128]{4,3,2,1,0:T(8,128)(2,1)} %param.7), channel_id=1, source_target_pairs={{0,2},{2,4},{4,6},{6,8},{8,10},{10,12},{12,14},{14,0},{1,3},{3,5},... | collective-permute-start | bytes 786440 | tf_op jit(solution)/shard_map/ppermute | solution.py:372
  3.6 13.6 %collective-permute-start.1 = (bf16[1,1,128,8,128]{4,3,2,1,0:T(8,128)(2,1)}, bf16[1,1,128,8,128]{4,3,2,1,0:T(8,128)(2,1)S(1)}, u32[]{:S(2)}, u32[]{:S(2)}) collective-permute-start(bf16[1,1,128,8,128]{4,3,2,1,0:T(8,128)(2,1)} %param.8), channel_id=1, source_target_pairs={{0,14},{2,0},{4,2},{6,4},{8,6},{10,8},{12,10},{14,12},{1,15},{3,1}... | collective-permute-start | bytes 786440 | tf_op jit(solution)/shard_map/ppermute | solution.py:372
  17.2 15.0 %collective-permute-start.3 = (bf16[1024,128]{1,0:T(8,128)(2,1)S(1)}, bf16[1024,128]{1,0:T(8,128)(2,1)S(1)}, u32[]{:S(2)}, u32[]{:S(2)}) collective-permute-start(bf16[1024,128]{1,0:T(8,128)(2,1)S(1)} %broadcast_select_fusion), channel_id=1, source_target_pairs={{0,1},{1,0},{2,3},{3,2},{4,5},{5,4},{6,7},{7,6},{8,9},{9,8},{10,11... | collective-permute-start | bytes 786440 | tf_op jit(solution)/shard_map/ppermute | solution.py:376
  17.3 1.0 %copy-start = (bf16[1,128,8,128]{3,2,1,0:T(8,128)(2,1)S(1)}, bf16[1,128,8,128]{3,2,1,0:T(8,128)(2,1)}, u32[]{:S(2)}) copy-start(bf16[1,128,8,128]{3,2,1,0:T(8,128)(2,1)} %param.11) | copy-start | bytes 786436
  18.3 0.9 %copy-start.1 = (bf16[1,128,8,128]{3,2,1,0:T(8,128)(2,1)S(1)}, bf16[1,128,8,128]{3,2,1,0:T(8,128)(2,1)}, u32[]{:S(2)}) copy-start(bf16[1,128,8,128]{3,2,1,0:T(8,128)(2,1)} %param.12) | copy-start | bytes 786436
  19.2 0.9 %copy-start.2 = (bf16[1024,128]{1,0:T(8,128)(2,1)S(1)}, bf16[1024,128]{1,0:T(8,128)(2,1)}, u32[]{:S(2)}) copy-start(bf16[1024,128]{1,0:T(8,128)(2,1)} %sketch.1) | copy-start | bytes 786436
  20.2 0.7 %copy-start.3 = (bf16[1,1,2,4096]{3,2,1,0:T(2,128)(2,1)S(1)}, bf16[1,1,2,4096]{3,2,1,0:T(2,128)(2,1)}, u32[]{:S(2)}) copy-start(bf16[1,1,2,4096]{3,2,1,0:T(2,128)(2,1)} %param.9) | copy-start | bytes 49156
  28.7 3.6 %collective-permute-start.4 = (bf16[32,128]{1,0:T(8,128)(2,1)S(1)}, bf16[32,128]{1,0:T(8,128)(2,1)S(1)}, u32[]{:S(2)}, u32[]{:S(2)}) collective-permute-start(bf16[32,128]{1,0:T(8,128)(2,1)S(1)} %get-tuple-element.14.core.core_own), channel_id=1, source_target_pairs={{0,1},{1,0},{2,3},{3,2},{4,5},{5,4},{6,7},{7,6},{8,9},{9,8},{10,11... | collective-permute-start | bytes 24584 | tf_op jit(solution)/shard_map/ppermute | solution.py:376
  32.2 15.4 %collective-permute-start.2 = (bf16[1024,128]{1,0:T(8,128)(2,1)S(1)}, bf16[1024,128]{1,0:T(8,128)(2,1)S(1)}, u32[]{:S(2)}, u32[]{:S(2)}) collective-permute-start(bf16[1024,128]{1,0:T(8,128)(2,1)S(1)} %get-tuple-element.17), channel_id=1, source_target_pairs={{0,1},{1,0},{2,3},{3,2},{4,5},{5,4},{6,7},{7,6},{8,9},{9,8},{10,11... | collective-permute-start | bytes 786440 | tf_op jit(solution)/shard_map/ppermute | solution.py:376
  46.7 4.4 %collective-permute-start.5 = (bf16[1024,128]{1,0:T(8,128)(2,1)S(1)}, bf16[1024,128]{1,0:T(8,128)(2,1)S(1)}, u32[]{:S(2)}, u32[]{:S(2)}) collective-permute-start(bf16[1024,128]{1,0:T(8,128)(2,1)S(1)} %get-tuple-element.22), channel_id=1, source_target_pairs={{0,1},{1,0},{2,3},{3,2},{4,5},{5,4},{6,7},{7,6},{8,9},{9,8},{10,11... | collective-permute-start | bytes 786440 | tf_op jit(solution)/shard_map/ppermute | solution.py:376
where the time goes:
time: 52.2 us; the launch traced here: 52 us
  Pallas kernels  28.7 us (55%)
  waiting for transfers between devices  9.85 us (19%)
  starting transfers between devices  7.64 us (15%)
  local copies, waits for them, and re-layouts  3.56 us (7%)
  between operations  1.34 us (3%)
  other arithmetic  0.86 us (2%)
    pallas_call x4, Pallas kernels, call(): pl.pallas_call(kernel, out_shape=[jax.ShapeDtypeStruct(s, t) for s, t in...  28.7 us
    ppermute x2, waiting for transfers between devices, shifted(): lax.ppermute(block, axis, [(i, (i + steps) % count) for i in range(count)])  9.84 us
    ppermute x2, starting transfers between devices, shifted(): lax.ppermute(block, axis, [(i, (i + steps) % count) for i in range(count)])  6.09 us
    unnamed x8, local copies, waits for them, and re-layouts  3.56 us
    ppermute x4, starting transfers between devices, exchanged(): return lax.ppermute(block, axis, [(0, 1), (1, 0)])  1.55 us
  transfers between devices with their start and end apart: 6, of which 2 were waited for; matrix products, arithmetic and copies ran while one was open for 0% of the time, Pallas kernels for 55%

commit v1 on v0

v1 whole, which is shorter than its diff:
```python
import functools

import jax
import jax.numpy as jnp
from jax import lax
from jax.experimental import pallas as pl
from jax.experimental.pallas import tpu as pltpu
from jax.sharding import PartitionSpec as P

F32 = jnp.float32
BF16 = jnp.bfloat16
VMEM_BYTES = 24 * 1024 * 1024


def nn(a, b):
    return jnp.dot(a, b, preferred_element_type=F32)


def nt(a, b):
    return lax.dot_general(a, b, (((1,), (1,)), ((), ())), preferred_element_type=F32)


def split(x):
    high = x.astype(BF16)
    return high, (x - high.astype(F32)).astype(BF16)


def iota(shape, axis):
    return lax.broadcasted_iota(jnp.int32, shape, axis)


def chol_inverse(grams, near, beside=()):
    beside = list(beside)
    n = grams[0].shape[0]
    blocks = n // 8
    count = len(grams)
    lane = iota((8, n), 1)
    sub = iota((8, n), 0)
    at = [sub == j for j in range(8)]
    after = [sub > j for j in range(8)]
    tiles = [[g[8 * i : 8 * i + 8, :] for i in range(blocks)] for g in grams]

    def over_lanes(x, j):
        return jnp.broadcast_to(x[:, j : j + 1], (8, n))

    def over_rows(x, j):
        return jnp.broadcast_to(x[j : j + 1, :], (8, n))

    for b in range(blocks):
        own = (lane >= 8 * b) & (lane < 8 * b + 8)
        eye = jnp.where(lane - 8 * b == sub, 1.0, 0.0)
        by_element = range(b + 1, min(blocks, b + 1 + near))
        by_matmul = range(by_element.stop, blocks)
        diag = [[over_lanes(tiles[q][b], 8 * b + j) for j in range(8)] for q in range(count)]
        below = [
            [[over_lanes(tiles[q][i], 8 * b + j) for j in range(8)] for i in by_element]
            for q in range(count)
        ]
        forward = [jnp.where(own, eye, tiles[q][b]) for q in range(count)]
        full = list(forward)
        pivots = [jnp.ones((8, n), F32) for _ in range(count)]
        for step in beside[b * len(beside) // blocks : (b + 1) * len(beside) // blocks]:
            step()
        for j in range(8):
            for q in range(count):
                c = diag[q]
                pivot = over_rows(c[j], j)
                inverse = 1.0 / pivot
                pivots[q] = jnp.where(at[j], pivot, pivots[q])
                for k in range(j + 1, 8):
                    m = over_rows(c[k], j) * inverse
                    c[k] = jnp.where(at[j], m, c[k] - c[j] * m)
                row = over_rows(forward[q], j) * inverse
                forward[q] = jnp.where(after[j], forward[q] - c[j] * row, forward[q])
                full[q] = jnp.where(at[j], row, full[q] - c[j] * row)
        for q in range(count):
            rows = [over_rows(full[q], j) for j in range(8)]
            for i in by_element:
                terms = [below[q][i - b - 1][j] * rows[j] for j in range(8)]
                while len(terms) > 1:
                    terms = [x + y for x, y in zip(terms[::2], terms[1::2])]
                tiles[q][i] = jnp.where(own, 0.0, tiles[q][i]) - terms[0]
            if by_matmul:
                rest = jnp.concatenate([tiles[q][i] for i in by_matmul], axis=0)
                padded = [full[q], jnp.zeros((n - 8 * b - 8, n), F32)]
                if b:
                    padded = [jnp.zeros((8 * b, n), F32)] + padded
                update = jnp.dot(
                    rest,
                    jnp.concatenate(padded, axis=0),
                    precision=lax.Precision.HIGHEST,
                    preferred_element_type=F32,
                )
                for x, i in enumerate(by_matmul):
                    tiles[q][i] = jnp.where(own, 0.0, tiles[q][i]) - update[8 * x : 8 * x + 8]
            tiles[q][b] = jnp.where(lane <= sub + 8 * b, forward[q] * lax.rsqrt(pivots[q]), 0.0)
    return [jnp.concatenate(t, axis=0) for t in tiles]


def leg(scratch, j):
    chi = scratch.shape[1]
    return scratch[pl.ds(j, chi, stride=scratch.shape[0] // chi), :]


def kron_step(lhs, rhs, x_ref, t, transposed=False):
    chi = lhs.shape[1]
    bond = lhs.shape[0] // chi
    if transposed:
        product = nt(lhs[...], rhs[t * chi : (t + 2) * chi, :])
    else:
        product = nn(lhs[...], rhs[:, t * chi : (t + 2) * chi])
    for s in range(bond):
        at = (s * bond + t) * 8
        for g in range(chi // 8):
            rows = product[s * chi + g * 8 : s * chi + g * 8 + 8, :]
            x_ref[at : at + 16, g * chi : (g + 1) * chi] = jnp.concatenate(
                [rows[:, :chi], rows[:, chi:]], axis=0
            ).astype(BF16)


def absorb_step(kron, x_ref, m_ref, g, chi):
    bond = m_ref.shape[0] // chi
    out = nn(kron[...], x_ref[:, g * chi : (g + 2) * chi])
    for o in range(bond):
        for d in range(bond):
            rows = out[(o * bond + d) * 8 : (o * bond + d) * 8 + 8, :]
            at = o * chi + g * 8
            m_ref[at : at + 16, d * chi : (d + 1) * chi] = jnp.concatenate(
                [rows[:, :chi], rows[:, chi:]], axis=0
            ).astype(BF16)


def kron_steps(lhs, rhs, x_ref, transposed=False):
    bond = lhs.shape[0] // lhs.shape[1]
    return [
        functools.partial(kron_step, lhs, rhs, x_ref, t, transposed) for t in range(0, bond, 2)
    ]


def absorb_steps(kron, x_ref, m_ref, chi):
    return [
        functools.partial(absorb_step, kron, x_ref, m_ref, g, chi) for g in range(0, chi // 8, 2)
    ]


def square_core(flat):
    half = flat.shape[1] // 2
    size = flat.shape[0] * 2
    i = iota((size, flat.shape[0]), 0)
    j = iota((size, flat.shape[0]), 1)
    even = jnp.where(i == 2 * j, 1.0, 0.0).astype(BF16)
    odd = jnp.where(i == 2 * j + 1, 1.0, 0.0).astype(BF16)
    return (nn(even, flat[:, :half]) + nn(odd, flat[:, half:])).astype(BF16)


def swap_order(size, bond):
    i = iota((size, size), 0)
    j = iota((size, size), 1)
    hit = (i // bond == j % bond) & (i % bond == j // bond)
    return jnp.where(hit, 1.0, 0.0).astype(BF16)


def spread(size):
    i = iota((size * 8, size), 0)
    j = iota((size * 8, size), 1)
    return jnp.where(i // 8 == j, 1.0, 0.0).astype(BF16)


def kron_of(spread_rows, size):
    wide = nt(spread_rows.astype(BF16), spread(size))
    i = iota(wide.shape, 0)
    j = iota(wide.shape, 1)
    return jnp.where(i % 8 == j % 8, wide, 0.0).astype(BF16)


def spread_ahead(core, bond):
    size = core.shape[0]
    return nt(spread(size), nn(swap_order(size, bond), core).astype(BF16))


def spread_turned(core, bond):
    size = core.shape[0]
    return nn(spread(size), nt(swap_order(size, bond), core).astype(BF16))


def spread_back(core, bond):
    size = core.shape[0]
    return nn(spread(size), nn(core, swap_order(size, bond)).astype(BF16))


def mirrored(core, bond):
    size = core.shape[0]
    i = iota((size, size), 0)
    j = iota((size, size), 1)
    total = jnp.zeros((size, size), F32)
    for u in range(bond):
        pick = jnp.where(j == (i // bond) * bond + u, 1.0, 0.0).astype(BF16)
        picked = jnp.where(i % bond == j % bond, nn(pick, core), 0.0).astype(BF16)
        place = jnp.where(j == u * bond + i // bond, 1.0, 0.0).astype(BF16)
        total = total + nn(picked, place)
    return total.astype(BF16)


def begin_kernel(left, right, sites, choice, first, second, core, chosen, sems):
    side = lax.axis_index("row")

    def start(one, other):
        pltpu.make_async_copy(one, first, sems.at[0]).start()
        pltpu.make_async_copy(other, second, sems.at[1]).start()

    pl.when(side == 0)(functools.partial(start, left, right))
    pl.when(side == 1)(functools.partial(start, right, left))
    copy = pltpu.make_async_copy(sites, chosen, sems.at[2])
    copy.start()
    copy.wait()
    total = jnp.zeros((1, chosen.shape[1]), F32)
    for p in range(chosen.shape[0]):
        total = total + jnp.where(choice[0, 0] == p, chosen[p : p + 1, :].astype(F32), 0.0)
    flat = [total[:, i : i + core.shape[1]] for i in range(0, total.shape[1], core.shape[1])]
    core[...] = jnp.concatenate(flat, axis=0).astype(BF16)
    pltpu.make_async_copy(left, first, sems.at[0]).wait()
    pltpu.make_async_copy(right, second, sems.at[1]).wait()


def edges_kernel(
    top_hbm,
    bottom_hbm,
    sketch_hbm,
    basis,
    basis_lanes,
    edge,
    first,
    sketch_t,
    top,
    bottom,
    sketch,
    wide,
    wide_sketch,
    legs_top,
    legs_bottom,
    sems,
):
    side = lax.axis_index("row")
    chi = top.shape[1]
    bond = top.shape[0] // chi
    copies = [
        pltpu.make_async_copy(source, target, sems.at[i])
        for i, (source, target) in enumerate(
            ((top_hbm, top), (bottom_hbm, bottom), (sketch_hbm, sketch))
        )
    ]
    for copy in copies:
        copy.start()
    for env, legs, mine in ((top, legs_top, 0), (bottom, legs_bottom, 1)):
        copies[mine].wait()
        wide[...] = env[...].astype(F32)

        @pl.when(side == 0)
        def _():
            for u in range(bond):
                block = leg(wide, u).T.astype(BF16)
                legs[:, u * chi : (u + 1) * chi] = block
                if mine == 0:
                    first[u * chi : (u + 1) * chi, :] = block

        @pl.when(side == 1)
        def _():
            for u in range(bond):
                block = leg(wide, u).astype(BF16)
                legs[:, u * chi : (u + 1) * chi] = block
                if mine == 1:
                    first[u * chi : (u + 1) * chi, :] = block

    copies[2].wait()
    wide_sketch[...] = sketch[...].astype(F32)

    def turn_sketch(o):
        sketch_t[o * chi : (o + 1) * chi, :] = leg(wide_sketch, o).T.astype(BF16)

    inverse_top, inverse_bottom = chol_inverse(
        [nt(legs_top[...], legs_top[...]), nt(legs_bottom[...], legs_bottom[...])],
        1,
        [functools.partial(turn_sketch, o) for o in range(bond)],
    )
    high, low = split(inverse_top)
    ortho = (nn(high, legs_top[...]) + nn(low, legs_top[...])).astype(BF16)
    basis_lanes[...] = ortho
    for u in range(bond):
        basis[u * chi : (u + 1) * chi, :] = ortho[:, u * chi : (u + 1) * chi]
    high, low = split(inverse_bottom)
    edge[...] = (nn(high, legs_bottom[...]) + nn(low, legs_bottom[...])).astype(BF16)


def finish(absorbed, closing, wide):
    chi = closing.shape[0]
    bond = absorbed.shape[0] // chi
    unscaled = nt(absorbed[...], closing)
    mean = jnp.sum(unscaled * unscaled) * (1.0 / (unscaled.shape[0] * unscaled.shape[1]))
    scaled = unscaled * lax.rsqrt(mean + 1e-06)
    for o in range(bond):
        wide[pl.ds(o, chi, stride=bond), :] = scaled[o * chi : (o + 1) * chi, :]
    return wide[...].astype(BF16)


def prepare_kernel(
    basis_lanes, sketch_t, site, site_other, kron_0, kron_1, kron_first, sketched, x, kron_sketch
):
    side = lax.axis_index("row")
    chi = basis_lanes.shape[0]
    bond = basis_lanes.shape[1] // chi
    size = bond * bond
    is_left = side == 0
    core = square_core(site[...])
    other = square_core(site_other[...])
    mirrored_own = mirrored(core, bond)
    mirrored_other = mirrored(other, bond)
    swap = swap_order(size, bond)
    wide = spread(size)
    ahead = spread_ahead(core, bond)
    kron_0[...] = kron_of(jnp.where(is_left, ahead, nn(wide, mirrored_other)), size)
    kron_1[...] = kron_of(
        jnp.where(is_left, spread_ahead(other, bond), nn(wide, mirrored_own)), size
    )
    kron_first[...] = kron_of(jnp.where(is_left, ahead, spread_back(core, bond)), size)
    turned = nn(nn(swap, mirrored_own).astype(BF16), swap).astype(BF16)
    kron_sketch[...] = kron_of(
        jnp.where(is_left, nn(wide, turned), spread_turned(other, bond)), size
    )
    for step in kron_steps(sketch_t, basis_lanes, x) + absorb_steps(kron_sketch, x, sketched, chi):
        step()


def upper_kernel(
    basis,
    sketched,
    first,
    arrived_x,
    arrived_y,
    kron_0,
    kron_first,
    next_basis,
    new,
    x_first,
    middle,
    lanes_1,
    wide_x,
    wide_y,
    rows_0,
    lanes_0,
    ahead,
    x,
    absorbed,
):
    is_left = lax.axis_index("row") == 0
    chi = basis.shape[1]
    bond = basis.shape[0] // chi
    blocks = [slice(j * chi, (j + 1) * chi) for j in range(bond)]
    wide_x[...] = arrived_x[...].astype(F32)
    wide_y[...] = arrived_y[...].astype(F32)
    for j in range(bond):
        block = jnp.where(is_left, leg(wide_x, j), leg(wide_y, j)).astype(BF16)
        rows_0[blocks[j], :] = block
        lanes_0[:, blocks[j]] = block
    stacked = nn(sketched[...], rows_0[...])
    range_t = jnp.concatenate([stacked[blocks[d], :] for d in range(bond)], axis=1)
    high, low = split(range_t)
    gram = nt(high, high) + (nt(high, low) + nt(low, high))

    def ready_ahead(j):
        block = leg(wide_x, j)
        ahead[:, blocks[j]] = jnp.where(is_left, block, block.T).astype(BF16)

    def ready_next(j):
        lanes_1[:, blocks[j]] = jnp.where(is_left, leg(wide_y, j), leg(wide_x, j)).astype(BF16)

    beside = (
        kron_steps(basis, lanes_0, x)
        + absorb_steps(kron_0, x, absorbed, chi)
        + [functools.partial(ready_ahead, j) for j in range(bond)]
        + kron_steps(first, ahead, x_first)
        + absorb_steps(kron_first, x_first, middle, chi)
        + [functools.partial(ready_next, j) for j in range(bond)]
    )
    (inverse,) = chol_inverse([gram], 2, beside)
    inverse_high, inverse_low = split(inverse)
    closing = (
        nn(inverse_high, high) + (nn(inverse_high, low) + nn(inverse_low, high))
    ).astype(BF16)
    for d in range(bond):
        next_basis[blocks[d], :] = closing[:, blocks[d]]
    new[...] = finish(absorbed, closing, wide_x)


def state_kernel(middle, received, carried, back, wide, behind):
    side = lax.axis_index("row")
    chi = received.shape[1]
    bond = received.shape[0] // chi
    wide[...] = received[...].astype(F32)

    @pl.when(side == 0)
    def _():
        for j in range(bond):
            at = slice(j * chi, (j + 1) * chi)
            block = leg(wide, j)
            behind[:, at] = block.T.astype(BF16)
            back[at, :] = block.astype(BF16)

    @pl.when(side == 1)
    def _():
        for j in range(bond):
            at = slice(j * chi, (j + 1) * chi)
            block = leg(wide, j)
            behind[:, at] = block.astype(BF16)
            back[at, :] = block.T.astype(BF16)

    state = nn(behind[...], middle[...]).astype(BF16)
    for s in range(bond):
        carried[s * chi : (s + 1) * chi, :] = state[:, s * chi : (s + 1) * chi]


def lower_kernel(basis, edge, lanes, kron, new_0, keep, send, wide, x, absorbed):
    side = lax.axis_index("row")
    chi = basis.shape[1]
    for step in kron_steps(basis, lanes, x) + absorb_steps(kron, x, absorbed, chi):
        step()
    new = finish(absorbed, edge[...], wide)

    @pl.when(side == 0)
    def _():
        keep[...] = new_0[...]
        send[...] = new

    @pl.when(side == 1)
    def _():
        keep[...] = new
        send[...] = new_0[...]


def gradient_kernel(x_first, back, carried, choice, gradient, x_second):
    side = lax.axis_index("row")
    chi = back.shape[1]
    bond = back.shape[0] // chi
    size = bond * bond
    for step in kron_steps(back, carried, x_second, True):
        step()
    product = nt(x_first[...], x_second[...])
    i = iota(product.shape, 0)
    j = iota(product.shape, 1)
    product = jnp.where(i % 8 == j % 8, product, 0.0)
    gather = spread(size)
    high, low = split(product)
    half = nn(high, gather) + nn(low, gather)
    i = iota((size, size * 8), 0)
    j = iota((size, size * 8), 1) // 8
    ordered = jnp.where((i // bond == j % bond) & (i % bond == j // bond), 1.0, 0.0).astype(BF16)
    high, low = split(half)
    env = nn(ordered, high) + nn(ordered, low)
    env = jnp.where(side == 0, env, env.T) * (bond / chi)
    for p in range(gradient.shape[0]):
        kept = jnp.where(choice[0, 0] == p, env, 0.0)
        for r in range(size):
            gradient[p : p + 1, r * size : (r + 1) * size] = kept[r : r + 1, :]


def call(kernel, out_shapes, scratch, inputs, flops, in_place=(), copies=0):
    inputs = [
        pltpu.with_memory_space_constraint(x, pltpu.HBM) if i in in_place else x
        for i, x in enumerate(inputs)
    ]
    vmem = pl.BlockSpec(memory_space=pltpu.VMEM)
    smem = pl.BlockSpec(memory_space=pltpu.SMEM)
    return pl.pallas_call(
        kernel,
        out_shape=[jax.ShapeDtypeStruct(s, t) for s, t in out_shapes],
        in_specs=[
            smem
            if x.dtype == jnp.int32
            else pl.BlockSpec(memory_space=pltpu.HBM)
            if i in in_place
            else vmem
            for i, x in enumerate(inputs)
        ],
        out_specs=[vmem for _ in out_shapes],
        scratch_shapes=[pltpu.VMEM(s, t) for s, t in scratch]
        + ([pltpu.SemaphoreType.DMA((copies,))] if copies else []),
        compiler_params=pltpu.CompilerParams(vmem_limit_bytes=VMEM_BYTES),
        cost_estimate=pl.CostEstimate(flops=flops, bytes_accessed=2**21, transcendentals=0),
    )(*inputs)


def moved(block, pairs):
    return lax.ppermute(block, ("col", "row"), pairs)


def exchanged(block, axis):
    return lax.ppermute(block, axis, [(0, 1), (1, 0)])


def local(left_bounds, right_bounds, site_tensors, configuration, top_env, bottom_env, sketch):
    chi = left_bounds.shape[2]
    bond = left_bounds.shape[3]
    rows = chi * bond
    size = bond * bond
    tall = (rows, chi)
    flat = (chi, rows)
    kron = (size * 8, size * 8)
    stack = (size * 8, chi // 8 * chi)
    square = (rows, rows)
    count = lax.axis_size("col")
    sites = site_tensors.reshape(site_tensors.shape[2:])
    is_upper = lax.axis_index("row") == 0
    first_sent, second_sent, site = call(
        begin_kernel,
        [(tall, BF16), (tall, BF16), ((size // 2, size * 2), BF16)],
        [(sites.shape, BF16)],
        [left_bounds.reshape(tall), right_bounds.reshape(tall), sites, configuration],
        2**20,
        in_place=(0, 1, 2),
        copies=3,
    )
    ahead, behind = (
        [2 * ((c + step) % count) for c in range(count)] for step in (1, -1)
    )
    arrived_x = moved(
        first_sent,
        [(2 * c, ahead[c]) for c in range(count)]
        + [(2 * c + 1, behind[c] + 1) for c in range(count)],
    )
    arrived_y = moved(
        second_sent,
        [(2 * c, behind[c] + 1) for c in range(count)]
        + [(2 * c + 1, ahead[c]) for c in range(count)],
    )
    site_other = exchanged(site, "row")
    basis, basis_lanes, edge, first, sketch_t = call(
        edges_kernel,
        [(tall, BF16), (flat, BF16), (flat, BF16), (tall, BF16), (tall, BF16)],
        [(tall, BF16)] * 3 + [(tall, F32), (tall, F32), (flat, BF16), (flat, BF16)],
        [top_env.reshape(tall), bottom_env.reshape(tall), sketch],
        2**31,
        in_place=(0, 1, 2),
        copies=3,
    )
    site_other, basis_lanes = lax.optimization_barrier((site_other, basis_lanes))
    kron_0, kron_1, kron_first, sketched = call(
        prepare_kernel,
        [(kron, BF16), (kron, BF16), (kron, BF16), (square, BF16)],
        [(stack, BF16), (kron, BF16)],
        [basis_lanes, sketch_t, site, site_other],
        2**31,
    )
    sketched, arrived_x, arrived_y = lax.optimization_barrier((sketched, arrived_x, arrived_y))
    swapped = exchanged(arrived_y, "row")
    next_basis, new, x_first, middle, lanes = call(
        upper_kernel,
        [(tall, BF16), (tall, BF16), (stack, BF16), (square, BF16), (flat, BF16)],
        [
            (tall, F32),
            (tall, F32),
            (tall, BF16),
            (flat, BF16),
            (flat, BF16),
            (stack, BF16),
            (square, BF16),
        ],
        [basis, sketched, first, arrived_x, arrived_y, kron_0, kron_first],
        2**33,
    )
    carried, back = call(
        state_kernel,
        [(tall, BF16), (tall, BF16)],
        [(tall, F32), (flat, BF16)],
        [middle, swapped],
        2**30,
    )
    next_basis, carried = lax.optimization_barrier((next_basis, carried))
    carried = exchanged(carried, "row")
    keep, send = call(
        lower_kernel,
        [(tall, BF16), (tall, BF16)],
        [(tall, F32), (stack, BF16), (square, BF16)],
        [next_basis, edge, lanes, kron_1, new],
        2**32,
    )
    received = exchanged(send, "row")
    (gradient,) = call(
        gradient_kernel,
        [(sites.shape, F32)],
        [(stack, BF16)],
        [x_first, back, carried, configuration],
        2**31,
    )
    received, gradient = lax.optimization_barrier((received, gradient))
    left_new = jnp.where(is_upper, keep, received)
    right_new = jnp.where(is_upper, received, keep)
    return (
        gradient.reshape(site_tensors.shape),
        left_new.reshape(left_bounds.shape),
        right_new.reshape(right_bounds.shape),
    )


def solution(mesh):
    return jax.shard_map(
        local,
        mesh=mesh,
        in_specs=(
            P(("grp", "row"), "col", None, None, None),
            P(("grp", "row"), "col", None, None, None),
            P(("grp", "row"), "col", None, None),
            P(("grp", "row"), "col"),
            P(("grp", "col"), None, None, None),
            P(("grp", "col"), None, None, None),
            P(),
        ),
        out_specs=(
            P(("grp", "row"), "col", None, None),
            P(("grp", "row"), "col", None, None, None),
            P(("grp", "row"), "col", None, None, None),
        ),
        check_vma=False,
    )
```

time: 52.2 us -> 38.1 us (0.73)
  waiting for transfers between devices: 9.85 us -> 0.02 us
  local copies, waits for them, and re-layouts: 3.56 us -> 0 us
  Pallas kernels: 28.7 us -> 27.4 us
  other arithmetic: 0.86 us -> 1.78 us
    ppermute x2, waiting for transfers between devices: 9.84 us -> 0.01 us  [moved(): return lax.ppermute(block, ('col', 'row'), pairs)]
    unnamed x8 -> x0, local copies, waits for them, and re-layouts: 3.56 us -> none
    pallas_call x4 -> x7, Pallas kernels: 28.7 us -> 27.4 us  [call(): pl.pallas_call(kernel, out_shape=[jax.ShapeDtypeStruct(s, t) for s, t in...]
    reshape x1, other arithmetic: 0.83 us -> 1.78 us  [local(): right_new.reshape(right_bounds.shape)]
  transfers between devices with their start and end apart: 6 -> 6, of which waited for: 2 -> 0; matrix products, arithmetic and copies ran while one was open for 0% -> 0% of each run, Pallas kernels for 55% -> 68%
where the time goes in v1:
time: 38.1 us; the launch traced here: 37.7 us
  Pallas kernels  27.4 us (72%)
  starting transfers between devices  7.15 us (19%)
  other arithmetic  1.78 us (5%)
  between operations  1.38 us (4%)
    pallas_call x7, Pallas kernels, call(): pl.pallas_call(kernel, out_shape=[jax.ShapeDtypeStruct(s, t) for s, t in...  27.4 us
    ppermute x2, starting transfers between devices, moved(): return lax.ppermute(block, ('col', 'row'), pairs)  5.89 us
    reshape x1, other arithmetic, local(): right_new.reshape(right_bounds.shape)  1.78 us
    ppermute x4, starting transfers between devices, exchanged(): return lax.ppermute(block, axis, [(0, 1), (1, 0)])  1.25 us
  transfers between devices with their start and end apart: 6, of which 0 were waited for; matrix products, arithmetic and copies ran while one was open for 0% of the time, Pallas kernels for 68%

profile of v1, /device:TPU:0, one launch (start us, length us, event | category | flops | bytes accessed | tf_op | source)
XLA Modules:
  0.0 37.7 jit_solution(13400199574236128470)
XLA Ops:
  1.3 1.1 %shard_map.95 = (bf16[1024,128]{1,0:T(8,128)(2,1)S(1)}, bf16[1024,128]{1,0:T(8,128)(2,1)S(1)}, bf16[32,128]{1,0:T(8,128)(2,1)S(1)}) custom-call(bf16[1024,128]{1,0:T(8,128)(2,1)} %bitcast.10, bf16[1024,128]{1,0:T(8,128)(2,1)} %bitcast.11, bf16[2,4096]{1,0:T(2,128)(2,1)} %bitcast.12, s32[1,1]{1,0:T(1,128)S(6)} %copy.10.choice), custom_call_target="tpu_custom_call" | custom-call | flops 1048576 | bytes 2097152 | tf_op jit(solution)/shard_map/pallas_call | solution.py:472
  2.3 0.5 %collective-permute-start = (bf16[32,128]{1,0:T(8,128)(2,1)S(1)}, bf16[32,128]{1,0:T(8,128)(2,1)S(1)}, u32[]{:S(2)}, u32[]{:S(2)}) collective-permute-start(bf16[32,128]{1,0:T(8,128)(2,1)S(1)} %get-tuple-element.34.site), channel_id=1, source_target_pairs={{0,1},{1,0},{2,3},{3,2},{4,5},{5,4},{6,7},{7,6},{8,9},{9,8},{10,11... | collective-permute-start | bytes 24584 | tf_op jit(solution)/shard_map/ppermute | solution.py:496
  2.9 2.6 %collective-permute-start.1 = (bf16[1024,128]{1,0:T(8,128)(2,1)S(1)}, bf16[1024,128]{1,0:T(8,128)(2,1)S(1)}, u32[]{:S(2)}, u32[]{:S(2)}) collective-permute-start(bf16[1024,128]{1,0:T(8,128)(2,1)S(1)} %get-tuple-element.40), channel_id=1, source_target_pairs={{0,2},{2,4},{4,6},{6,8},{8,10},{10,12},{12,14},{14,0},{1,15},{3,1}... | collective-permute-start | bytes 786440 | tf_op jit(solution)/shard_map/ppermute | solution.py:492
  5.4 3.3 %collective-permute-start.2 = (bf16[1024,128]{1,0:T(8,128)(2,1)S(1)}, bf16[1024,128]{1,0:T(8,128)(2,1)S(1)}, u32[]{:S(2)}, u32[]{:S(2)}) collective-permute-start(bf16[1024,128]{1,0:T(8,128)(2,1)S(1)} %get-tuple-element.41), channel_id=1, source_target_pairs={{0,15},{2,1},{4,3},{6,5},{8,7},{10,9},{12,11},{14,13},{1,2},{3,4},... | collective-permute-start | bytes 786440 | tf_op jit(solution)/shard_map/ppermute | solution.py:492
  8.8 6.0 %shard_map.94 = (bf16[1024,128]{1,0:T(8,128)(2,1)S(1)}, bf16[128,1024]{1,0:T(8,128)(2,1)S(1)}, bf16[128,1024]{1,0:T(8,128)(2,1)S(1)}, bf16[1024,128]{1,0:T(8,128)(2,1)S(1)}, bf16[1024,128]{1,0:T(8,128)(2,1)S(1)}) custom-call(bf16[1024,128]{1,0:T(8,128)(2,1)} %bitcast.13, bf16[1024,128]{1,0:T(8,128)(2,1)} %bitcast.14, bf16[1024,128]{1,0:T(8,128)(2,1)} %sketch_hbm.1), custom_call_target="tpu_custom_call" | custom-call | flops 2147483648 | bytes 2097152 | tf_op jit(solution)/shard_map/pallas_call | solution.py:472
  14.8 0.0 collective-permute-done.site_other
  14.8 3.9 %shard_map.96 = (bf16[512,512]{1,0:T(8,128)(2,1)S(1)}, bf16[512,512]{1,0:T(8,128)(2,1)S(1)}, bf16[512,512]{1,0:T(8,128)(2,1)S(1)}, bf16[1024,1024]{1,0:T(8,128)(2,1)S(1)}) custom-call(bf16[128,1024]{1,0:T(8,128)(2,1)S(1)} %get-tuple-element.36.basis_lanes, bf16[1024,128]{1,0:T(8,128)(2,1)S(1)} %get-tuple-element.37.sketch_t, ...), custom_call_target="tpu_custom_call" | custom-call | flops 2147483648 | bytes 2097152 | tf_op jit(solution)/shard_map/pallas_call | solution.py:472
  18.8 0.0 collective-permute-done.1.arrived_x
  18.8 0.0 collective-permute-done.2.arrived_y
  18.8 0.1 collective-permute-start.3
  18.9 9.1 %shard_map.97 = (bf16[1024,128]{1,0:T(8,128)(2,1)S(1)}, bf16[1024,128]{1,0:T(8,128)(2,1)S(1)}, bf16[512,2048]{1,0:T(8,128)(2,1)S(1)}, bf16[1024,1024]{1,0:T(8,128)(2,1)S(1)}, bf16[128,1024]{1,0:T(8,128)(2,1)S(1)}) custom-call(bf16[1024,128]{1,0:T(8,128)(2,1)S(1)} %get-tuple-element.33.basis, bf16[1024,1024]{1,0:T(8,128)(2,1)S(1)} %get-tuple-element.42.sketched, ...), custom_call_target="tpu_custom_call" | custom-call | flops 8589934592 | bytes 2097152 | tf_op jit(solution)/shard_map/pallas_call | solution.py:472
  27.9 0.0 collective-permute-done.3.received
  27.9 0.6 %shard_map.98 = (bf16[1024,128]{1,0:T(8,128)(2,1)S(1)}, bf16[1024,128]{1,0:T(8,128)(2,1)S(1)}) custom-call(bf16[1024,1024]{1,0:T(8,128)(2,1)S(1)} %get-tuple-element.49.middle, bf16[1024,128]{1,0:T(8,128)(2,1)S(1)} %collective-permute-done.3.received), custom_call_target="tpu_custom_call" | custom-call | flops 1073741824 | bytes 2097152 | tf_op jit(solution)/shard_map/pallas_call | solution.py:472
  28.6 0.6 %collective-permute-start.5 = (bf16[1024,128]{1,0:T(8,128)(2,1)S(1)}, bf16[1024,128]{1,0:T(8,128)(2,1)S(1)}, u32[]{:S(2)}, u32[]{:S(2)}) collective-permute-start(bf16[1024,128]{1,0:T(8,128)(2,1)S(1)} %get-tuple-element.59), channel_id=1, source_target_pairs={{0,1},{1,0},{2,3},{3,2},{4,5},{5,4},{6,7},{7,6},{8,9},{9,8},{10,11... | collective-permute-start | bytes 786440 | tf_op jit(solution)/shard_map/ppermute | solution.py:496
  29.2 3.2 %shard_map.99 = (bf16[1024,128]{1,0:T(8,128)(2,1)S(1)}, bf16[1024,128]{1,0:T(8,128)(2,1)S(1)}) custom-call(bf16[1024,128]{1,0:T(8,128)(2,1)S(1)} %get-tuple-element.51.basis, bf16[128,1024]{1,0:T(8,128)(2,1)S(1)} %get-tuple-element.52.edge, bf16[128,1024]{1,0:T(8,128)(2,1)S(1)} %get-tuple-element.53.lanes, bf16[512,512]{1,0:T(8,128)(2,1)S(1)} %get-tuple-element.54.kron, ...), custom_call_target="tpu_custom_call" | custom-call | flops 4294967296 | bytes 2097152 | tf_op jit(solution)/shard_map/pallas_call | solution.py:472
  32.3 0.1 collective-permute-start.4
  32.4 0.0 collective-permute-done.5.carried
  32.4 3.5 %shard_map.100 = f32[2,4096]{1,0:T(2,128)} custom-call(bf16[512,2048]{1,0:T(8,128)(2,1)S(1)} %get-tuple-element.57.x_first, bf16[1024,128]{1,0:T(8,128)(2,1)S(1)} %get-tuple-element.58.back, bf16[1024,128]{1,0:T(8,128)(2,1)S(1)} %collective-permute-done.5.carried, s32[1,1]{1,0:T(1,128)S(6)} %copy.10.choice), custom_call_target="tpu_custom_call" | custom-call | flops 2147483648 | bytes 2097152 | tf_op jit(solution)/shard_map/pallas_call | solution.py:472
  36.0 0.0 collective-permute-done.4
  36.0 1.8 %select_bitcast_fusion = (bf16[1,1,128,8,128]{4,3,2,1,0:T(8,128)(2,1)}, bf16[1,1,128,8,128]{4,3,2,1,0:T(8,128)(2,1)}) fusion(bf16[1024,128]{1,0:T(8,128)(2,1)} %collective-permute-done.4, bf16[1024,128]{1,0:T(8,128)(2,1)S(1)} %get-tuple-element.61, pred[]{:T(512)S(6)} %eq.3), kind=kLoop, calls=%fused_computation | loop fusion | flops 262144 | bytes 1048577 | tf_op jit(solution)/shard_map/reshape | solution.py:599
Async XLA Ops:
  2.3 12.5 %collective-permute-start = (bf16[32,128]{1,0:T(8,128)(2,1)S(1)}, bf16[32,128]{1,0:T(8,128)(2,1)S(1)}, u32[]{:S(2)}, u32[]{:S(2)}) collective-permute-start(bf16[32,128]{1,0:T(8,128)(2,1)S(1)} %get-tuple-element.34.site), channel_id=1, source_target_pairs={{0,1},{1,0},{2,3},{3,2},{4,5},{5,4},{6,7},{7,6},{8,9},{9,8},{10,11... | collective-permute-start | bytes 24584 | tf_op jit(solution)/shard_map/ppermute | solution.py:496
  2.9 15.9 %collective-permute-start.1 = (bf16[1024,128]{1,0:T(8,128)(2,1)S(1)}, bf16[1024,128]{1,0:T(8,128)(2,1)S(1)}, u32[]{:S(2)}, u32[]{:S(2)}) collective-permute-start(bf16[1024,128]{1,0:T(8,128)(2,1)S(1)} %get-tuple-element.40), channel_id=1, source_target_pairs={{0,2},{2,4},{4,6},{6,8},{8,10},{10,12},{12,14},{14,0},{1,15},{3,1}... | collective-permute-start | bytes 786440 | tf_op jit(solution)/shard_map/ppermute | solution.py:492
  5.4 13.4 %collective-permute-start.2 = (bf16[1024,128]{1,0:T(8,128)(2,1)S(1)}, bf16[1024,128]{1,0:T(8,128)(2,1)S(1)}, u32[]{:S(2)}, u32[]{:S(2)}) collective-permute-start(bf16[1024,128]{1,0:T(8,128)(2,1)S(1)} %get-tuple-element.41), channel_id=1, source_target_pairs={{0,15},{2,1},{4,3},{6,5},{8,7},{10,9},{12,11},{14,13},{1,2},{3,4},... | collective-permute-start | bytes 786440 | tf_op jit(solution)/shard_map/ppermute | solution.py:492
  18.8 9.2 %collective-permute-start.3 = (bf16[1024,128]{1,0:T(8,128)(2,1)S(1)}, bf16[1024,128]{1,0:T(8,128)(2,1)S(1)}, u32[]{:S(2)}, u32[]{:S(2)}) collective-permute-start(bf16[1024,128]{1,0:T(8,128)(2,1)S(1)} %collective-permute-done.2.arrived_y), channel_id=1, source_target_pairs={{0,1},{1,0},{2,3},{3,2},{4,5},{5,4},{6,7},{7,6},{8,9},{9,8},{10,11... | collective-permute-start | bytes 786440 | tf_op jit(solution)/shard_map/ppermute | solution.py:496
  28.6 3.9 %collective-permute-start.5 = (bf16[1024,128]{1,0:T(8,128)(2,1)S(1)}, bf16[1024,128]{1,0:T(8,128)(2,1)S(1)}, u32[]{:S(2)}, u32[]{:S(2)}) collective-permute-start(bf16[1024,128]{1,0:T(8,128)(2,1)S(1)} %get-tuple-element.59), channel_id=1, source_target_pairs={{0,1},{1,0},{2,3},{3,2},{4,5},{5,4},{6,7},{7,6},{8,9},{9,8},{10,11... | collective-permute-start | bytes 786440 | tf_op jit(solution)/shard_map/ppermute | solution.py:496
  32.3 3.6 %collective-permute-start.4 = (bf16[1024,128]{1,0:T(8,128)(2,1)S(1)}, bf16[1024,128]{1,0:T(8,128)(2,1)}, u32[]{:S(2)}, u32[]{:S(2)}) collective-permute-start(bf16[1024,128]{1,0:T(8,128)(2,1)S(1)} %get-tuple-element.56), channel_id=1, source_target_pairs={{0,1},{1,0},{2,3},{3,2},{4,5},{5,4},{6,7},{7,6},{8,9},{9,8},{10,11... | collective-permute-start | bytes 786440 | tf_op jit(solution)/shard_map/ppermute | solution.py:496

commit v2 on v1

--- a/solution.py
+++ b/solution.py
@@ -102,15 +102,16 @@
     return scratch[pl.ds(j, chi, stride=scratch.shape[0] // chi), :]
 
 
-def kron_step(lhs, rhs, x_ref, t, transposed=False):
+def kron_step(lhs, rhs, x_ref, t, first, count, transposed):
     chi = lhs.shape[1]
     bond = lhs.shape[0] // chi
+    some = lhs[first * chi : (first + count) * chi, :]
     if transposed:
-        product = nt(lhs[...], rhs[t * chi : (t + 2) * chi, :])
+        product = nt(some, rhs[t * chi : (t + 2) * chi, :])
     else:
-        product = nn(lhs[...], rhs[:, t * chi : (t + 2) * chi])
-    for s in range(bond):
-        at = (s * bond + t) * 8
+        product = nn(some, rhs[:, t * chi : (t + 2) * chi])
+    for s in range(count):
+        at = ((first + s) * bond + t) * 8
         for g in range(chi // 8):
             rows = product[s * chi + g * 8 : s * chi + g * 8 + 8, :]
             x_ref[at : at + 16, g * chi : (g + 1) * chi] = jnp.concatenate(
@@ -118,28 +119,36 @@
             ).astype(BF16)
 
 
-def absorb_step(kron, x_ref, m_ref, g, chi):
+def absorb_step(kron, x_ref, m_ref, chi, g, first, count):
     bond = m_ref.shape[0] // chi
-    out = nn(kron[...], x_ref[:, g * chi : (g + 2) * chi])
-    for o in range(bond):
+    step = bond * 8
+    out = nn(kron[first * step : (first + count) * step, :], x_ref[:, g * chi : (g + 2) * chi])
+    for o in range(count):
         for d in range(bond):
             rows = out[(o * bond + d) * 8 : (o * bond + d) * 8 + 8, :]
-            at = o * chi + g * 8
+            at = (first + o) * chi + g * 8
             m_ref[at : at + 16, d * chi : (d + 1) * chi] = jnp.concatenate(
                 [rows[:, :chi], rows[:, chi:]], axis=0
             ).astype(BF16)
 
 
-def kron_steps(lhs, rhs, x_ref, transposed=False):
+def kron_steps(lhs, rhs, x_ref, transposed=False, count=1):
     bond = lhs.shape[0] // lhs.shape[1]
+    count = min(count, bond)
     return [
-        functools.partial(kron_step, lhs, rhs, x_ref, t, transposed) for t in range(0, bond, 2)
+        functools.partial(kron_step, lhs, rhs, x_ref, t, first, count, transposed)
+        for t in range(0, bond, 2)
+        for first in range(0, bond, count)
     ]
 
 
-def absorb_steps(kron, x_ref, m_ref, chi):
+def absorb_steps(kron, x_ref, m_ref, chi, count=2):
+    bond = m_ref.shape[0] // chi
+    count = min(count, bond)
     return [
-        functools.partial(absorb_step, kron, x_ref, m_ref, g, chi) for g in range(0, chi // 8, 2)
+        functools.partial(absorb_step, kron, x_ref, m_ref, chi, g, first, count)
+        for g in range(0, chi // 8, 2)
+        for first in range(0, bond, count)
     ]
 
 
@@ -226,11 +235,17 @@
     top_hbm,
     bottom_hbm,
     sketch_hbm,
+    site,
+    site_other,
     basis,
     basis_lanes,
     edge,
     first,
     sketch_t,
+    kron_0,
+    kron_1,
+    kron_first,
+    kron_sketch,
     top,
     bottom,
     sketch,
@@ -277,10 +292,33 @@
     def turn_sketch(o):
         sketch_t[o * chi : (o + 1) * chi, :] = leg(wide_sketch, o).T.astype(BF16)
 
+    is_left = side == 0
+    size = bond * bond
+    swap = swap_order(size, bond)
+    rows_of = spread(size)
+    core = square_core(site[...])
+    core_other = square_core(site_other[...])
+    mirrored_own = mirrored(core, bond)
+    mirrored_other = mirrored(core_other, bond)
+    ahead = spread_ahead(core, bond)
+    turned = nn(nn(swap, mirrored_own).astype(BF16), swap).astype(BF16)
+    krons = (
+        (kron_sketch, nn(rows_of, turned), spread_turned(core_other, bond)),
+        (kron_0, ahead, nn(rows_of, mirrored_other)),
+        (kron_first, ahead, spread_back(core, bond)),
+        (kron_1, spread_ahead(core_other, bond), nn(rows_of, mirrored_own)),
+    )
+
+    def build_kron(target, left, right, part):
+        step = size * 8 // 4
+        at = slice(part * step, (part + 1) * step)
+        target[at, :] = kron_of(jnp.where(is_left, left[at, :], right[at, :]), size)
+
     inverse_top, inverse_bottom = chol_inverse(
         [nt(legs_top[...], legs_top[...]), nt(legs_bottom[...], legs_bottom[...])],
         1,
-        [functools.partial(turn_sketch, o) for o in range(bond)],
+        [functools.partial(turn_sketch, o) for o in range(bond)]
+        + [functools.partial(build_kron, *args, part) for args in krons for part in range(4)],
     )
     high, low = split(inverse_top)
     ortho = (nn(high, legs_top[...]) + nn(low, legs_top[...])).astype(BF16)
@@ -295,37 +333,15 @@
     chi = closing.shape[0]
     bond = absorbed.shape[0] // chi
     unscaled = nt(absorbed[...], closing)
-    mean = jnp.sum(unscaled * unscaled) * (1.0 / (unscaled.shape[0] * unscaled.shape[1]))
-    scaled = unscaled * lax.rsqrt(mean + 1e-06)
     for o in range(bond):
-        wide[pl.ds(o, chi, stride=bond), :] = scaled[o * chi : (o + 1) * chi, :]
-    return wide[...].astype(BF16)
-
-
-def prepare_kernel(
-    basis_lanes, sketch_t, site, site_other, kron_0, kron_1, kron_first, sketched, x, kron_sketch
-):
-    side = lax.axis_index("row")
+        wide[pl.ds(o, chi, stride=bond), :] = unscaled[o * chi : (o + 1) * chi, :]
+    squares = jnp.sum(unscaled * unscaled, axis=0, keepdims=True)
+    mean = jnp.sum(squares, axis=1, keepdims=True) * (1.0 / (chi * bond * chi))
+    return (wide[...] * lax.rsqrt(mean + 1e-06)).astype(BF16)
+
+
+def prepare_kernel(basis_lanes, sketch_t, kron_sketch, sketched, x):
     chi = basis_lanes.shape[0]
-    bond = basis_lanes.shape[1] // chi
-    size = bond * bond
-    is_left = side == 0
-    core = square_core(site[...])
-    other = square_core(site_other[...])
-    mirrored_own = mirrored(core, bond)
-    mirrored_other = mirrored(other, bond)
-    swap = swap_order(size, bond)
-    wide = spread(size)
-    ahead = spread_ahead(core, bond)
-    kron_0[...] = kron_of(jnp.where(is_left, ahead, nn(wide, mirrored_other)), size)
-    kron_1[...] = kron_of(
-        jnp.where(is_left, spread_ahead(other, bond), nn(wide, mirrored_own)), size
-    )
-    kron_first[...] = kron_of(jnp.where(is_left, ahead, spread_back(core, bond)), size)
-    turned = nn(nn(swap, mirrored_own).astype(BF16), swap).astype(BF16)
-    kron_sketch[...] = kron_of(
-        jnp.where(is_left, nn(wide, turned), spread_turned(other, bond)), size
-    )
     for step in kron_steps(sketch_t, basis_lanes, x) + absorb_steps(kron_sketch, x, sketched, chi):
         step()
 
@@ -343,8 +359,8 @@
     x_first,
     middle,
     lanes_1,
-    wide_x,
-    wide_y,
+    wide_0,
+    wide_1,
     rows_0,
     lanes_0,
     ahead,
@@ -355,40 +371,52 @@
     chi = basis.shape[1]
     bond = basis.shape[0] // chi
     blocks = [slice(j * chi, (j + 1) * chi) for j in range(bond)]
-    wide_x[...] = arrived_x[...].astype(F32)
-    wide_y[...] = arrived_y[...].astype(F32)
+    @pl.when(is_left)
+    def _():
+        wide_0[...] = arrived_x[...].astype(F32)
+
+    @pl.when(jnp.logical_not(is_left))
+    def _():
+        wide_0[...] = arrived_y[...].astype(F32)
+
     for j in range(bond):
-        block = jnp.where(is_left, leg(wide_x, j), leg(wide_y, j)).astype(BF16)
-        rows_0[blocks[j], :] = block
-        lanes_0[:, blocks[j]] = block
+        rows_0[blocks[j], :] = leg(wide_0, j).astype(BF16)
     stacked = nn(sketched[...], rows_0[...])
     range_t = jnp.concatenate([stacked[blocks[d], :] for d in range(bond)], axis=1)
     high, low = split(range_t)
     gram = nt(high, high) + (nt(high, low) + nt(low, high))
 
+    def ready_lanes():
+        for j in range(bond):
+            lanes_0[:, blocks[j]] = rows_0[blocks[j], :]
+
+    def ready_other(part):
+        step = wide_1.shape[0] // 4
+        at = slice(part * step, (part + 1) * step)
+        wide_1[at, :] = jnp.where(is_left, arrived_y[at, :], arrived_x[at, :]).astype(F32)
+
     def ready_ahead(j):
-        block = leg(wide_x, j)
-        ahead[:, blocks[j]] = jnp.where(is_left, block, block.T).astype(BF16)
-
-    def ready_next(j):
-        lanes_1[:, blocks[j]] = jnp.where(is_left, leg(wide_y, j), leg(wide_x, j)).astype(BF16)
+        block = leg(wide_1, j)
+        lanes_1[:, blocks[j]] = block.astype(BF16)
+        ahead[:, blocks[j]] = jnp.where(is_left, leg(wide_0, j), block.T).astype(BF16)
 
     beside = (
-        kron_steps(basis, lanes_0, x)
+        [ready_lanes]
+        + kron_steps(basis, lanes_0, x)
+        + [functools.partial(ready_other, part) for part in range(4)]
         + absorb_steps(kron_0, x, absorbed, chi)
         + [functools.partial(ready_ahead, j) for j in range(bond)]
         + kron_steps(first, ahead, x_first)
         + absorb_steps(kron_first, x_first, middle, chi)
-        + [functools.partial(ready_next, j) for j in range(bond)]
-    )
-    (inverse,) = chol_inverse([gram], 2, beside)
+    )
+    (inverse,) = chol_inverse([gram], 3, beside)
     inverse_high, inverse_low = split(inverse)
     closing = (
         nn(inverse_high, high) + (nn(inverse_high, low) + nn(inverse_low, high))
     ).astype(BF16)
     for d in range(bond):
         next_basis[blocks[d], :] = closing[:, blocks[d]]
-    new[...] = finish(absorbed, closing, wide_x)
+    new[...] = finish(absorbed, closing, wide_0)
 
 
 def state_kernel(middle, received, carried, back, wide, behind):
@@ -436,33 +464,63 @@
         send[...] = new_0[...]
 
 
-def gradient_kernel(x_first, back, carried, choice, gradient, x_second):
+def product_kernel(x_first, back, carried, product, x_second):
     side = lax.axis_index("row")
-    chi = back.shape[1]
-    bond = back.shape[0] // chi
-    size = bond * bond
     for step in kron_steps(back, carried, x_second, True):
         step()
-    product = nt(x_first[...], x_second[...])
+
+    @pl.when(side == 0)
+    def _():
+        product[...] = nt(x_first[...], x_second[...])
+
+    @pl.when(side == 1)
+    def _():
+        product[...] = nt(x_second[...], x_first[...])
+
+
+def place_kernel(product, choice, keep, received, gradient, left, right, entries, sems):
+    side = lax.axis_index("row")
+    is_left = side == 0
+    phys_count = gradient.shape[0]
+    size = product.shape[0] // 8
+    bond = round(size**0.5)
+    chi = keep.shape[1]
+
+    def start(one, other):
+        pltpu.make_async_copy(one, left, sems.at[0]).start()
+        pltpu.make_async_copy(other, right, sems.at[1]).start()
+
+    pl.when(side == 0)(functools.partial(start, keep, received))
+    pl.when(side == 1)(functools.partial(start, received, keep))
+
+    def one_hot(i, j, swapped):
+        i = i // 8
+        other = (i % bond) * bond + i // bond
+        return jnp.where(j == jnp.where(swapped, other, i), 1.0, 0.0).astype(BF16)
+
     i = iota(product.shape, 0)
     j = iota(product.shape, 1)
-    product = jnp.where(i % 8 == j % 8, product, 0.0)
-    gather = spread(size)
-    high, low = split(product)
-    half = nn(high, gather) + nn(low, gather)
-    i = iota((size, size * 8), 0)
-    j = iota((size, size * 8), 1) // 8
-    ordered = jnp.where((i // bond == j % bond) & (i % bond == j // bond), 1.0, 0.0).astype(BF16)
-    high, low = split(half)
-    env = nn(ordered, high) + nn(ordered, low)
-    env = jnp.where(side == 0, env, env.T) * (bond / chi)
-    for p in range(gradient.shape[0]):
-        kept = jnp.where(choice[0, 0] == p, env, 0.0)
-        for r in range(size):
-            gradient[p : p + 1, r * size : (r + 1) * size] = kept[r : r + 1, :]
-
-
-def call(kernel, out_shapes, scratch, inputs, flops, in_place=(), copies=0):
+    diagonal = jnp.where(i % 8 == j % 8, product[...], 0.0).astype(BF16)
+    wide = (size * 8, size * 2)
+    half = jnp.zeros((size // 2, size * 2), F32)
+    for odd in range(2):
+        columns = one_hot(iota(wide, 0), iota(wide, 1) - odd * size, side == 1)
+        rows = one_hot(iota(wide[::-1], 1), iota(wide[::-1], 0) * 2 + odd, is_left)[: size // 2]
+        high, low = split(nn(diagonal, columns))
+        half = half + (nn(rows, high) + nn(rows, low))
+    half = half * (bond / chi)
+    phys = iota((phys_count, size * 2), 0)
+    for r in range(size // 2):
+        row = jnp.broadcast_to(half[r : r + 1, :], phys.shape)
+        entries[:, r * size * 2 : (r + 1) * size * 2] = jnp.where(phys == choice[0, 0], row, 0.0)
+    copy = pltpu.make_async_copy(entries, gradient, sems.at[2])
+    copy.start()
+    pltpu.make_async_copy(keep, left, sems.at[0]).wait()
+    pltpu.make_async_copy(keep, right, sems.at[1]).wait()
+    copy.wait()
+
+
+def call(kernel, out_shapes, scratch, inputs, flops, in_place=(), copies=0, out_space=pltpu.VMEM):
     inputs = [
         pltpu.with_memory_space_constraint(x, pltpu.HBM) if i in in_place else x
         for i, x in enumerate(inputs)
@@ -480,7 +538,7 @@
             else vmem
             for i, x in enumerate(inputs)
         ],
-        out_specs=[vmem for _ in out_shapes],
+        out_specs=[pl.BlockSpec(memory_space=out_space) for _ in out_shapes],
         scratch_shapes=[pltpu.VMEM(s, t) for s, t in scratch]
         + ([pltpu.SemaphoreType.DMA((copies,))] if copies else []),
         compiler_params=pltpu.CompilerParams(vmem_limit_bytes=VMEM_BYTES),
@@ -508,7 +566,6 @@
     square = (rows, rows)
     count = lax.axis_size("col")
     sites = site_tensors.reshape(site_tensors.shape[2:])
-    is_upper = lax.axis_index("row") == 0
     first_sent, second_sent, site = call(
         begin_kernel,
         [(tall, BF16), (tall, BF16), ((size // 2, size * 2), BF16)],
@@ -532,21 +589,20 @@
         + [(2 * c + 1, ahead[c]) for c in range(count)],
     )
     site_other = exchanged(site, "row")
-    basis, basis_lanes, edge, first, sketch_t = call(
+    basis, basis_lanes, edge, first, sketch_t, kron_0, kron_1, kron_first, kron_sketch = call(
         edges_kernel,
-        [(tall, BF16), (flat, BF16), (flat, BF16), (tall, BF16), (tall, BF16)],
+        [(tall, BF16), (flat, BF16), (flat, BF16), (tall, BF16), (tall, BF16)] + [(kron, BF16)] * 4,
         [(tall, BF16)] * 3 + [(tall, F32), (tall, F32), (flat, BF16), (flat, BF16)],
-        [top_env.reshape(tall), bottom_env.reshape(tall), sketch],
+        [top_env.reshape(tall), bottom_env.reshape(tall), sketch, site, site_other],
         2**31,
         in_place=(0, 1, 2),
         copies=3,
     )
-    site_other, basis_lanes = lax.optimization_barrier((site_other, basis_lanes))
-    kron_0, kron_1, kron_first, sketched = call(
+    (sketched,) = call(
         prepare_kernel,
-        [(kron, BF16), (kron, BF16), (kron, BF16), (square, BF16)],
-        [(stack, BF16), (kron, BF16)],
-        [basis_lanes, sketch_t, site, site_other],
+        [(square, BF16)],
+        [(stack, BF16)],
+        [basis_lanes, sketch_t, kron_sketch],
         2**31,
     )
     sketched, arrived_x, arrived_y = lax.optimization_barrier((sketched, arrived_x, arrived_y))
@@ -583,16 +639,23 @@
         2**32,
     )
     received = exchanged(send, "row")
-    (gradient,) = call(
-        gradient_kernel,
+    (product,) = call(
+        product_kernel,
+        [(kron, F32)],
+        [(stack, BF16)],
+        [x_first, back, carried],
+        2**31,
+    )
+    received, product = lax.optimization_barrier((received, product))
+    gradient, left_new, right_new = call(
+        place_kernel,
+        [(sites.shape, F32), (tall, BF16), (tall, BF16)],
         [(sites.shape, F32)],
-        [(stack, BF16)],
-        [x_first, back, carried, configuration],
-        2**31,
-    )
-    received, gradient = lax.optimization_barrier((received, gradient))
-    left_new = jnp.where(is_upper, keep, received)
-    right_new = jnp.where(is_upper, received, keep)
+        [product, configuration, keep, received],
+        2**30,
+        copies=3,
+        out_space=pltpu.HBM,
+    )
     return (
         gradient.reshape(site_tensors.shape),
         left_new.reshape(left_bounds.shape),

time: 38.1 us -> 34.1 us (0.90)
  Pallas kernels: 27.4 us -> 24.8 us
  other arithmetic: 1.78 us -> 0 us
    pallas_call x7 -> x8, Pallas kernels: 27.4 us -> 24.8 us  [call(): pl.pallas_call(kernel, out_shape=[jax.ShapeDtypeStruct(s, t) for s, t in...]
    reshape x1 -> x0, other arithmetic: 1.78 us -> none  [local(): right_new.reshape(right_bounds.shape)]
  transfers between devices with their start and end apart: 6 -> 6, of which waited for: 0 -> 0; matrix products, arithmetic and copies ran while one was open for 0% -> 0% of each run, Pallas kernels for 68% -> 63%
where the time goes in v2:
time: 34.1 us; the launch traced here: 33.8 us
  Pallas kernels  24.8 us (73%)
  starting transfers between devices  7.44 us (22%)
  between operations  1.53 us (4%)
    pallas_call x8, Pallas kernels, call(): pl.pallas_call(kernel, out_shape=[jax.ShapeDtypeStruct(s, t) for s, t in...  24.8 us
    ppermute x2, starting transfers between devices, moved(): return lax.ppermute(block, ('col', 'row'), pairs)  5.89 us
    ppermute x4, starting transfers between devices, exchanged(): return lax.ppermute(block, axis, [(0, 1), (1, 0)])  1.55 us
  transfers between devices with their start and end apart: 6, of which 0 were waited for; matrix products, arithmetic and copies ran while one was open for 0% of the time, Pallas kernels for 63%

profile of v2, /device:TPU:0, one launch (start us, length us, event | category | flops | bytes accessed | tf_op | source)
XLA Modules:
  0.0 33.8 jit_solution(3642355135443122869)
XLA Ops:
  1.3 1.1 %shard_map.94 = (bf16[1024,128]{1,0:T(8,128)(2,1)S(1)}, bf16[1024,128]{1,0:T(8,128)(2,1)S(1)}, bf16[32,128]{1,0:T(8,128)(2,1)S(1)}) custom-call(bf16[1024,128]{1,0:T(8,128)(2,1)} %bitcast.8, bf16[1024,128]{1,0:T(8,128)(2,1)} %bitcast.9, bf16[2,4096]{1,0:T(2,128)(2,1)} %bitcast.10, s32[1,1]{1,0:T(1,128)S(6)} %copy.10.choice), custom_call_target="tpu_custom_call" | custom-call | flops 1048576 | bytes 2097152 | tf_op jit(solution)/shard_map/pallas_call | solution.py:530
  2.3 0.5 %collective-permute-start = (bf16[32,128]{1,0:T(8,128)(2,1)S(1)}, bf16[32,128]{1,0:T(8,128)(2,1)S(1)}, u32[]{:S(2)}, u32[]{:S(2)}) collective-permute-start(bf16[32,128]{1,0:T(8,128)(2,1)S(1)} %get-tuple-element.34.site), channel_id=1, source_target_pairs={{0,1},{1,0},{2,3},{3,2},{4,5},{5,4},{6,7},{7,6},{8,9},{9,8},{10,11... | collective-permute-start | bytes 24584 | tf_op jit(solution)/shard_map/ppermute | solution.py:554
  2.9 2.6 %collective-permute-start.1 = (bf16[1024,128]{1,0:T(8,128)(2,1)S(1)}, bf16[1024,128]{1,0:T(8,128)(2,1)S(1)}, u32[]{:S(2)}, u32[]{:S(2)}) collective-permute-start(bf16[1024,128]{1,0:T(8,128)(2,1)S(1)} %get-tuple-element.39), channel_id=1, source_target_pairs={{0,2},{2,4},{4,6},{6,8},{8,10},{10,12},{12,14},{14,0},{1,15},{3,1}... | collective-permute-start | bytes 786440 | tf_op jit(solution)/shard_map/ppermute | solution.py:550
  5.4 3.3 %collective-permute-start.2 = (bf16[1024,128]{1,0:T(8,128)(2,1)S(1)}, bf16[1024,128]{1,0:T(8,128)(2,1)S(1)}, u32[]{:S(2)}, u32[]{:S(2)}) collective-permute-start(bf16[1024,128]{1,0:T(8,128)(2,1)S(1)} %get-tuple-element.40), channel_id=1, source_target_pairs={{0,15},{2,1},{4,3},{6,5},{8,7},{10,9},{12,11},{14,13},{1,2},{3,4},... | collective-permute-start | bytes 786440 | tf_op jit(solution)/shard_map/ppermute | solution.py:550
  8.8 0.0 collective-permute-done.site_other
  8.8 7.2 %shard_map.95 = (bf16[1024,128]{1,0:T(8,128)(2,1)S(1)}, bf16[128,1024]{1,0:T(8,128)(2,1)S(1)}, bf16[128,1024]{1,0:T(8,128)(2,1)S(1)}, bf16[1024,128]{1,0:T(8,128...) custom-call(bf16[1024,128]{1,0:T(8,128)(2,1)} %bitcast.11, ...), custom_call_target="tpu_custom_call" | custom-call | flops 2147483648 | bytes 2097152 | tf_op jit(solution)/shard_map/pallas_call | solution.py:530
  15.9 1.9 %shard_map.96.sketched = bf16[1024,1024]{1,0:T(8,128)(2,1)S(1)} custom-call(bf16[128,1024]{1,0:T(8,128)(2,1)S(1)} %get-tuple-element.36.basis_lanes, bf16[1024,128]{1,0:T(8,128)(2,1)S(1)} %get-tuple-element.37.sketch_t, bf16[512,512]{1,0:T(8,128)(2,1)S(1)} %get-tuple-element.38.kron_sketch), custom_call_target="tpu_custom_call" | custom-call | flops 2147483648 | bytes 2097152 | tf_op jit(solution)/shard_map/pallas_call | solution.py:530
  17.8 0.0 collective-permute-done.1.arrived_x
  17.8 0.0 collective-permute-done.2.arrived_y
  17.9 0.4 %collective-permute-start.3 = (bf16[1024,128]{1,0:T(8,128)(2,1)S(1)}, bf16[1024,128]{1,0:T(8,128)(2,1)S(1)}, u32[]{:S(2)}, u32[]{:S(2)}) collective-permute-start(bf16[1024,128]{1,0:T(8,128)(2,1)S(1)} %collective-permute-done.2.arrived_y), channel_id=1, source_target_pairs={{0,1},{1,0},{2,3},{3,2},{4,5},{5,4},{6,7},{7,6},{8,9},{9,8},{10,11... | collective-permute-start | bytes 786440 | tf_op jit(solution)/shard_map/ppermute | solution.py:554
  18.2 7.8 %shard_map.97 = (bf16[1024,128]{1,0:T(8,128)(2,1)S(1)}, bf16[1024,128]{1,0:T(8,128)(2,1)S(1)}, bf16[512,2048]{1,0:T(8,128)(2,1)S(1)}, bf16[1024,1024]{1,0:T(8,128)(2,1)S(1)}, bf16[128,1024]{1,0:T(8,128)(2,1)S(1)}) custom-call(bf16[1024,128]{1,0:T(8,128)(2,1)S(1)} %get-tuple-element.35.basis, bf16[1024,1024]{1,0:T(8,128)(2,1)S(1)} %shard_map.96.sketched, ...), custom_call_target="tpu_custom_call" | custom-call | flops 8589934592 | bytes 2097152 | tf_op jit(solution)/shard_map/pallas_call | solution.py:530
  26.0 0.0 collective-permute-done.3.received
  26.0 0.6 %shard_map.98 = (bf16[1024,128]{1,0:T(8,128)(2,1)S(1)}, bf16[1024,128]{1,0:T(8,128)(2,1)S(1)}) custom-call(bf16[1024,1024]{1,0:T(8,128)(2,1)S(1)} %get-tuple-element.48.middle, bf16[1024,128]{1,0:T(8,128)(2,1)S(1)} %collective-permute-done.3.received), custom_call_target="tpu_custom_call" | custom-call | flops 1073741824 | bytes 2097152 | tf_op jit(solution)/shard_map/pallas_call | solution.py:530
  26.7 0.3 collective-permute-start.5
  27.0 2.6 %shard_map.99 = (bf16[1024,128]{1,0:T(8,128)(2,1)S(1)}, bf16[1024,128]{1,0:T(8,128)(2,1)S(1)}) custom-call(bf16[1024,128]{1,0:T(8,128)(2,1)S(1)} %get-tuple-element.50.basis, bf16[128,1024]{1,0:T(8,128)(2,1)S(1)} %get-tuple-element.51.edge, bf16[128,1024]{1,0:T(8,128)(2,1)S(1)} %get-tuple-element.52.lanes, bf16[512,512]{1,0:T(8,128)(2,1)S(1)} %get-tuple-element.53.kron, ...), custom_call_target="tpu_custom_call" | custom-call | flops 4294967296 | bytes 2097152 | tf_op jit(solution)/shard_map/pallas_call | solution.py:530
  29.6 0.4 %collective-permute-start.4 = (bf16[1024,128]{1,0:T(8,128)(2,1)S(1)}, bf16[1024,128]{1,0:T(8,128)(2,1)S(1)}, u32[]{:S(2)}, u32[]{:S(2)}) collective-permute-start(bf16[1024,128]{1,0:T(8,128)(2,1)S(1)} %get-tuple-element.55), channel_id=1, source_target_pairs={{0,1},{1,0},{2,3},{3,2},{4,5},{5,4},{6,7},{7,6},{8,9},{9,8},{10,11... | collective-permute-start | bytes 786440 | tf_op jit(solution)/shard_map/ppermute | solution.py:554
  29.9 0.0 collective-permute-done.5.carried
  29.9 2.0 %shard_map.100.product = f32[512,512]{1,0:T(8,128)S(1)} custom-call(bf16[512,2048]{1,0:T(8,128)(2,1)S(1)} %get-tuple-element.56.x_first, bf16[1024,128]{1,0:T(8,128)(2,1)S(1)} %get-tuple-element.57.back, bf16[1024,128]{1,0:T(8,128)(2,1)S(1)} %collective-permute-done.5.carried), custom_call_target="tpu_custom_call" | custom-call | flops 2147483648 | bytes 2097152 | tf_op jit(solution)/shard_map/pallas_call | solution.py:530
  31.9 0.0 collective-permute-done.4.received
  31.9 1.7 %shard_map.101 = (f32[2,4096]{1,0:T(2,128)}, bf16[1024,128]{1,0:T(8,128)(2,1)}, bf16[1024,128]{1,0:T(8,128)(2,1)}) custom-call(f32[512,512]{1,0:T(8,128)S(1)} %shard_map.100.product, s32[1,1]{1,0:T(1,128)S(6)} %copy.10.choice, bf16[1024,128]{1,0:T(8,128)(2,1)S(1)} %get-tuple-element.60.keep, bf16[1024,128]{1,0:T(8,128)(2,1)S(1)} %collective-permute-done.4.received), custom_call_target="tpu_custom_call" | custom-call | flops 1073741824 | bytes 2097152 | tf_op jit(solution)/shard_map/pallas_call | solution.py:530
Async XLA Ops:
  2.3 6.4 %collective-permute-start = (bf16[32,128]{1,0:T(8,128)(2,1)S(1)}, bf16[32,128]{1,0:T(8,128)(2,1)S(1)}, u32[]{:S(2)}, u32[]{:S(2)}) collective-permute-start(bf16[32,128]{1,0:T(8,128)(2,1)S(1)} %get-tuple-element.34.site), channel_id=1, source_target_pairs={{0,1},{1,0},{2,3},{3,2},{4,5},{5,4},{6,7},{7,6},{8,9},{9,8},{10,11... | collective-permute-start | bytes 24584 | tf_op jit(solution)/shard_map/ppermute | solution.py:554
  2.9 15.0 %collective-permute-start.1 = (bf16[1024,128]{1,0:T(8,128)(2,1)S(1)}, bf16[1024,128]{1,0:T(8,128)(2,1)S(1)}, u32[]{:S(2)}, u32[]{:S(2)}) collective-permute-start(bf16[1024,128]{1,0:T(8,128)(2,1)S(1)} %get-tuple-element.39), channel_id=1, source_target_pairs={{0,2},{2,4},{4,6},{6,8},{8,10},{10,12},{12,14},{14,0},{1,15},{3,1}... | collective-permute-start | bytes 786440 | tf_op jit(solution)/shard_map/ppermute | solution.py:550
  5.4 12.4 %collective-permute-start.2 = (bf16[1024,128]{1,0:T(8,128)(2,1)S(1)}, bf16[1024,128]{1,0:T(8,128)(2,1)S(1)}, u32[]{:S(2)}, u32[]{:S(2)}) collective-permute-start(bf16[1024,128]{1,0:T(8,128)(2,1)S(1)} %get-tuple-element.40), channel_id=1, source_target_pairs={{0,15},{2,1},{4,3},{6,5},{8,7},{10,9},{12,11},{14,13},{1,2},{3,4},... | collective-permute-start | bytes 786440 | tf_op jit(solution)/shard_map/ppermute | solution.py:550
  17.9 8.2 %collective-permute-start.3 = (bf16[1024,128]{1,0:T(8,128)(2,1)S(1)}, bf16[1024,128]{1,0:T(8,128)(2,1)S(1)}, u32[]{:S(2)}, u32[]{:S(2)}) collective-permute-start(bf16[1024,128]{1,0:T(8,128)(2,1)S(1)} %collective-permute-done.2.arrived_y), channel_id=1, source_target_pairs={{0,1},{1,0},{2,3},{3,2},{4,5},{5,4},{6,7},{7,6},{8,9},{9,8},{10,11... | collective-permute-start | bytes 786440 | tf_op jit(solution)/shard_map/ppermute | solution.py:554
  26.7 3.3 %collective-permute-start.5 = (bf16[1024,128]{1,0:T(8,128)(2,1)S(1)}, bf16[1024,128]{1,0:T(8,128)(2,1)S(1)}, u32[]{:S(2)}, u32[]{:S(2)}) collective-permute-start(bf16[1024,128]{1,0:T(8,128)(2,1)S(1)} %get-tuple-element.58), channel_id=1, source_target_pairs={{0,1},{1,0},{2,3},{3,2},{4,5},{5,4},{6,7},{7,6},{8,9},{9,8},{10,11... | collective-permute-start | bytes 786440 | tf_op jit(solution)/shard_map/ppermute | solution.py:554
  29.6 2.4 %collective-permute-start.4 = (bf16[1024,128]{1,0:T(8,128)(2,1)S(1)}, bf16[1024,128]{1,0:T(8,128)(2,1)S(1)}, u32[]{:S(2)}, u32[]{:S(2)}) collective-permute-start(bf16[1024,128]{1,0:T(8,128)(2,1)S(1)} %get-tuple-element.55), channel_id=1, source_target_pairs={{0,1},{1,0},{2,3},{3,2},{4,5},{5,4},{6,7},{7,6},{8,9},{9,8},{10,11... | collective-permute-start | bytes 786440 | tf_op jit(solution)/shard_map/ppermute | solution.py:554

commit v3 on v2

--- a/solution.py
+++ b/solution.py
@@ -10,6 +10,7 @@
 F32 = jnp.float32
 BF16 = jnp.bfloat16
 VMEM_BYTES = 24 * 1024 * 1024
+PART = 4
 
 
 def nn(a, b):
@@ -102,64 +103,72 @@
     return scratch[pl.ds(j, chi, stride=scratch.shape[0] // chi), :]
 
 
-def kron_step(lhs, rhs, x_ref, t, first, count, transposed):
+def weave(one, two, target, at):
+    chi = one.shape[0]
+    for g in range(0, chi, 2 * PART):
+        rows = [block[k : k + PART, :] for k in (g, g + PART) for block in (one, two)]
+        target[at + 2 * g : at + 2 * g + 4 * PART, :] = jnp.concatenate(rows, axis=0).astype(BF16)
+
+
+def kron_step(lhs, rhs, x_ref, t, pair, transposed):
     chi = lhs.shape[1]
     bond = lhs.shape[0] // chi
-    some = lhs[first * chi : (first + count) * chi, :]
+    some = lhs[pair * 2 * chi : (pair + 1) * 2 * chi, :]
     if transposed:
         product = nt(some, rhs[t * chi : (t + 2) * chi, :])
     else:
         product = nn(some, rhs[:, t * chi : (t + 2) * chi])
-    for s in range(count):
-        at = ((first + s) * bond + t) * 8
-        for g in range(chi // 8):
-            rows = product[s * chi + g * 8 : s * chi + g * 8 + 8, :]
-            x_ref[at : at + 16, g * chi : (g + 1) * chi] = jnp.concatenate(
-                [rows[:, :chi], rows[:, chi:]], axis=0
-            ).astype(BF16)
+    at = (pair * bond + t) * 2 * PART
+    for g in range(chi // PART):
+        rows = product[g * 2 * PART : (g + 1) * 2 * PART, :]
+        x_ref[at : at + 4 * PART, g * chi : (g + 1) * chi] = jnp.concatenate(
+            [rows[:, :chi], rows[:, chi:]], axis=0
+        ).astype(BF16)
 
 
 def absorb_step(kron, x_ref, m_ref, chi, g, first, count):
     bond = m_ref.shape[0] // chi
-    step = bond * 8
-    out = nn(kron[first * step : (first + count) * step, :], x_ref[:, g * chi : (g + 2) * chi])
+    step = bond * PART
+    out = nn(kron[first * step : (first + count) * step, :], x_ref[:, g * chi : (g + 4) * chi])
     for o in range(count):
-        for d in range(bond):
-            rows = out[(o * bond + d) * 8 : (o * bond + d) * 8 + 8, :]
-            at = (first + o) * chi + g * 8
-            m_ref[at : at + 16, d * chi : (d + 1) * chi] = jnp.concatenate(
-                [rows[:, :chi], rows[:, chi:]], axis=0
-            ).astype(BF16)
-
-
-def kron_steps(lhs, rhs, x_ref, transposed=False, count=1):
+        for d in range(0, bond, 2):
+            rows = out[(o * bond + d) * PART : (o * bond + d + 2) * PART, :]
+            parts = [rows[:, k * chi : (k + 1) * chi] for k in range(4)]
+            at = (first + o) * chi + g * PART
+            for k in range(2):
+                m_ref[at : at + 4 * PART, (d + k) * chi : (d + k + 1) * chi] = jnp.concatenate(
+                    [part[k * PART : (k + 1) * PART, :] for part in parts], axis=0
+                ).astype(BF16)
+
+
+def kron_steps(lhs, rhs, x_ref, transposed=False):
     bond = lhs.shape[0] // lhs.shape[1]
-    count = min(count, bond)
     return [
-        functools.partial(kron_step, lhs, rhs, x_ref, t, first, count, transposed)
+        functools.partial(kron_step, lhs, rhs, x_ref, t, pair, transposed)
         for t in range(0, bond, 2)
+        for pair in range(bond // 2)
+    ]
+
+
+def absorb_steps(kron, x_ref, m_ref, chi, count=4):
+    bond = m_ref.shape[0] // chi
+    return [
+        functools.partial(absorb_step, kron, x_ref, m_ref, chi, g, first, count)
+        for g in range(0, chi // PART, 4)
         for first in range(0, bond, count)
     ]
 
 
-def absorb_steps(kron, x_ref, m_ref, chi, count=2):
-    bond = m_ref.shape[0] // chi
-    count = min(count, bond)
-    return [
-        functools.partial(absorb_step, kron, x_ref, m_ref, chi, g, first, count)
-        for g in range(0, chi // 8, 2)
-        for first in range(0, bond, count)
-    ]
-
-
-def square_core(flat):
-    half = flat.shape[1] // 2
-    size = flat.shape[0] * 2
-    i = iota((size, flat.shape[0]), 0)
-    j = iota((size, flat.shape[0]), 1)
+def square_core(row):
+    values = row[...].astype(F32)
+    size = round(values.shape[1] ** 0.5)
+    flat = [values[:, i : i + 2 * size] for i in range(0, size * size, 2 * size)]
+    flat = jnp.concatenate(flat, axis=0).astype(BF16)
+    i = iota((size, size // 2), 0)
+    j = iota((size, size // 2), 1)
     even = jnp.where(i == 2 * j, 1.0, 0.0).astype(BF16)
     odd = jnp.where(i == 2 * j + 1, 1.0, 0.0).astype(BF16)
-    return (nn(even, flat[:, :half]) + nn(odd, flat[:, half:])).astype(BF16)
+    return (nn(even, flat[:, :size]) + nn(odd, flat[:, size:])).astype(BF16)
 
 
 def swap_order(size, bond):
@@ -170,16 +179,26 @@
 
 
 def spread(size):
-    i = iota((size * 8, size), 0)
-    j = iota((size * 8, size), 1)
-    return jnp.where(i // 8 == j, 1.0, 0.0).astype(BF16)
+    i = iota((size * PART, size), 0)
+    j = iota((size * PART, size), 1)
+    return jnp.where(i // PART == j, 1.0, 0.0).astype(BF16)
+
+
+def woven_pair(i, bond):
+    i = i // PART
+    s = (i // (2 * bond)) * 2 + i % 2
+    t = (i // 4) % (bond // 2) * 2 + (i // 2) % 2
+    return s, t
 
 
 def kron_of(spread_rows, size):
-    wide = nt(spread_rows.astype(BF16), spread(size))
+    bond = round(size**0.5)
+    s, t = woven_pair(iota((size * PART, size), 0), bond)
+    spread_columns = jnp.where(s * bond + t == iota((size * PART, size), 1), 1.0, 0.0).astype(BF16)
+    wide = nt(spread_rows.astype(BF16), spread_columns)
     i = iota(wide.shape, 0)
     j = iota(wide.shape, 1)
-    return jnp.where(i % 8 == j % 8, wide, 0.0).astype(BF16)
+    return jnp.where(i % PART == j % PART, wide, 0.0).astype(BF16)
 
 
 def spread_ahead(core, bond):
@@ -225,8 +244,7 @@
     total = jnp.zeros((1, chosen.shape[1]), F32)
     for p in range(chosen.shape[0]):
         total = total + jnp.where(choice[0, 0] == p, chosen[p : p + 1, :].astype(F32), 0.0)
-    flat = [total[:, i : i + core.shape[1]] for i in range(0, total.shape[1], core.shape[1])]
-    core[...] = jnp.concatenate(flat, axis=0).astype(BF16)
+    core[...] = total.astype(BF16)
     pltpu.make_async_copy(left, first, sems.at[0]).wait()
     pltpu.make_async_copy(right, second, sems.at[1]).wait()
 
@@ -272,25 +290,27 @@
 
         @pl.when(side == 0)
         def _():
-            for u in range(bond):
-                block = leg(wide, u).T.astype(BF16)
-                legs[:, u * chi : (u + 1) * chi] = block
+            for u in range(0, bond, 2):
+                pair = [leg(wide, u).T, leg(wide, u + 1).T]
+                for k in range(2):
+                    legs[:, (u + k) * chi : (u + k + 1) * chi] = pair[k].astype(BF16)
                 if mine == 0:
-                    first[u * chi : (u + 1) * chi, :] = block
+                    weave(*pair, first, u * chi)
 
         @pl.when(side == 1)
         def _():
-            for u in range(bond):
-                block = leg(wide, u).astype(BF16)
-                legs[:, u * chi : (u + 1) * chi] = block
+            for u in range(0, bond, 2):
+                pair = [leg(wide, u), leg(wide, u + 1)]
+                for k in range(2):
+                    legs[:, (u + k) * chi : (u + k + 1) * chi] = pair[k].astype(BF16)
                 if mine == 1:
-                    first[u * chi : (u + 1) * chi, :] = block
+                    weave(*pair, first, u * chi)
 
     copies[2].wait()
     wide_sketch[...] = sketch[...].astype(F32)
 
     def turn_sketch(o):
-        sketch_t[o * chi : (o + 1) * chi, :] = leg(wide_sketch, o).T.astype(BF16)
+        weave(leg(wide_sketch, o).T, leg(wide_sketch, o + 1).T, sketch_t, o * chi)
 
     is_left = side == 0
     size = bond * bond
@@ -310,21 +330,22 @@
     )
 
     def build_kron(target, left, right, part):
-        step = size * 8 // 4
+        step = size * PART // 4
         at = slice(part * step, (part + 1) * step)
         target[at, :] = kron_of(jnp.where(is_left, left[at, :], right[at, :]), size)
 
     inverse_top, inverse_bottom = chol_inverse(
         [nt(legs_top[...], legs_top[...]), nt(legs_bottom[...], legs_bottom[...])],
         1,
-        [functools.partial(turn_sketch, o) for o in range(bond)]
+        [functools.partial(turn_sketch, o) for o in range(0, bond, 2)]
         + [functools.partial(build_kron, *args, part) for args in krons for part in range(4)],
     )
     high, low = split(inverse_top)
-    ortho = (nn(high, legs_top[...]) + nn(low, legs_top[...])).astype(BF16)
-    basis_lanes[...] = ortho
-    for u in range(bond):
-        basis[u * chi : (u + 1) * chi, :] = ortho[:, u * chi : (u + 1) * chi]
+    ortho = nn(high, legs_top[...]) + nn(low, legs_top[...])
+    basis_lanes[...] = ortho.astype(BF16)
+    blocks = [ortho[:, u * chi : (u + 1) * chi] for u in range(bond)]
+    for u in range(0, bond, 2):
+        weave(blocks[u], blocks[u + 1], basis, u * chi)
     high, low = split(inverse_bottom)
     edge[...] = (nn(high, legs_bottom[...]) + nn(low, legs_bottom[...])).astype(BF16)
 
@@ -355,7 +376,8 @@
     kron_0,
     kron_first,
     next_basis,
-    new,
+    closing,
+    absorbed,
     x_first,
     middle,
     lanes_1,
@@ -365,7 +387,6 @@
     lanes_0,
     ahead,
     x,
-    absorbed,
 ):
     is_left = lax.axis_index("row") == 0
     chi = basis.shape[1]
@@ -411,12 +432,10 @@
     )
     (inverse,) = chol_inverse([gram], 3, beside)
     inverse_high, inverse_low = split(inverse)
-    closing = (
-        nn(inverse_high, high) + (nn(inverse_high, low) + nn(inverse_low, high))
-    ).astype(BF16)
-    for d in range(bond):
-        next_basis[blocks[d], :] = closing[:, blocks[d]]
-    new[...] = finish(absorbed, closing, wide_0)
+    ortho = nn(inverse_high, high) + (nn(inverse_high, low) + nn(inverse_low, high))
+    closing[...] = ortho.astype(BF16)
+    for d in range(0, bond, 2):
+        weave(ortho[:, blocks[d]], ortho[:, blocks[d + 1]], next_basis, d * chi)
 
 
 def state_kernel(middle, received, carried, back, wide, behind):
@@ -427,41 +446,44 @@
 
     @pl.when(side == 0)
     def _():
-        for j in range(bond):
-            at = slice(j * chi, (j + 1) * chi)
-            block = leg(wide, j)
-            behind[:, at] = block.T.astype(BF16)
-            back[at, :] = block.astype(BF16)
+        for j in range(0, bond, 2):
+            pair = [leg(wide, j), leg(wide, j + 1)]
+            for k in range(2):
+                behind[:, (j + k) * chi : (j + k + 1) * chi] = pair[k].T.astype(BF16)
+            weave(*pair, back, j * chi)
 
     @pl.when(side == 1)
     def _():
-        for j in range(bond):
-            at = slice(j * chi, (j + 1) * chi)
-            block = leg(wide, j)
-            behind[:, at] = block.astype(BF16)
-            back[at, :] = block.T.astype(BF16)
+        for j in range(0, bond, 2):
+            pair = [leg(wide, j), leg(wide, j + 1)]
+            for k in range(2):
+                behind[:, (j + k) * chi : (j + k + 1) * chi] = pair[k].astype(BF16)
+            weave(pair[0].T, pair[1].T, back, j * chi)
 
     state = nn(behind[...], middle[...]).astype(BF16)
     for s in range(bond):
         carried[s * chi : (s + 1) * chi, :] = state[:, s * chi : (s + 1) * chi]
 
 
-def lower_kernel(basis, edge, lanes, kron, new_0, keep, send, wide, x, absorbed):
+def lower_kernel(
+    basis, edge, lanes, kron, closing_0, absorbed_0, keep, send, wide_0, wide, x, absorbed
+):
     side = lax.axis_index("row")
     chi = basis.shape[1]
+    new_0 = finish(absorbed_0, closing_0[...], wide_0)
     for step in kron_steps(basis, lanes, x) + absorb_steps(kron, x, absorbed, chi):
         step()
-    new = finish(absorbed, edge[...], wide)
+    new_1 = finish(absorbed, edge[...], wide)
 
     @pl.when(side == 0)
     def _():
-        keep[...] = new_0[...]
-        send[...] = new
+        keep[...] = new_0
+        send[...] = new_1
 
     @pl.when(side == 1)
     def _():
-        keep[...] = new
-        send[...] = new_0[...]
+        keep[...] = new_1
+        send[...] = new_0
 
 
 def product_kernel(x_first, back, carried, product, x_second):
@@ -482,7 +504,7 @@
     side = lax.axis_index("row")
     is_left = side == 0
     phys_count = gradient.shape[0]
-    size = product.shape[0] // 8
+    size = product.shape[0] // PART
     bond = round(size**0.5)
     chi = keep.shape[1]
 
@@ -494,14 +516,14 @@
     pl.when(side == 1)(functools.partial(start, received, keep))
 
     def one_hot(i, j, swapped):
-        i = i // 8
-        other = (i % bond) * bond + i // bond
-        return jnp.where(j == jnp.where(swapped, other, i), 1.0, 0.0).astype(BF16)
+        s, t = woven_pair(i, bond)
+        at = jnp.where(swapped, t * bond + s, s * bond + t)
+        return jnp.where(j == at, 1.0, 0.0).astype(BF16)
 
     i = iota(product.shape, 0)
     j = iota(product.shape, 1)
-    diagonal = jnp.where(i % 8 == j % 8, product[...], 0.0).astype(BF16)
-    wide = (size * 8, size * 2)
+    diagonal = jnp.where(i % PART == j % PART, product[...], 0.0).astype(BF16)
+    wide = (size * PART, size * 2)
     half = jnp.zeros((size // 2, size * 2), F32)
     for odd in range(2):
         columns = one_hot(iota(wide, 0), iota(wide, 1) - odd * size, side == 1)
@@ -561,14 +583,14 @@
     size = bond * bond
     tall = (rows, chi)
     flat = (chi, rows)
-    kron = (size * 8, size * 8)
-    stack = (size * 8, chi // 8 * chi)
+    kron = (size * PART, size * PART)
+    stack = (size * PART, chi // PART * chi)
     square = (rows, rows)
     count = lax.axis_size("col")
     sites = site_tensors.reshape(site_tensors.shape[2:])
     first_sent, second_sent, site = call(
         begin_kernel,
-        [(tall, BF16), (tall, BF16), ((size // 2, size * 2), BF16)],
+        [(tall, BF16), (tall, BF16), ((1, size * size), BF16)],
         [(sites.shape, BF16)],
         [left_bounds.reshape(tall), right_bounds.reshape(tall), sites, configuration],
         2**20,
@@ -607,18 +629,17 @@
     )
     sketched, arrived_x, arrived_y = lax.optimization_barrier((sketched, arrived_x, arrived_y))
     swapped = exchanged(arrived_y, "row")
-    next_basis, new, x_first, middle, lanes = call(
+    next_basis, closing, absorbed, x_first, middle, lanes = call(
         upper_kernel,
-        [(tall, BF16), (tall, BF16), (stack, BF16), (square, BF16), (flat, BF16)],
         [
-            (tall, F32),
-            (tall, F32),
             (tall, BF16),
             (flat, BF16),
-            (flat, BF16),
+            (square, BF16),
             (stack, BF16),
             (square, BF16),
+            (flat, BF16),
         ],
+        [(tall, F32), (tall, F32), (tall, BF16), (flat, BF16), (flat, BF16), (stack, BF16)],
         [basis, sketched, first, arrived_x, arrived_y, kron_0, kron_first],
         2**33,
     )
@@ -634,8 +655,8 @@
     keep, send = call(
         lower_kernel,
         [(tall, BF16), (tall, BF16)],
-        [(tall, F32), (stack, BF16), (square, BF16)],
-        [next_basis, edge, lanes, kron_1, new],
+        [(tall, F32), (tall, F32), (stack, BF16), (square, BF16)],
+        [next_basis, edge, lanes, kron_1, closing, absorbed],
         2**32,
     )
     received = exchanged(send, "row")

time: 34.1 us -> 32.4 us (0.950)
  Pallas kernels: 24.8 us -> 22.3 us
  starting transfers between devices: 7.44 us -> 8.09 us
    pallas_call x8, Pallas kernels: 24.8 us -> 22.3 us  [call(): pl.pallas_call(kernel, out_shape=[jax.ShapeDtypeStruct(s, t) for s, t in...]
    ppermute x4, starting transfers between devices: 1.55 us -> 2.2 us  [exchanged(): return lax.ppermute(block, axis, [(0, 1), (1, 0)])]
  transfers between devices with their start and end apart: 6 -> 6, of which waited for: 0 -> 1; matrix products, arithmetic and copies ran while one was open for 0% -> 0% of each run, Pallas kernels for 63% -> 60%
where the time goes in v3:
time: 32.4 us; the launch traced here: 32.1 us
  Pallas kernels  22.3 us (69%)
  starting transfers between devices  8.09 us (25%)
  between operations  1.51 us (5%)
    pallas_call x8, Pallas kernels, call(): pl.pallas_call(kernel, out_shape=[jax.ShapeDtypeStruct(s, t) for s, t in...  22.3 us
    ppermute x2, starting transfers between devices, moved(): return lax.ppermute(block, ('col', 'row'), pairs)  5.89 us
    ppermute x4, starting transfers between devices, exchanged(): return lax.ppermute(block, axis, [(0, 1), (1, 0)])  2.2 us
  transfers between devices with their start and end apart: 6, of which 1 were waited for; matrix products, arithmetic and copies ran while one was open for 0% of the time, Pallas kernels for 60%

profile of v3, /device:TPU:0, one launch (start us, length us, event | category | flops | bytes accessed | tf_op | source)
XLA Modules:
  0.0 32.1 jit_solution(5634688046994541366)
XLA Ops:
  1.3 1.1 %shard_map.94 = (bf16[1024,128]{1,0:T(8,128)(2,1)S(1)}, bf16[1024,128]{1,0:T(8,128)(2,1)S(1)}, bf16[1,4096]{1,0:T(2,128)(2,1)S(1)}) custom-call(bf16[1024,128]{1,0:T(8,128)(2,1)} %bitcast.8, bf16[1024,128]{1,0:T(8,128)(2,1)} %bitcast.9, bf16[2,4096]{1,0:T(2,128)(2,1)} %bitcast.10, s32[1,1]{1,0:T(1,128)S(6)} %copy.10.choice), custom_call_target="tpu_custom_call" | custom-call | flops 1048576 | bytes 2097152 | tf_op jit(solution)/shard_map/pallas_call | solution.py:552
  2.3 0.5 %collective-permute-start = (bf16[1,4096]{1,0:T(2,128)(2,1)S(1)}, bf16[1,4096]{1,0:T(2,128)(2,1)S(1)}, u32[]{:S(2)}, u32[]{:S(2)}) collective-permute-start(bf16[1,4096]{1,0:T(2,128)(2,1)S(1)} %get-tuple-element.35.site), channel_id=1, source_target_pairs={{0,1},{1,0},{2,3},{3,2},{4,5},{5,4},{6,7},{7,6},{8,9},{9,8},{10,11... | collective-permute-start | bytes 24584 | tf_op jit(solution)/shard_map/ppermute | solution.py:576
  2.9 2.6 %collective-permute-start.1 = (bf16[1024,128]{1,0:T(8,128)(2,1)S(1)}, bf16[1024,128]{1,0:T(8,128)(2,1)S(1)}, u32[]{:S(2)}, u32[]{:S(2)}) collective-permute-start(bf16[1024,128]{1,0:T(8,128)(2,1)S(1)} %get-tuple-element.40), channel_id=1, source_target_pairs={{0,2},{2,4},{4,6},{6,8},{8,10},{10,12},{12,14},{14,0},{1,15},{3,1}... | collective-permute-start | bytes 786440 | tf_op jit(solution)/shard_map/ppermute | solution.py:572
  5.4 3.3 %collective-permute-start.2 = (bf16[1024,128]{1,0:T(8,128)(2,1)S(1)}, bf16[1024,128]{1,0:T(8,128)(2,1)S(1)}, u32[]{:S(2)}, u32[]{:S(2)}) collective-permute-start(bf16[1024,128]{1,0:T(8,128)(2,1)S(1)} %get-tuple-element.41), channel_id=1, source_target_pairs={{0,15},{2,1},{4,3},{6,5},{8,7},{10,9},{12,11},{14,13},{1,2},{3,4},... | collective-permute-start | bytes 786440 | tf_op jit(solution)/shard_map/ppermute | solution.py:572
  8.8 0.0 collective-permute-done.site_other
  8.8 6.9 %shard_map.95 = (bf16[1024,128]{1,0:T(8,128)(2,1)S(1)}, bf16[128,1024]{1,0:T(8,128)(2,1)S(1)}, bf16[128,1024]{1,0:T(8,128)(2,1)S(1)}, bf16[1024,128]{1,0:T(8,128...) custom-call(bf16[1024,128]{1,0:T(8,128)(2,1)} %bitcast.11, ...), custom_call_target="tpu_custom_call" | custom-call | flops 2147483648 | bytes 2097152 | tf_op jit(solution)/shard_map/pallas_call | solution.py:552
  15.6 1.3 %shard_map.96.sketched = bf16[1024,1024]{1,0:T(8,128)(2,1)S(1)} custom-call(bf16[128,1024]{1,0:T(8,128)(2,1)S(1)} %get-tuple-element.37.basis_lanes, bf16[1024,128]{1,0:T(8,128)(2,1)S(1)} %get-tuple-element.38.sketch_t, bf16[256,256]{1,0:T(8,128)(2,1)S(1)} %get-tuple-element.39.kron_sketch), custom_call_target="tpu_custom_call" | custom-call | flops 2147483648 | bytes 2097152 | tf_op jit(solution)/shard_map/pallas_call | solution.py:552
  17.0 0.2 collective-permute-done.1.arrived_x
  17.2 0.0 collective-permute-done.2.arrived_y
  17.2 1.0 %collective-permute-start.3 = (bf16[1024,128]{1,0:T(8,128)(2,1)S(1)}, bf16[1024,128]{1,0:T(8,128)(2,1)S(1)}, u32[]{:S(2)}, u32[]{:S(2)}) collective-permute-start(bf16[1024,128]{1,0:T(8,128)(2,1)S(1)} %collective-permute-done.2.arrived_y), channel_id=1, source_target_pairs={{0,1},{1,0},{2,3},{3,2},{4,5},{5,4},{6,7},{7,6},{8,9},{9,8},{10,11... | collective-permute-start | bytes 786440 | tf_op jit(solution)/shard_map/ppermute | solution.py:576
  18.2 6.9 %shard_map.97 = (bf16[1024,128]{1,0:T(8,128)(2,1)S(1)}, bf16[128,1024]{1,0:T(8,128)(2,1)S(1)}, bf16[1024,1024]{1,0:T(8,128)(2,1)S(1)}, bf16[256,4096]{1,0:T(8,12...) custom-call(bf16[1024,128]{1,0:T(8,128)(2,1)S(1)} %get-tuple-element.36.basis, ...), custom_call_target="tpu_custom_call" | custom-call | flops 8589934592 | bytes 2097152 | tf_op jit(solution)/shard_map/pallas_call | solution.py:552
  25.2 0.0 collective-permute-done.3.received
  25.2 0.6 %shard_map.98 = (bf16[1024,128]{1,0:T(8,128)(2,1)S(1)}, bf16[1024,128]{1,0:T(8,128)(2,1)S(1)}) custom-call(bf16[1024,1024]{1,0:T(8,128)(2,1)S(1)} %get-tuple-element.49.middle, bf16[1024,128]{1,0:T(8,128)(2,1)S(1)} %collective-permute-done.3.received), custom_call_target="tpu_custom_call" | custom-call | flops 1073741824 | bytes 2097152 | tf_op jit(solution)/shard_map/pallas_call | solution.py:552
  25.9 0.1 collective-permute-start.5
  25.9 2.7 %shard_map.99 = (bf16[1024,128]{1,0:T(8,128)(2,1)S(1)}, bf16[1024,128]{1,0:T(8,128)(2,1)S(1)}) custom-call(bf16[1024,128]{1,0:T(8,128)(2,1)S(1)} %get-tuple-element.51.basis, bf16[128,1024]{1,0:T(8,128)(2,1)S(1)} %get-tuple-element.52.edge, bf16[128,1024]{1,0:T(8,128)(2,1)S(1)} %get-tuple-element.53.lanes, bf16[256,256]{1,0:T(8,128)(2,1)S(1)} %get-tuple-element.54.kron, ...), custom_call_target="tpu_custom_call" | custom-call | flops 4294967296 | bytes 2097152 | tf_op jit(solution)/shard_map/pallas_call | solution.py:552
  28.6 0.6 %collective-permute-start.4 = (bf16[1024,128]{1,0:T(8,128)(2,1)S(1)}, bf16[1024,128]{1,0:T(8,128)(2,1)S(1)}, u32[]{:S(2)}, u32[]{:S(2)}) collective-permute-start(bf16[1024,128]{1,0:T(8,128)(2,1)S(1)} %get-tuple-element.57), channel_id=1, source_target_pairs={{0,1},{1,0},{2,3},{3,2},{4,5},{5,4},{6,7},{7,6},{8,9},{9,8},{10,11... | collective-permute-start | bytes 786440 | tf_op jit(solution)/shard_map/ppermute | solution.py:576
  29.2 0.0 collective-permute-done.5.carried
  29.2 1.4 %shard_map.100.product = f32[256,256]{1,0:T(8,128)S(1)} custom-call(bf16[256,4096]{1,0:T(8,128)(2,1)S(1)} %get-tuple-element.58.x_first, bf16[1024,128]{1,0:T(8,128)(2,1)S(1)} %get-tuple-element.59.back, bf16[1024,128]{1,0:T(8,128)(2,1)S(1)} %collective-permute-done.5.carried), custom_call_target="tpu_custom_call" | custom-call | flops 2147483648 | bytes 2097152 | tf_op jit(solution)/shard_map/pallas_call | solution.py:552
  30.6 0.0 collective-permute-done.4.received
  30.6 1.3 %shard_map.101 = (f32[2,4096]{1,0:T(2,128)}, bf16[1024,128]{1,0:T(8,128)(2,1)}, bf16[1024,128]{1,0:T(8,128)(2,1)}) custom-call(f32[256,256]{1,0:T(8,128)S(1)} %shard_map.100.product, s32[1,1]{1,0:T(1,128)S(6)} %copy.10.choice, bf16[1024,128]{1,0:T(8,128)(2,1)S(1)} %get-tuple-element.62.keep, bf16[1024,128]{1,0:T(8,128)(2,1)S(1)} %collective-permute-done.4.received), custom_call_target="tpu_custom_call" | custom-call | flops 1073741824 | bytes 2097152 | tf_op jit(solution)/shard_map/pallas_call | solution.py:552
Async XLA Ops:
  2.3 6.4 %collective-permute-start = (bf16[1,4096]{1,0:T(2,128)(2,1)S(1)}, bf16[1,4096]{1,0:T(2,128)(2,1)S(1)}, u32[]{:S(2)}, u32[]{:S(2)}) collective-permute-start(bf16[1,4096]{1,0:T(2,128)(2,1)S(1)} %get-tuple-element.35.site), channel_id=1, source_target_pairs={{0,1},{1,0},{2,3},{3,2},{4,5},{5,4},{6,7},{7,6},{8,9},{9,8},{10,11... | collective-permute-start | bytes 24584 | tf_op jit(solution)/shard_map/ppermute | solution.py:576
  2.9 14.3 %collective-permute-start.1 = (bf16[1024,128]{1,0:T(8,128)(2,1)S(1)}, bf16[1024,128]{1,0:T(8,128)(2,1)S(1)}, u32[]{:S(2)}, u32[]{:S(2)}) collective-permute-start(bf16[1024,128]{1,0:T(8,128)(2,1)S(1)} %get-tuple-element.40), channel_id=1, source_target_pairs={{0,2},{2,4},{4,6},{6,8},{8,10},{10,12},{12,14},{14,0},{1,15},{3,1}... | collective-permute-start | bytes 786440 | tf_op jit(solution)/shard_map/ppermute | solution.py:572
  5.4 11.8 %collective-permute-start.2 = (bf16[1024,128]{1,0:T(8,128)(2,1)S(1)}, bf16[1024,128]{1,0:T(8,128)(2,1)S(1)}, u32[]{:S(2)}, u32[]{:S(2)}) collective-permute-start(bf16[1024,128]{1,0:T(8,128)(2,1)S(1)} %get-tuple-element.41), channel_id=1, source_target_pairs={{0,15},{2,1},{4,3},{6,5},{8,7},{10,9},{12,11},{14,13},{1,2},{3,4},... | collective-permute-start | bytes 786440 | tf_op jit(solution)/shard_map/ppermute | solution.py:572
  17.2 8.0 %collective-permute-start.3 = (bf16[1024,128]{1,0:T(8,128)(2,1)S(1)}, bf16[1024,128]{1,0:T(8,128)(2,1)S(1)}, u32[]{:S(2)}, u32[]{:S(2)}) collective-permute-start(bf16[1024,128]{1,0:T(8,128)(2,1)S(1)} %collective-permute-done.2.arrived_y), channel_id=1, source_target_pairs={{0,1},{1,0},{2,3},{3,2},{4,5},{5,4},{6,7},{7,6},{8,9},{9,8},{10,11... | collective-permute-start | bytes 786440 | tf_op jit(solution)/shard_map/ppermute | solution.py:576
  25.9 3.3 %collective-permute-start.5 = (bf16[1024,128]{1,0:T(8,128)(2,1)S(1)}, bf16[1024,128]{1,0:T(8,128)(2,1)S(1)}, u32[]{:S(2)}, u32[]{:S(2)}) collective-permute-start(bf16[1024,128]{1,0:T(8,128)(2,1)S(1)} %get-tuple-element.60), channel_id=1, source_target_pairs={{0,1},{1,0},{2,3},{3,2},{4,5},{5,4},{6,7},{7,6},{8,9},{9,8},{10,11... | collective-permute-start | bytes 786440 | tf_op jit(solution)/shard_map/ppermute | solution.py:576
  28.6 2.0 %collective-permute-start.4 = (bf16[1024,128]{1,0:T(8,128)(2,1)S(1)}, bf16[1024,128]{1,0:T(8,128)(2,1)S(1)}, u32[]{:S(2)}, u32[]{:S(2)}) collective-permute-start(bf16[1024,128]{1,0:T(8,128)(2,1)S(1)} %get-tuple-element.57), channel_id=1, source_target_pairs={{0,1},{1,0},{2,3},{3,2},{4,5},{5,4},{6,7},{7,6},{8,9},{9,8},{10,11... | collective-permute-start | bytes 786440 | tf_op jit(solution)/shard_map/ppermute | solution.py:576

commit v4 on v3

--- a/solution.py
+++ b/solution.py
@@ -160,9 +160,9 @@
 
 
 def square_core(row):
-    values = row[...].astype(F32)
-    size = round(values.shape[1] ** 0.5)
-    flat = [values[:, i : i + 2 * size] for i in range(0, size * size, 2 * size)]
+    row = row[...].astype(F32)
+    size = round(row.shape[1] ** 0.5)
+    flat = [row[:, i : i + 2 * size] for i in range(0, size * size, 2 * size)]
     flat = jnp.concatenate(flat, axis=0).astype(BF16)
     i = iota((size, size // 2), 0)
     j = iota((size, size // 2), 1)
@@ -229,44 +229,26 @@
     return total.astype(BF16)
 
 
-def begin_kernel(left, right, sites, choice, first, second, core, chosen, sems):
-    side = lax.axis_index("row")
-
-    def start(one, other):
-        pltpu.make_async_copy(one, first, sems.at[0]).start()
-        pltpu.make_async_copy(other, second, sems.at[1]).start()
-
-    pl.when(side == 0)(functools.partial(start, left, right))
-    pl.when(side == 1)(functools.partial(start, right, left))
-    copy = pltpu.make_async_copy(sites, chosen, sems.at[2])
-    copy.start()
-    copy.wait()
-    total = jnp.zeros((1, chosen.shape[1]), F32)
-    for p in range(chosen.shape[0]):
-        total = total + jnp.where(choice[0, 0] == p, chosen[p : p + 1, :].astype(F32), 0.0)
-    core[...] = total.astype(BF16)
-    pltpu.make_async_copy(left, first, sems.at[0]).wait()
-    pltpu.make_async_copy(right, second, sems.at[1]).wait()
-
-
 def edges_kernel(
     top_hbm,
     bottom_hbm,
     sketch_hbm,
-    site,
-    site_other,
+    sites_hbm,
+    choice,
     basis,
     basis_lanes,
     edge,
     first,
     sketch_t,
-    kron_0,
-    kron_1,
+    site,
     kron_first,
-    kron_sketch,
+    own_upper,
+    own_lower,
+    own_sketch,
     top,
     bottom,
     sketch,
+    sites,
     wide,
     wide_sketch,
     legs_top,
@@ -279,7 +261,7 @@
     copies = [
         pltpu.make_async_copy(source, target, sems.at[i])
         for i, (source, target) in enumerate(
-            ((top_hbm, top), (bottom_hbm, bottom), (sketch_hbm, sketch))
+            ((top_hbm, top), (bottom_hbm, bottom), (sketch_hbm, sketch), (sites_hbm, sites))
         )
     ]
     for copy in copies:
@@ -312,33 +294,28 @@
     def turn_sketch(o):
         weave(leg(wide_sketch, o).T, leg(wide_sketch, o + 1).T, sketch_t, o * chi)
 
-    is_left = side == 0
-    size = bond * bond
-    swap = swap_order(size, bond)
-    rows_of = spread(size)
-    core = square_core(site[...])
-    core_other = square_core(site_other[...])
-    mirrored_own = mirrored(core, bond)
-    mirrored_other = mirrored(core_other, bond)
-    ahead = spread_ahead(core, bond)
-    turned = nn(nn(swap, mirrored_own).astype(BF16), swap).astype(BF16)
-    krons = (
-        (kron_sketch, nn(rows_of, turned), spread_turned(core_other, bond)),
-        (kron_0, ahead, nn(rows_of, mirrored_other)),
-        (kron_first, ahead, spread_back(core, bond)),
-        (kron_1, spread_ahead(core_other, bond), nn(rows_of, mirrored_own)),
-    )
-
-    def build_kron(target, left, right, part):
-        step = size * PART // 4
-        at = slice(part * step, (part + 1) * step)
-        target[at, :] = kron_of(jnp.where(is_left, left[at, :], right[at, :]), size)
+    copies[3].wait()
+    row = jnp.zeros((1, sites.shape[1]), F32)
+    for p in range(sites.shape[0]):
+        row = row + jnp.where(choice[0, 0] == p, sites[p : p + 1, :].astype(F32), 0.0)
+    site[...] = row.astype(BF16)
+
+    def build_kron():
+        size = bond * bond
+        core = square_core(site)
+        swap = swap_order(size, bond)
+        wide = spread(size)
+        ahead = spread_ahead(core, bond)
+        own_upper[...] = ahead.astype(BF16)
+        own_lower[...] = nn(wide, nn(swap, core).astype(BF16)).astype(BF16)
+        turned = nn(nn(swap, mirrored(core, bond)).astype(BF16), swap).astype(BF16)
+        own_sketch[...] = nn(wide, turned).astype(BF16)
+        kron_first[...] = kron_of(jnp.where(side == 0, ahead, spread_back(core, bond)), size)
 
     inverse_top, inverse_bottom = chol_inverse(
         [nt(legs_top[...], legs_top[...]), nt(legs_bottom[...], legs_bottom[...])],
         1,
-        [functools.partial(turn_sketch, o) for o in range(0, bond, 2)]
-        + [functools.partial(build_kron, *args, part) for args in krons for part in range(4)],
+        [functools.partial(turn_sketch, o) for o in range(0, bond, 2)] + [build_kron],
     )
     high, low = split(inverse_top)
     ortho = nn(high, legs_top[...]) + nn(low, legs_top[...])
@@ -347,58 +324,120 @@
     for u in range(0, bond, 2):
         weave(blocks[u], blocks[u + 1], basis, u * chi)
     high, low = split(inverse_bottom)
-    edge[...] = (nn(high, legs_bottom[...]) + nn(low, legs_bottom[...])).astype(BF16)
-
-
-def finish(absorbed, closing, wide):
-    chi = closing.shape[0]
-    bond = absorbed.shape[0] // chi
-    unscaled = nt(absorbed[...], closing)
-    for o in range(bond):
-        wide[pl.ds(o, chi, stride=bond), :] = unscaled[o * chi : (o + 1) * chi, :]
-    squares = jnp.sum(unscaled * unscaled, axis=0, keepdims=True)
+    ortho = (nn(high, legs_bottom[...]) + nn(low, legs_bottom[...])).astype(BF16)
+    for d in range(bond):
+        edge[d * chi : (d + 1) * chi, :] = ortho[:, d * chi : (d + 1) * chi]
+
+
+def scaled(blocks, wide):
+    chi = blocks[0].shape[0]
+    bond = len(blocks)
+    squares = jnp.zeros((1, chi), F32)
+    for o, block in enumerate(blocks):
+        wide[pl.ds(o, chi, stride=bond), :] = block
+        squares = squares + jnp.sum(block * block, axis=0, keepdims=True)
     mean = jnp.sum(squares, axis=1, keepdims=True) * (1.0 / (chi * bond * chi))
     return (wide[...] * lax.rsqrt(mean + 1e-06)).astype(BF16)
 
 
-def prepare_kernel(basis_lanes, sketch_t, kron_sketch, sketched, x):
-    chi = basis_lanes.shape[0]
-    for step in kron_steps(sketch_t, basis_lanes, x) + absorb_steps(kron_sketch, x, sketched, chi):
+def join_kernel(basis_lanes, sketch_t, x):
+    for step in kron_steps(sketch_t, basis_lanes, x):
         step()
+
+
+def prepare_kernel(
+    x, site_other, own_upper, own_lower, own_sketch, kron_0, kron_1, sketched, kron_sketch
+):
+    is_left = lax.axis_index("row") == 0
+    size = x.shape[0] // PART
+    bond = round(size**0.5)
+    chi = sketched.shape[0] // bond
+    wide = spread(size)
+    other = square_core(site_other)
+    turned = spread_turned(other, bond)
+    kron_sketch[...] = kron_of(jnp.where(is_left, own_sketch[...], turned.astype(BF16)), size)
+    steps = absorb_steps(kron_sketch, x, sketched, chi)
+    for step in steps[:6]:
+        step()
+    across = mirrored(other, bond)
+    for step in steps[6:11]:
+        step()
+    upper = nn(wide, across).astype(BF16)
+    kron_0[...] = kron_of(jnp.where(is_left, own_upper[...], upper), size)
+    for step in steps[11:]:
+        step()
+    lower = nt(wide, across).astype(BF16)
+    kron_1[...] = kron_of(jnp.where(is_left, lower, own_lower[...]), size)
+
+
+def begin_kernel(
+    first, western, eastern, kron, x_first, back, carried, wide_w, wide_e, ahead, behind, middle
+):
+    side = lax.axis_index("row")
+    chi = first.shape[1]
+    bond = first.shape[0] // chi
+    wide_w[...] = western[...].astype(F32)
+    wide_e[...] = eastern[...].astype(F32)
+
+    def ready(ahead_of, behind_of, back_of):
+        for j in range(0, bond, 2):
+            for k in range(2):
+                at = slice((j + k) * chi, (j + k + 1) * chi)
+                ahead[:, at] = ahead_of(j + k).astype(BF16)
+                behind[:, at] = behind_of(j + k).astype(BF16)
+            weave(back_of(j), back_of(j + 1), back, j * chi)
+
+    west = functools.partial(leg, wide_w)
+    east = functools.partial(leg, wide_e)
+
+    @pl.when(side == 0)
+    def _():
+        ready(west, lambda j: east(j).T, east)
+
+    @pl.when(side == 1)
+    def _():
+        ready(lambda j: east(j).T, west, lambda j: west(j).T)
+
+    for step in kron_steps(first, ahead, x_first) + absorb_steps(kron, x_first, middle, chi):
+        step()
+    state = nn(behind[...], middle[...]).astype(BF16)
+    for s in range(bond):
+        carried[s * chi : (s + 1) * chi, :] = state[:, s * chi : (s + 1) * chi]
 
 
 def upper_kernel(
     basis,
+    edge,
     sketched,
-    first,
-    arrived_x,
-    arrived_y,
+    western,
+    eastern,
+    western_other,
+    eastern_other,
     kron_0,
-    kron_first,
-    next_basis,
+    kron_1,
     closing,
     absorbed,
-    x_first,
-    middle,
-    lanes_1,
+    closed,
     wide_0,
     wide_1,
     rows_0,
     lanes_0,
-    ahead,
+    woven_1,
     x,
+    x_next,
 ):
     is_left = lax.axis_index("row") == 0
     chi = basis.shape[1]
     bond = basis.shape[0] // chi
     blocks = [slice(j * chi, (j + 1) * chi) for j in range(bond)]
+
     @pl.when(is_left)
     def _():
-        wide_0[...] = arrived_x[...].astype(F32)
+        wide_0[...] = western[...].astype(F32)
 
     @pl.when(jnp.logical_not(is_left))
     def _():
-        wide_0[...] = arrived_y[...].astype(F32)
+        wide_0[...] = eastern_other[...].astype(F32)
 
     for j in range(bond):
         rows_0[blocks[j], :] = leg(wide_0, j).astype(BF16)
@@ -414,66 +453,35 @@
     def ready_other(part):
         step = wide_1.shape[0] // 4
         at = slice(part * step, (part + 1) * step)
-        wide_1[at, :] = jnp.where(is_left, arrived_y[at, :], arrived_x[at, :]).astype(F32)
-
-    def ready_ahead(j):
-        block = leg(wide_1, j)
-        lanes_1[:, blocks[j]] = block.astype(BF16)
-        ahead[:, blocks[j]] = jnp.where(is_left, leg(wide_0, j), block.T).astype(BF16)
+        wide_1[at, :] = jnp.where(is_left, western_other[at, :], eastern[at, :]).astype(F32)
+
+    def ready_woven(j):
+        weave(leg(wide_1, j), leg(wide_1, j + 1), woven_1, j * chi)
 
     beside = (
         [ready_lanes]
         + kron_steps(basis, lanes_0, x)
         + [functools.partial(ready_other, part) for part in range(4)]
         + absorb_steps(kron_0, x, absorbed, chi)
-        + [functools.partial(ready_ahead, j) for j in range(bond)]
-        + kron_steps(first, ahead, x_first)
-        + absorb_steps(kron_first, x_first, middle, chi)
+        + [functools.partial(ready_woven, j) for j in range(0, bond, 2)]
+        + kron_steps(woven_1, edge, x_next, True)
+        + absorb_steps(kron_1, x_next, closed, chi)
     )
     (inverse,) = chol_inverse([gram], 3, beside)
     inverse_high, inverse_low = split(inverse)
     ortho = nn(inverse_high, high) + (nn(inverse_high, low) + nn(inverse_low, high))
     closing[...] = ortho.astype(BF16)
-    for d in range(0, bond, 2):
-        weave(ortho[:, blocks[d]], ortho[:, blocks[d + 1]], next_basis, d * chi)
-
-
-def state_kernel(middle, received, carried, back, wide, behind):
+
+
+def lower_kernel(closing, absorbed, closed, keep, send, wide_0, wide_1):
     side = lax.axis_index("row")
-    chi = received.shape[1]
-    bond = received.shape[0] // chi
-    wide[...] = received[...].astype(F32)
-
-    @pl.when(side == 0)
-    def _():
-        for j in range(0, bond, 2):
-            pair = [leg(wide, j), leg(wide, j + 1)]
-            for k in range(2):
-                behind[:, (j + k) * chi : (j + k + 1) * chi] = pair[k].T.astype(BF16)
-            weave(*pair, back, j * chi)
-
-    @pl.when(side == 1)
-    def _():
-        for j in range(0, bond, 2):
-            pair = [leg(wide, j), leg(wide, j + 1)]
-            for k in range(2):
-                behind[:, (j + k) * chi : (j + k + 1) * chi] = pair[k].astype(BF16)
-            weave(pair[0].T, pair[1].T, back, j * chi)
-
-    state = nn(behind[...], middle[...]).astype(BF16)
-    for s in range(bond):
-        carried[s * chi : (s + 1) * chi, :] = state[:, s * chi : (s + 1) * chi]
-
-
-def lower_kernel(
-    basis, edge, lanes, kron, closing_0, absorbed_0, keep, send, wide_0, wide, x, absorbed
-):
-    side = lax.axis_index("row")
-    chi = basis.shape[1]
-    new_0 = finish(absorbed_0, closing_0[...], wide_0)
-    for step in kron_steps(basis, lanes, x) + absorb_steps(kron, x, absorbed, chi):
-        step()
-    new_1 = finish(absorbed, edge[...], wide)
+    chi = closing.shape[0]
+    bond = closing.shape[1] // chi
+    blocks = [slice(j * chi, (j + 1) * chi) for j in range(bond)]
+    upper = nt(absorbed[...], closing[...])
+    new_0 = scaled([upper[at, :] for at in blocks], wide_0)
+    lower = nn(closing[...], closed[...])
+    new_1 = scaled([lower[:, at] for at in blocks], wide_1)
 
     @pl.when(side == 0)
     def _():
@@ -554,7 +562,7 @@
         out_shape=[jax.ShapeDtypeStruct(s, t) for s, t in out_shapes],
         in_specs=[
             smem
-            if x.dtype == jnp.int32
+            if x.shape == (1, 1)
             else pl.BlockSpec(memory_space=pltpu.HBM)
             if i in in_place
             else vmem
@@ -568,8 +576,9 @@
     )(*inputs)
 
 
-def moved(block, pairs):
-    return lax.ppermute(block, ("col", "row"), pairs)
+def shifted(block, axis, steps):
+    count = lax.axis_size(axis)
+    return lax.ppermute(block, axis, [(i, (i + steps) % count) for i in range(count)])
 
 
 def exchanged(block, axis):
@@ -586,78 +595,83 @@
     kron = (size * PART, size * PART)
     stack = (size * PART, chi // PART * chi)
     square = (rows, rows)
-    count = lax.axis_size("col")
     sites = site_tensors.reshape(site_tensors.shape[2:])
-    first_sent, second_sent, site = call(
-        begin_kernel,
-        [(tall, BF16), (tall, BF16), ((1, size * size), BF16)],
-        [(sites.shape, BF16)],
-        [left_bounds.reshape(tall), right_bounds.reshape(tall), sites, configuration],
-        2**20,
-        in_place=(0, 1, 2),
-        copies=3,
-    )
-    ahead, behind = (
-        [2 * ((c + step) % count) for c in range(count)] for step in (1, -1)
-    )
-    arrived_x = moved(
-        first_sent,
-        [(2 * c, ahead[c]) for c in range(count)]
-        + [(2 * c + 1, behind[c] + 1) for c in range(count)],
-    )
-    arrived_y = moved(
-        second_sent,
-        [(2 * c, behind[c] + 1) for c in range(count)]
-        + [(2 * c + 1, ahead[c]) for c in range(count)],
-    )
-    site_other = exchanged(site, "row")
-    basis, basis_lanes, edge, first, sketch_t, kron_0, kron_1, kron_first, kron_sketch = call(
+    western = shifted(left_bounds.reshape(tall), "col", 1)
+    eastern = shifted(right_bounds.reshape(tall), "col", -1)
+    basis, basis_lanes, edge, first, sketch_t, site, kron_first, *own = call(
         edges_kernel,
-        [(tall, BF16), (flat, BF16), (flat, BF16), (tall, BF16), (tall, BF16)] + [(kron, BF16)] * 4,
-        [(tall, BF16)] * 3 + [(tall, F32), (tall, F32), (flat, BF16), (flat, BF16)],
-        [top_env.reshape(tall), bottom_env.reshape(tall), sketch, site, site_other],
-        2**31,
-        in_place=(0, 1, 2),
-        copies=3,
-    )
-    (sketched,) = call(
-        prepare_kernel,
-        [(square, BF16)],
-        [(stack, BF16)],
-        [basis_lanes, sketch_t, kron_sketch],
-        2**31,
-    )
-    sketched, arrived_x, arrived_y = lax.optimization_barrier((sketched, arrived_x, arrived_y))
-    swapped = exchanged(arrived_y, "row")
-    next_basis, closing, absorbed, x_first, middle, lanes = call(
-        upper_kernel,
         [
             (tall, BF16),
             (flat, BF16),
-            (square, BF16),
+            (tall, BF16),
+            (tall, BF16),
+            (tall, BF16),
+            ((1, size * size), BF16),
+            (kron, BF16),
+        ]
+        + [((size * PART, size), BF16)] * 3,
+        [(tall, BF16)] * 3
+        + [(sites.shape, BF16), (tall, F32), (tall, F32), (flat, BF16), (flat, BF16)],
+        [top_env.reshape(tall), bottom_env.reshape(tall), sketch, sites, configuration],
+        2**31,
+        in_place=(0, 1, 2, 3),
+        copies=4,
+    )
+    site_other = exchanged(site, "row")
+    (joined,) = call(join_kernel, [(stack, BF16)], [], [basis_lanes, sketch_t], 2**30)
+    site_other, joined = lax.optimization_barrier((site_other, joined))
+    kron_0, kron_1, sketched = call(
+        prepare_kernel,
+        [(kron, BF16), (kron, BF16), (square, BF16)],
+        [(kron, BF16)],
+        [joined, site_other, *own],
+        2**31,
+    )
+    sketched, western, eastern = lax.optimization_barrier((sketched, western, eastern))
+    western_other = exchanged(western, "row")
+    eastern_other = exchanged(eastern, "row")
+    x_first, back, carried = call(
+        begin_kernel,
+        [(stack, BF16), (tall, BF16), (tall, BF16)],
+        [(tall, F32), (tall, F32), (flat, BF16), (flat, BF16), (square, BF16)],
+        [first, western, eastern, kron_first],
+        2**32,
+    )
+    sketched, carried, western_other, eastern_other = lax.optimization_barrier(
+        (sketched, carried, western_other, eastern_other)
+    )
+    carried = exchanged(carried, "row")
+    closing, absorbed, closed = call(
+        upper_kernel,
+        [(flat, BF16), (square, BF16), (square, BF16)],
+        [
+            (tall, F32),
+            (tall, F32),
+            (tall, BF16),
+            (flat, BF16),
+            (tall, BF16),
             (stack, BF16),
-            (square, BF16),
-            (flat, BF16),
+            (stack, BF16),
         ],
-        [(tall, F32), (tall, F32), (tall, BF16), (flat, BF16), (flat, BF16), (stack, BF16)],
-        [basis, sketched, first, arrived_x, arrived_y, kron_0, kron_first],
+        [
+            basis,
+            edge,
+            sketched,
+            western,
+            eastern,
+            western_other,
+            eastern_other,
+            kron_0,
+            kron_1,
+        ],
         2**33,
     )
-    carried, back = call(
-        state_kernel,
-        [(tall, BF16), (tall, BF16)],
-        [(tall, F32), (flat, BF16)],
-        [middle, swapped],
-        2**30,
-    )
-    next_basis, carried = lax.optimization_barrier((next_basis, carried))
-    carried = exchanged(carried, "row")
     keep, send = call(
         lower_kernel,
         [(tall, BF16), (tall, BF16)],
-        [(tall, F32), (tall, F32), (stack, BF16), (square, BF16)],
-        [next_basis, edge, lanes, kron_1, closing, absorbed],
-        2**32,
+        [(tall, F32), (tall, F32)],
+        [closing, absorbed, closed],
+        2**31,
     )
     received = exchanged(send, "row")
     (product,) = call(

time: 32.4 us -> 31.8 us (0.981)
  starting transfers between devices: 8.09 us -> 7.38 us
    ppermute x4 -> x5, starting transfers between devices: 2.2 us -> 1.28 us  [exchanged(): return lax.ppermute(block, axis, [(0, 1), (1, 0)])]
    ppermute x4 -> x5, waiting for transfers between devices: 0.01 us -> 0.48 us  [exchanged(): return lax.ppermute(block, axis, [(0, 1), (1, 0)])]
  transfers between devices with their start and end apart: 6 -> 7, of which waited for: 1 -> 1; matrix products, arithmetic and copies ran while one was open for 0% -> 0% of each run, Pallas kernels for 60% -> 66%
where the time goes in v4:
time: 31.8 us; the launch traced here: 31.6 us
  Pallas kernels  22.2 us (70%)
  starting transfers between devices  7.38 us (23%)
  between operations  1.55 us (5%)
  waiting for transfers between devices  0.49 us (2%)
    pallas_call x8, Pallas kernels, call(): pl.pallas_call(kernel, out_shape=[jax.ShapeDtypeStruct(s, t) for s, t in...  22.2 us
    ppermute x2, starting transfers between devices, shifted(): lax.ppermute(block, axis, [(i, (i + steps) % count) for i in range(count)])  6.09 us
    ppermute x5, starting transfers between devices, exchanged(): return lax.ppermute(block, axis, [(0, 1), (1, 0)])  1.28 us
  transfers between devices with their start and end apart: 7, of which 1 were waited for; matrix products, arithmetic and copies ran while one was open for 0% of the time, Pallas kernels for 66%

profile of v4, /device:TPU:0, one launch (start us, length us, event | category | flops | bytes accessed | tf_op | source)
XLA Modules:
  0.0 31.6 jit_solution(12126087551049491489)
XLA Ops:
  0.6 3.0 %collective-permute-start.1 = (bf16[1024,128]{1,0:T(8,128)(2,1)}, bf16[1024,128]{1,0:T(8,128)(2,1)S(1)}, u32[]{:S(2)}, u32[]{:S(2)}) collective-permute-start(bf16[1024,128]{1,0:T(8,128)(2,1)} %bitcast.10), channel_id=1, source_target_pairs={{0,2},{2,4},{4,6},{6,8},{8,10},{10,12},{12,14},{14,0},{1,3},{3,5},... | collective-permute-start | bytes 786440 | tf_op jit(solution)/shard_map/ppermute | solution.py:581
  3.6 3.1 %collective-permute-start.2 = (bf16[1024,128]{1,0:T(8,128)(2,1)}, bf16[1024,128]{1,0:T(8,128)(2,1)S(1)}, u32[]{:S(2)}, u32[]{:S(2)}) collective-permute-start(bf16[1024,128]{1,0:T(8,128)(2,1)} %bitcast.11), channel_id=1, source_target_pairs={{0,14},{2,0},{4,2},{6,4},{8,6},{10,8},{12,10},{14,12},{1,15},{3,1}... | collective-permute-start | bytes 786440 | tf_op jit(solution)/shard_map/ppermute | solution.py:581
  7.4 6.8 %shard_map.94 = (bf16[1024,128]{1,0:T(8,128)(2,1)S(1)}, bf16[128,1024]{1,0:T(8,128)(2,1)S(1)}, bf16[1024,128]{1,0:T(8,128)(2,1)S(1)}, bf16[1024,128]{1,0:T(8,128...) custom-call(bf16[1024,128]{1,0:T(8,128)(2,1)} %bitcast.8, ...), custom_call_target="tpu_custom_call" | custom-call | flops 2147483648 | bytes 2097152 | tf_op jit(solution)/shard_map/pallas_call | solution.py:560
  14.2 0.1 collective-permute-start
  14.2 0.7 %shard_map.95.x = bf16[256,4096]{1,0:T(8,128)(2,1)S(1)} custom-call(bf16[128,1024]{1,0:T(8,128)(2,1)S(1)} %get-tuple-element.41.basis_lanes, bf16[1024,128]{1,0:T(8,128)(2,1)S(1)} %get-tuple-element.42.sketch_t), custom_call_target="tpu_custom_call" | custom-call | flops 1073741824 | bytes 2097152 | tf_op jit(solution)/shard_map/pallas_call | solution.py:560
  14.9 0.5 %collective-permute-done.site_other = bf16[1,4096]{1,0:T(2,128)(2,1)S(1)} collective-permute-done((bf16[1,4096]{1,0:T(2,128)(2,1)S(1)}, bf16[1,4096]{1,0:T(2,128)(2,1)S(1)}, u32[]{:S(2)}, u32[]{:S(2)}) %collective-permute-start) | collective-permute-done | bytes 8224 | tf_op jit(solution)/shard_map/ppermute | solution.py:585
  15.4 1.8 %shard_map.96 = (bf16[256,256]{1,0:T(8,128)(2,1)S(1)}, bf16[256,256]{1,0:T(8,128)(2,1)S(1)}, bf16[1024,1024]{1,0:T(8,128)(2,1)S(1)}) custom-call(bf16[256,4096]{1,0:T(8,128)(2,1)S(1)} %shard_map.95.x, bf16[1,4096]{1,0:T(2,128)(2,1)S(1)} %collective-permute-done.site_other, bf16[256,64]{1,0:T(8,128)(2,1)S(1)} %get-tuple-element.45.own_upper, ...), custom_call_target="tpu_custom_call" | custom-call | flops 2147483648 | bytes 2097152 | tf_op jit(solution)/shard_map/pallas_call | solution.py:560
  17.3 0.0 collective-permute-done.1.western
  17.3 0.0 collective-permute-done.2.eastern
  17.3 0.2 collective-permute-start.3
  17.5 0.3 %collective-permute-start.4 = (bf16[1024,128]{1,0:T(8,128)(2,1)S(1)}, bf16[1024,128]{1,0:T(8,128)(2,1)S(1)}, u32[]{:S(2)}, u32[]{:S(2)}) collective-permute-start(bf16[1024,128]{1,0:T(8,128)(2,1)S(1)} %collective-permute-done.2.eastern), channel_id=1, source_target_pairs={{0,1},{1,0},{2,3},{3,2},{4,5},{5,4},{6,7},{7,6},{8,9},{9,8},{10,11... | collective-permute-start | bytes 786440 | tf_op jit(solution)/shard_map/ppermute | solution.py:585
  17.9 2.1 %shard_map.97 = (bf16[256,4096]{1,0:T(8,128)(2,1)S(1)}, bf16[1024,128]{1,0:T(8,128)(2,1)S(1)}, bf16[1024,128]{1,0:T(8,128)(2,1)S(1)}) custom-call(bf16[1024,128]{1,0:T(8,128)(2,1)S(1)} %get-tuple-element.50.first, bf16[1024,128]{1,0:T(8,128)(2,1)S(1)} %collective-permute-done.1.western, bf16[1024,128]{1,0:T(8,128)(2,1)S(1)} %collective-permute-done.2.eastern, ...), custom_call_target="tpu_custom_call" | custom-call | flops 4294967296 | bytes 2097152 | tf_op jit(solution)/shard_map/pallas_call | solution.py:560
  20.0 0.0 collective-permute-done.3.western_other
  20.0 0.0 collective-permute-done.4.eastern_other
  20.0 0.2 collective-permute-start.6
  20.3 6.8 %shard_map.98 = (bf16[128,1024]{1,0:T(8,128)(2,1)S(1)}, bf16[1024,1024]{1,0:T(8,128)(2,1)S(1)}, bf16[1024,1024]{1,0:T(8,128)(2,1)S(1)}) custom-call(bf16[1024,128]{1,0:T(8,128)(2,1)S(1)} %get-tuple-element.38.basis, bf16[1024,128]{1,0:T(8,128)(2,1)S(1)} %get-tuple-element.39.edge, bf16[1024,1024]{1,0:T(8,128)(2,1)S(1)} %get-tuple-element.55.sketched, ...), custom_call_target="tpu_custom_call" | custom-call | flops 8589934592 | bytes 2097152 | tf_op jit(solution)/shard_map/pallas_call | solution.py:560
  27.1 1.2 %shard_map.99 = (bf16[1024,128]{1,0:T(8,128)(2,1)S(1)}, bf16[1024,128]{1,0:T(8,128)(2,1)S(1)}) custom-call(bf16[128,1024]{1,0:T(8,128)(2,1)S(1)} %get-tuple-element.60.closing, bf16[1024,1024]{1,0:T(8,128)(2,1)S(1)} %get-tuple-element.61.absorbed, bf16[1024,1024]{1,0:T(8,128)(2,1)S(1)} %get-tuple-element.62.closed), custom_call_target="tpu_custom_call" | custom-call | flops 2147483648 | bytes 2097152 | tf_op jit(solution)/shard_map/pallas_call | solution.py:560
  28.3 0.4 %collective-permute-start.5 = (bf16[1024,128]{1,0:T(8,128)(2,1)S(1)}, bf16[1024,128]{1,0:T(8,128)(2,1)S(1)}, u32[]{:S(2)}, u32[]{:S(2)}) collective-permute-start(bf16[1024,128]{1,0:T(8,128)(2,1)S(1)} %get-tuple-element.63), channel_id=1, source_target_pairs={{0,1},{1,0},{2,3},{3,2},{4,5},{5,4},{6,7},{7,6},{8,9},{9,8},{10,11... | collective-permute-start | bytes 786440 | tf_op jit(solution)/shard_map/ppermute | solution.py:585
  28.7 0.0 collective-permute-done.6.carried
  28.7 1.4 %shard_map.100.product = f32[256,256]{1,0:T(8,128)S(1)} custom-call(bf16[256,4096]{1,0:T(8,128)(2,1)S(1)} %get-tuple-element.64.x_first, bf16[1024,128]{1,0:T(8,128)(2,1)S(1)} %get-tuple-element.65.back, bf16[1024,128]{1,0:T(8,128)(2,1)S(1)} %collective-permute-done.6.carried), custom_call_target="tpu_custom_call" | custom-call | flops 2147483648 | bytes 2097152 | tf_op jit(solution)/shard_map/pallas_call | solution.py:560
  30.1 0.0 collective-permute-done.5.received
  30.1 1.3 %shard_map.101 = (f32[2,4096]{1,0:T(2,128)}, bf16[1024,128]{1,0:T(8,128)(2,1)}, bf16[1024,128]{1,0:T(8,128)(2,1)}) custom-call(f32[256,256]{1,0:T(8,128)S(1)} %shard_map.100.product, s32[1,1]{1,0:T(1,128)S(6)} %copy.10.choice, bf16[1024,128]{1,0:T(8,128)(2,1)S(1)} %get-tuple-element.68.keep, bf16[1024,128]{1,0:T(8,128)(2,1)S(1)} %collective-permute-done.5.received), custom_call_target="tpu_custom_call" | custom-call | flops 1073741824 | bytes 2097152 | tf_op jit(solution)/shard_map/pallas_call | solution.py:560
Async XLA Ops:
  0.6 16.6 %collective-permute-start.1 = (bf16[1024,128]{1,0:T(8,128)(2,1)}, bf16[1024,128]{1,0:T(8,128)(2,1)S(1)}, u32[]{:S(2)}, u32[]{:S(2)}) collective-permute-start(bf16[1024,128]{1,0:T(8,128)(2,1)} %bitcast.10), channel_id=1, source_target_pairs={{0,2},{2,4},{4,6},{6,8},{8,10},{10,12},{12,14},{14,0},{1,3},{3,5},... | collective-permute-start | bytes 786440 | tf_op jit(solution)/shard_map/ppermute | solution.py:581
  3.6 13.7 %collective-permute-start.2 = (bf16[1024,128]{1,0:T(8,128)(2,1)}, bf16[1024,128]{1,0:T(8,128)(2,1)S(1)}, u32[]{:S(2)}, u32[]{:S(2)}) collective-permute-start(bf16[1024,128]{1,0:T(8,128)(2,1)} %bitcast.11), channel_id=1, source_target_pairs={{0,14},{2,0},{4,2},{6,4},{8,6},{10,8},{12,10},{14,12},{1,15},{3,1}... | collective-permute-start | bytes 786440 | tf_op jit(solution)/shard_map/ppermute | solution.py:581
  14.2 1.2 %collective-permute-start = (bf16[1,4096]{1,0:T(2,128)(2,1)S(1)}, bf16[1,4096]{1,0:T(2,128)(2,1)S(1)}, u32[]{:S(2)}, u32[]{:S(2)}) collective-permute-start(bf16[1,4096]{1,0:T(2,128)(2,1)S(1)} %get-tuple-element.40), channel_id=1, source_target_pairs={{0,1},{1,0},{2,3},{3,2},{4,5},{5,4},{6,7},{7,6},{8,9},{9,8},{10,11... | collective-permute-start | bytes 24584 | tf_op jit(solution)/shard_map/ppermute | solution.py:585
  17.3 2.7 %collective-permute-start.3 = (bf16[1024,128]{1,0:T(8,128)(2,1)S(1)}, bf16[1024,128]{1,0:T(8,128)(2,1)S(1)}, u32[]{:S(2)}, u32[]{:S(2)}) collective-permute-start(bf16[1024,128]{1,0:T(8,128)(2,1)S(1)} %collective-permute-done.1.western), channel_id=1, source_target_pairs={{0,1},{1,0},{2,3},{3,2},{4,5},{5,4},{6,7},{7,6},{8,9},{9,8},{10,11... | collective-permute-start | bytes 786440 | tf_op jit(solution)/shard_map/ppermute | solution.py:585
  17.5 2.5 %collective-permute-start.4 = (bf16[1024,128]{1,0:T(8,128)(2,1)S(1)}, bf16[1024,128]{1,0:T(8,128)(2,1)S(1)}, u32[]{:S(2)}, u32[]{:S(2)}) collective-permute-start(bf16[1024,128]{1,0:T(8,128)(2,1)S(1)} %collective-permute-done.2.eastern), channel_id=1, source_target_pairs={{0,1},{1,0},{2,3},{3,2},{4,5},{5,4},{6,7},{7,6},{8,9},{9,8},{10,11... | collective-permute-start | bytes 786440 | tf_op jit(solution)/shard_map/ppermute | solution.py:585
  20.0 8.6 %collective-permute-start.6 = (bf16[1024,128]{1,0:T(8,128)(2,1)S(1)}, bf16[1024,128]{1,0:T(8,128)(2,1)S(1)}, u32[]{:S(2)}, u32[]{:S(2)}) collective-permute-start(bf16[1024,128]{1,0:T(8,128)(2,1)S(1)} %get-tuple-element.66), channel_id=1, source_target_pairs={{0,1},{1,0},{2,3},{3,2},{4,5},{5,4},{6,7},{7,6},{8,9},{9,8},{10,11... | collective-permute-start | bytes 786440 | tf_op jit(solution)/shard_map/ppermute | solution.py:585
  28.3 1.8 %collective-permute-start.5 = (bf16[1024,128]{1,0:T(8,128)(2,1)S(1)}, bf16[1024,128]{1,0:T(8,128)(2,1)S(1)}, u32[]{:S(2)}, u32[]{:S(2)}) collective-permute-start(bf16[1024,128]{1,0:T(8,128)(2,1)S(1)} %get-tuple-element.63), channel_id=1, source_target_pairs={{0,1},{1,0},{2,3},{3,2},{4,5},{5,4},{6,7},{7,6},{8,9},{9,8},{10,11... | collective-permute-start | bytes 786440 | tf_op jit(solution)/shard_map/ppermute | solution.py:585

commit v5 on v4

--- a/solution.py
+++ b/solution.py
@@ -467,7 +467,7 @@
         + kron_steps(woven_1, edge, x_next, True)
         + absorb_steps(kron_1, x_next, closed, chi)
     )
-    (inverse,) = chol_inverse([gram], 3, beside)
+    (inverse,) = chol_inverse([gram], 2, beside)
     inverse_high, inverse_low = split(inverse)
     ortho = nn(inverse_high, high) + (nn(inverse_high, low) + nn(inverse_low, high))
     closing[...] = ortho.astype(BF16)

time: 31.8 us -> 31.1 us (0.978)
  Pallas kernels: 22.2 us -> 21.5 us
    pallas_call x8, Pallas kernels: 22.2 us -> 21.5 us  [call(): pl.pallas_call(kernel, out_shape=[jax.ShapeDtypeStruct(s, t) for s, t in...]
  transfers between devices with their start and end apart: 7 -> 7, of which waited for: 1 -> 1; matrix products, arithmetic and copies ran while one was open for 0% -> 0% of each run, Pallas kernels for 66% -> 65%
where the time goes in v5:
time: 31.1 us; the launch traced here: 30.9 us
  Pallas kernels  21.5 us (69%)
  starting transfers between devices  7.37 us (24%)
  between operations  1.55 us (5%)
  waiting for transfers between devices  0.49 us (2%)
    pallas_call x8, Pallas kernels, call(): pl.pallas_call(kernel, out_shape=[jax.ShapeDtypeStruct(s, t) for s, t in...  21.5 us
    ppermute x2, starting transfers between devices, shifted(): lax.ppermute(block, axis, [(i, (i + steps) % count) for i in range(count)])  6.09 us
    ppermute x5, starting transfers between devices, exchanged(): return lax.ppermute(block, axis, [(0, 1), (1, 0)])  1.28 us
  transfers between devices with their start and end apart: 7, of which 1 were waited for; matrix products, arithmetic and copies ran while one was open for 0% of the time, Pallas kernels for 65%

profile of v5, /device:TPU:0, one launch (start us, length us, event | category | flops | bytes accessed | tf_op | source)
XLA Modules:
  0.0 30.9 jit_solution(18028463069208160290)
XLA Ops:
  0.6 3.0 %collective-permute-start.1 = (bf16[1024,128]{1,0:T(8,128)(2,1)}, bf16[1024,128]{1,0:T(8,128)(2,1)S(1)}, u32[]{:S(2)}, u32[]{:S(2)}) collective-permute-start(bf16[1024,128]{1,0:T(8,128)(2,1)} %bitcast.10), channel_id=1, source_target_pairs={{0,2},{2,4},{4,6},{6,8},{8,10},{10,12},{12,14},{14,0},{1,3},{3,5},... | collective-permute-start | bytes 786440 | tf_op jit(solution)/shard_map/ppermute | solution.py:581
  3.6 3.1 %collective-permute-start.2 = (bf16[1024,128]{1,0:T(8,128)(2,1)}, bf16[1024,128]{1,0:T(8,128)(2,1)S(1)}, u32[]{:S(2)}, u32[]{:S(2)}) collective-permute-start(bf16[1024,128]{1,0:T(8,128)(2,1)} %bitcast.11), channel_id=1, source_target_pairs={{0,14},{2,0},{4,2},{6,4},{8,6},{10,8},{12,10},{14,12},{1,15},{3,1}... | collective-permute-start | bytes 786440 | tf_op jit(solution)/shard_map/ppermute | solution.py:581
  7.4 6.8 %shard_map.94 = (bf16[1024,128]{1,0:T(8,128)(2,1)S(1)}, bf16[128,1024]{1,0:T(8,128)(2,1)S(1)}, bf16[1024,128]{1,0:T(8,128)(2,1)S(1)}, bf16[1024,128]{1,0:T(8,128...) custom-call(bf16[1024,128]{1,0:T(8,128)(2,1)} %bitcast.8, ...), custom_call_target="tpu_custom_call" | custom-call | flops 2147483648 | bytes 2097152 | tf_op jit(solution)/shard_map/pallas_call | solution.py:560
  14.2 0.1 collective-permute-start
  14.2 0.7 %shard_map.95.x = bf16[256,4096]{1,0:T(8,128)(2,1)S(1)} custom-call(bf16[128,1024]{1,0:T(8,128)(2,1)S(1)} %get-tuple-element.41.basis_lanes, bf16[1024,128]{1,0:T(8,128)(2,1)S(1)} %get-tuple-element.42.sketch_t), custom_call_target="tpu_custom_call" | custom-call | flops 1073741824 | bytes 2097152 | tf_op jit(solution)/shard_map/pallas_call | solution.py:560
  14.9 0.5 %collective-permute-done.site_other = bf16[1,4096]{1,0:T(2,128)(2,1)S(1)} collective-permute-done((bf16[1,4096]{1,0:T(2,128)(2,1)S(1)}, bf16[1,4096]{1,0:T(2,128)(2,1)S(1)}, u32[]{:S(2)}, u32[]{:S(2)}) %collective-permute-start) | collective-permute-done | bytes 8224 | tf_op jit(solution)/shard_map/ppermute | solution.py:585
  15.4 1.8 %shard_map.96 = (bf16[256,256]{1,0:T(8,128)(2,1)S(1)}, bf16[256,256]{1,0:T(8,128)(2,1)S(1)}, bf16[1024,1024]{1,0:T(8,128)(2,1)S(1)}) custom-call(bf16[256,4096]{1,0:T(8,128)(2,1)S(1)} %shard_map.95.x, bf16[1,4096]{1,0:T(2,128)(2,1)S(1)} %collective-permute-done.site_other, bf16[256,64]{1,0:T(8,128)(2,1)S(1)} %get-tuple-element.45.own_upper, ...), custom_call_target="tpu_custom_call" | custom-call | flops 2147483648 | bytes 2097152 | tf_op jit(solution)/shard_map/pallas_call | solution.py:560
  17.3 0.0 collective-permute-done.1.western
  17.3 0.0 collective-permute-done.2.eastern
  17.3 0.2 collective-permute-start.3
  17.5 0.3 %collective-permute-start.4 = (bf16[1024,128]{1,0:T(8,128)(2,1)S(1)}, bf16[1024,128]{1,0:T(8,128)(2,1)S(1)}, u32[]{:S(2)}, u32[]{:S(2)}) collective-permute-start(bf16[1024,128]{1,0:T(8,128)(2,1)S(1)} %collective-permute-done.2.eastern), channel_id=1, source_target_pairs={{0,1},{1,0},{2,3},{3,2},{4,5},{5,4},{6,7},{7,6},{8,9},{9,8},{10,11... | collective-permute-start | bytes 786440 | tf_op jit(solution)/shard_map/ppermute | solution.py:585
  17.9 2.1 %shard_map.97 = (bf16[256,4096]{1,0:T(8,128)(2,1)S(1)}, bf16[1024,128]{1,0:T(8,128)(2,1)S(1)}, bf16[1024,128]{1,0:T(8,128)(2,1)S(1)}) custom-call(bf16[1024,128]{1,0:T(8,128)(2,1)S(1)} %get-tuple-element.50.first, bf16[1024,128]{1,0:T(8,128)(2,1)S(1)} %collective-permute-done.1.western, bf16[1024,128]{1,0:T(8,128)(2,1)S(1)} %collective-permute-done.2.eastern, ...), custom_call_target="tpu_custom_call" | custom-call | flops 4294967296 | bytes 2097152 | tf_op jit(solution)/shard_map/pallas_call | solution.py:560
  20.0 0.0 collective-permute-done.3.western_other
  20.0 0.0 collective-permute-done.4.eastern_other
  20.0 0.2 collective-permute-start.6
  20.3 6.1 %shard_map.98 = (bf16[128,1024]{1,0:T(8,128)(2,1)S(1)}, bf16[1024,1024]{1,0:T(8,128)(2,1)S(1)}, bf16[1024,1024]{1,0:T(8,128)(2,1)S(1)}) custom-call(bf16[1024,128]{1,0:T(8,128)(2,1)S(1)} %get-tuple-element.38.basis, bf16[1024,128]{1,0:T(8,128)(2,1)S(1)} %get-tuple-element.39.edge, bf16[1024,1024]{1,0:T(8,128)(2,1)S(1)} %get-tuple-element.55.sketched, ...), custom_call_target="tpu_custom_call" | custom-call | flops 8589934592 | bytes 2097152 | tf_op jit(solution)/shard_map/pallas_call | solution.py:560
  26.4 1.2 %shard_map.99 = (bf16[1024,128]{1,0:T(8,128)(2,1)S(1)}, bf16[1024,128]{1,0:T(8,128)(2,1)S(1)}) custom-call(bf16[128,1024]{1,0:T(8,128)(2,1)S(1)} %get-tuple-element.60.closing, bf16[1024,1024]{1,0:T(8,128)(2,1)S(1)} %get-tuple-element.61.absorbed, bf16[1024,1024]{1,0:T(8,128)(2,1)S(1)} %get-tuple-element.62.closed), custom_call_target="tpu_custom_call" | custom-call | flops 2147483648 | bytes 2097152 | tf_op jit(solution)/shard_map/pallas_call | solution.py:560
  27.6 0.4 %collective-permute-start.5 = (bf16[1024,128]{1,0:T(8,128)(2,1)S(1)}, bf16[1024,128]{1,0:T(8,128)(2,1)S(1)}, u32[]{:S(2)}, u32[]{:S(2)}) collective-permute-start(bf16[1024,128]{1,0:T(8,128)(2,1)S(1)} %get-tuple-element.63), channel_id=1, source_target_pairs={{0,1},{1,0},{2,3},{3,2},{4,5},{5,4},{6,7},{7,6},{8,9},{9,8},{10,11... | collective-permute-start | bytes 786440 | tf_op jit(solution)/shard_map/ppermute | solution.py:585
  28.0 0.0 collective-permute-done.6.carried
  28.0 1.4 %shard_map.100.product = f32[256,256]{1,0:T(8,128)S(1)} custom-call(bf16[256,4096]{1,0:T(8,128)(2,1)S(1)} %get-tuple-element.64.x_first, bf16[1024,128]{1,0:T(8,128)(2,1)S(1)} %get-tuple-element.65.back, bf16[1024,128]{1,0:T(8,128)(2,1)S(1)} %collective-permute-done.6.carried), custom_call_target="tpu_custom_call" | custom-call | flops 2147483648 | bytes 2097152 | tf_op jit(solution)/shard_map/pallas_call | solution.py:560
  29.4 0.0 collective-permute-done.5.received
  29.4 1.3 %shard_map.101 = (f32[2,4096]{1,0:T(2,128)}, bf16[1024,128]{1,0:T(8,128)(2,1)}, bf16[1024,128]{1,0:T(8,128)(2,1)}) custom-call(f32[256,256]{1,0:T(8,128)S(1)} %shard_map.100.product, s32[1,1]{1,0:T(1,128)S(6)} %copy.10.choice, bf16[1024,128]{1,0:T(8,128)(2,1)S(1)} %get-tuple-element.68.keep, bf16[1024,128]{1,0:T(8,128)(2,1)S(1)} %collective-permute-done.5.received), custom_call_target="tpu_custom_call" | custom-call | flops 1073741824 | bytes 2097152 | tf_op jit(solution)/shard_map/pallas_call | solution.py:560
Async XLA Ops:
  0.6 16.6 %collective-permute-start.1 = (bf16[1024,128]{1,0:T(8,128)(2,1)}, bf16[1024,128]{1,0:T(8,128)(2,1)S(1)}, u32[]{:S(2)}, u32[]{:S(2)}) collective-permute-start(bf16[1024,128]{1,0:T(8,128)(2,1)} %bitcast.10), channel_id=1, source_target_pairs={{0,2},{2,4},{4,6},{6,8},{8,10},{10,12},{12,14},{14,0},{1,3},{3,5},... | collective-permute-start | bytes 786440 | tf_op jit(solution)/shard_map/ppermute | solution.py:581
  3.6 13.7 %collective-permute-start.2 = (bf16[1024,128]{1,0:T(8,128)(2,1)}, bf16[1024,128]{1,0:T(8,128)(2,1)S(1)}, u32[]{:S(2)}, u32[]{:S(2)}) collective-permute-start(bf16[1024,128]{1,0:T(8,128)(2,1)} %bitcast.11), channel_id=1, source_target_pairs={{0,14},{2,0},{4,2},{6,4},{8,6},{10,8},{12,10},{14,12},{1,15},{3,1}... | collective-permute-start | bytes 786440 | tf_op jit(solution)/shard_map/ppermute | solution.py:581
  14.2 1.2 %collective-permute-start = (bf16[1,4096]{1,0:T(2,128)(2,1)S(1)}, bf16[1,4096]{1,0:T(2,128)(2,1)S(1)}, u32[]{:S(2)}, u32[]{:S(2)}) collective-permute-start(bf16[1,4096]{1,0:T(2,128)(2,1)S(1)} %get-tuple-element.40), channel_id=1, source_target_pairs={{0,1},{1,0},{2,3},{3,2},{4,5},{5,4},{6,7},{7,6},{8,9},{9,8},{10,11... | collective-permute-start | bytes 24584 | tf_op jit(solution)/shard_map/ppermute | solution.py:585
  17.3 2.7 %collective-permute-start.3 = (bf16[1024,128]{1,0:T(8,128)(2,1)S(1)}, bf16[1024,128]{1,0:T(8,128)(2,1)S(1)}, u32[]{:S(2)}, u32[]{:S(2)}) collective-permute-start(bf16[1024,128]{1,0:T(8,128)(2,1)S(1)} %collective-permute-done.1.western), channel_id=1, source_target_pairs={{0,1},{1,0},{2,3},{3,2},{4,5},{5,4},{6,7},{7,6},{8,9},{9,8},{10,11... | collective-permute-start | bytes 786440 | tf_op jit(solution)/shard_map/ppermute | solution.py:585
  17.5 2.5 %collective-permute-start.4 = (bf16[1024,128]{1,0:T(8,128)(2,1)S(1)}, bf16[1024,128]{1,0:T(8,128)(2,1)S(1)}, u32[]{:S(2)}, u32[]{:S(2)}) collective-permute-start(bf16[1024,128]{1,0:T(8,128)(2,1)S(1)} %collective-permute-done.2.eastern), channel_id=1, source_target_pairs={{0,1},{1,0},{2,3},{3,2},{4,5},{5,4},{6,7},{7,6},{8,9},{9,8},{10,11... | collective-permute-start | bytes 786440 | tf_op jit(solution)/shard_map/ppermute | solution.py:585
  20.0 8.0 %collective-permute-start.6 = (bf16[1024,128]{1,0:T(8,128)(2,1)S(1)}, bf16[1024,128]{1,0:T(8,128)(2,1)S(1)}, u32[]{:S(2)}, u32[]{:S(2)}) collective-permute-start(bf16[1024,128]{1,0:T(8,128)(2,1)S(1)} %get-tuple-element.66), channel_id=1, source_target_pairs={{0,1},{1,0},{2,3},{3,2},{4,5},{5,4},{6,7},{7,6},{8,9},{9,8},{10,11... | collective-permute-start | bytes 786440 | tf_op jit(solution)/shard_map/ppermute | solution.py:585
  27.6 1.8 %collective-permute-start.5 = (bf16[1024,128]{1,0:T(8,128)(2,1)S(1)}, bf16[1024,128]{1,0:T(8,128)(2,1)S(1)}, u32[]{:S(2)}, u32[]{:S(2)}) collective-permute-start(bf16[1024,128]{1,0:T(8,128)(2,1)S(1)} %get-tuple-element.63), channel_id=1, source_target_pairs={{0,1},{1,0},{2,3},{3,2},{4,5},{5,4},{6,7},{7,6},{8,9},{9,8},{10,11... | collective-permute-start | bytes 786440 | tf_op jit(solution)/shard_map/ppermute | solution.py:585

commit v6 on v5

--- a/solution.py
+++ b/solution.py
@@ -405,7 +405,7 @@
         carried[s * chi : (s + 1) * chi, :] = state[:, s * chi : (s + 1) * chi]
 
 
-def upper_kernel(
+def rows_kernel(
     basis,
     edge,
     sketched,
@@ -415,7 +415,8 @@
     eastern_other,
     kron_0,
     kron_1,
-    closing,
+    keep,
+    send,
     absorbed,
     closed,
     wide_0,
@@ -470,25 +471,18 @@
     (inverse,) = chol_inverse([gram], 2, beside)
     inverse_high, inverse_low = split(inverse)
     ortho = nn(inverse_high, high) + (nn(inverse_high, low) + nn(inverse_low, high))
-    closing[...] = ortho.astype(BF16)
-
-
-def lower_kernel(closing, absorbed, closed, keep, send, wide_0, wide_1):
-    side = lax.axis_index("row")
-    chi = closing.shape[0]
-    bond = closing.shape[1] // chi
-    blocks = [slice(j * chi, (j + 1) * chi) for j in range(bond)]
-    upper = nt(absorbed[...], closing[...])
+    closing = ortho.astype(BF16)
+    upper = nt(absorbed[...], closing)
+    lower = nn(closing, closed[...])
     new_0 = scaled([upper[at, :] for at in blocks], wide_0)
-    lower = nn(closing[...], closed[...])
     new_1 = scaled([lower[:, at] for at in blocks], wide_1)
 
-    @pl.when(side == 0)
+    @pl.when(is_left)
     def _():
         keep[...] = new_0
         send[...] = new_1
 
-    @pl.when(side == 1)
+    @pl.when(jnp.logical_not(is_left))
     def _():
         keep[...] = new_1
         send[...] = new_0
@@ -613,19 +607,19 @@
         [(tall, BF16)] * 3
         + [(sites.shape, BF16), (tall, F32), (tall, F32), (flat, BF16), (flat, BF16)],
         [top_env.reshape(tall), bottom_env.reshape(tall), sketch, sites, configuration],
-        2**31,
+        2**24,
         in_place=(0, 1, 2, 3),
         copies=4,
     )
     site_other = exchanged(site, "row")
-    (joined,) = call(join_kernel, [(stack, BF16)], [], [basis_lanes, sketch_t], 2**30)
+    (joined,) = call(join_kernel, [(stack, BF16)], [], [basis_lanes, sketch_t], 2**24)
     site_other, joined = lax.optimization_barrier((site_other, joined))
     kron_0, kron_1, sketched = call(
         prepare_kernel,
         [(kron, BF16), (kron, BF16), (square, BF16)],
         [(kron, BF16)],
         [joined, site_other, *own],
-        2**31,
+        2**24,
     )
     sketched, western, eastern = lax.optimization_barrier((sketched, western, eastern))
     western_other = exchanged(western, "row")
@@ -641,10 +635,12 @@
         (sketched, carried, western_other, eastern_other)
     )
     carried = exchanged(carried, "row")
-    closing, absorbed, closed = call(
-        upper_kernel,
-        [(flat, BF16), (square, BF16), (square, BF16)],
+    keep, send = call(
+        rows_kernel,
+        [(tall, BF16), (tall, BF16)],
         [
+            (square, BF16),
+            (square, BF16),
             (tall, F32),
             (tall, F32),
             (tall, BF16),
@@ -666,13 +662,6 @@
         ],
         2**33,
     )
-    keep, send = call(
-        lower_kernel,
-        [(tall, BF16), (tall, BF16)],
-        [(tall, F32), (tall, F32)],
-        [closing, absorbed, closed],
-        2**31,
-    )
     received = exchanged(send, "row")
     (product,) = call(
         product_kernel,

time: 31.1 us -> 30.9 us (level)
    pallas_call x8 -> x7, Pallas kernels: 21.5 us -> 21.3 us  [call(): pl.pallas_call(kernel, out_shape=[jax.ShapeDtypeStruct(s, t) for s, t in...]
where the time goes in v6:
time: 30.9 us; the launch traced here: 30.8 us
  Pallas kernels  21.3 us (69%)
  starting transfers between devices  7.38 us (24%)
  between operations  1.54 us (5%)
  waiting for transfers between devices  0.49 us (2%)
    pallas_call x7, Pallas kernels, call(): pl.pallas_call(kernel, out_shape=[jax.ShapeDtypeStruct(s, t) for s, t in...  21.3 us
    ppermute x2, starting transfers between devices, shifted(): lax.ppermute(block, axis, [(i, (i + steps) % count) for i in range(count)])  6.09 us
    ppermute x5, starting transfers between devices, exchanged(): return lax.ppermute(block, axis, [(0, 1), (1, 0)])  1.29 us
  transfers between devices with their start and end apart: 7, of which 1 were waited for; matrix products, arithmetic and copies ran while one was open for 0% of the time, Pallas kernels for 65%

profile of v6, /device:TPU:0, one launch (start us, length us, event | category | flops | bytes accessed | tf_op | source)
XLA Modules:
  0.0 30.8 jit_solution(7382880142606271421)
XLA Ops:
  0.6 3.0 %collective-permute-start.1 = (bf16[1024,128]{1,0:T(8,128)(2,1)}, bf16[1024,128]{1,0:T(8,128)(2,1)S(1)}, u32[]{:S(2)}, u32[]{:S(2)}) collective-permute-start(bf16[1024,128]{1,0:T(8,128)(2,1)} %bitcast.11), channel_id=1, source_target_pairs={{0,2},{2,4},{4,6},{6,8},{8,10},{10,12},{12,14},{14,0},{1,3},{3,5},... | collective-permute-start | bytes 786440 | tf_op jit(solution)/shard_map/ppermute | solution.py:575
  3.6 3.1 %collective-permute-start.2 = (bf16[1024,128]{1,0:T(8,128)(2,1)}, bf16[1024,128]{1,0:T(8,128)(2,1)S(1)}, u32[]{:S(2)}, u32[]{:S(2)}) collective-permute-start(bf16[1024,128]{1,0:T(8,128)(2,1)} %bitcast.12), channel_id=1, source_target_pairs={{0,14},{2,0},{4,2},{6,4},{8,6},{10,8},{12,10},{14,12},{1,15},{3,1}... | collective-permute-start | bytes 786440 | tf_op jit(solution)/shard_map/ppermute | solution.py:575
  7.4 6.8 %shard_map.94 = (bf16[1024,128]{1,0:T(8,128)(2,1)S(1)}, bf16[128,1024]{1,0:T(8,128)(2,1)S(1)}, bf16[1024,128]{1,0:T(8,128)(2,1)S(1)}, bf16[1024,128]{1,0:T(8,128...) custom-call(bf16[1024,128]{1,0:T(8,128)(2,1)} %bitcast.8, ...), custom_call_target="tpu_custom_call" | custom-call | flops 16777216 | bytes 2097152 | tf_op jit(solution)/shard_map/pallas_call | solution.py:554
  14.2 0.1 collective-permute-start
  14.2 0.7 %shard_map.95.x = bf16[256,4096]{1,0:T(8,128)(2,1)S(1)} custom-call(bf16[128,1024]{1,0:T(8,128)(2,1)S(1)} %get-tuple-element.38.basis_lanes, bf16[1024,128]{1,0:T(8,128)(2,1)S(1)} %get-tuple-element.39.sketch_t), custom_call_target="tpu_custom_call" | custom-call | flops 16777216 | bytes 2097152 | tf_op jit(solution)/shard_map/pallas_call | solution.py:554
  14.9 0.5 %collective-permute-done.site_other = bf16[1,4096]{1,0:T(2,128)(2,1)S(1)} collective-permute-done((bf16[1,4096]{1,0:T(2,128)(2,1)S(1)}, bf16[1,4096]{1,0:T(2,128)(2,1)S(1)}, u32[]{:S(2)}, u32[]{:S(2)}) %collective-permute-start) | collective-permute-done | bytes 8224 | tf_op jit(solution)/shard_map/ppermute | solution.py:579
  15.4 1.8 %shard_map.96 = (bf16[256,256]{1,0:T(8,128)(2,1)S(1)}, bf16[256,256]{1,0:T(8,128)(2,1)S(1)}, bf16[1024,1024]{1,0:T(8,128)(2,1)S(1)}) custom-call(bf16[256,4096]{1,0:T(8,128)(2,1)S(1)} %shard_map.95.x, bf16[1,4096]{1,0:T(2,128)(2,1)S(1)} %collective-permute-done.site_other, bf16[256,64]{1,0:T(8,128)(2,1)S(1)} %get-tuple-element.42.own_upper, ...), custom_call_target="tpu_custom_call" | custom-call | flops 16777216 | bytes 2097152 | tf_op jit(solution)/shard_map/pallas_call | solution.py:554
  17.3 0.0 collective-permute-done.1.western
  17.3 0.0 collective-permute-done.2.eastern
  17.3 0.2 collective-permute-start.3
  17.5 0.3 %collective-permute-start.4 = (bf16[1024,128]{1,0:T(8,128)(2,1)S(1)}, bf16[1024,128]{1,0:T(8,128)(2,1)S(1)}, u32[]{:S(2)}, u32[]{:S(2)}) collective-permute-start(bf16[1024,128]{1,0:T(8,128)(2,1)S(1)} %collective-permute-done.2.eastern), channel_id=1, source_target_pairs={{0,1},{1,0},{2,3},{3,2},{4,5},{5,4},{6,7},{7,6},{8,9},{9,8},{10,11... | collective-permute-start | bytes 786440 | tf_op jit(solution)/shard_map/ppermute | solution.py:579
  17.9 2.1 %shard_map.97 = (bf16[256,4096]{1,0:T(8,128)(2,1)S(1)}, bf16[1024,128]{1,0:T(8,128)(2,1)S(1)}, bf16[1024,128]{1,0:T(8,128)(2,1)S(1)}) custom-call(bf16[1024,128]{1,0:T(8,128)(2,1)S(1)} %get-tuple-element.47.first, bf16[1024,128]{1,0:T(8,128)(2,1)S(1)} %collective-permute-done.1.western, bf16[1024,128]{1,0:T(8,128)(2,1)S(1)} %collective-permute-done.2.eastern, ...), custom_call_target="tpu_custom_call" | custom-call | flops 4294967296 | bytes 2097152 | tf_op jit(solution)/shard_map/pallas_call | solution.py:554
  20.0 0.0 collective-permute-done.3.western_other
  20.0 0.0 collective-permute-done.4.eastern_other
  20.0 0.2 collective-permute-start.6
  20.3 7.1 %shard_map.98 = (bf16[1024,128]{1,0:T(8,128)(2,1)S(1)}, bf16[1024,128]{1,0:T(8,128)(2,1)S(1)}) custom-call(bf16[1024,128]{1,0:T(8,128)(2,1)S(1)} %get-tuple-element.35.basis, bf16[1024,128]{1,0:T(8,128)(2,1)S(1)} %get-tuple-element.36.edge, bf16[1024,1024]{1,0:T(8,128)(2,1)S(1)} %get-tuple-element.52.sketched, ...), custom_call_target="tpu_custom_call" | custom-call | flops 8589934592 | bytes 2097152 | tf_op jit(solution)/shard_map/pallas_call | solution.py:554
  27.4 0.4 %collective-permute-start.5 = (bf16[1024,128]{1,0:T(8,128)(2,1)S(1)}, bf16[1024,128]{1,0:T(8,128)(2,1)S(1)}, u32[]{:S(2)}, u32[]{:S(2)}) collective-permute-start(bf16[1024,128]{1,0:T(8,128)(2,1)S(1)} %get-tuple-element.57), channel_id=1, source_target_pairs={{0,1},{1,0},{2,3},{3,2},{4,5},{5,4},{6,7},{7,6},{8,9},{9,8},{10,11... | collective-permute-start | bytes 786440 | tf_op jit(solution)/shard_map/ppermute | solution.py:579
  27.8 0.0 collective-permute-done.6.carried
  27.8 1.4 %shard_map.99.product = f32[256,256]{1,0:T(8,128)S(1)} custom-call(bf16[256,4096]{1,0:T(8,128)(2,1)S(1)} %get-tuple-element.58.x_first, bf16[1024,128]{1,0:T(8,128)(2,1)S(1)} %get-tuple-element.59.back, bf16[1024,128]{1,0:T(8,128)(2,1)S(1)} %collective-permute-done.6.carried), custom_call_target="tpu_custom_call" | custom-call | flops 2147483648 | bytes 2097152 | tf_op jit(solution)/shard_map/pallas_call | solution.py:554
  29.2 0.0 collective-permute-done.5.received
  29.3 1.3 %shard_map.100 = (f32[2,4096]{1,0:T(2,128)}, bf16[1024,128]{1,0:T(8,128)(2,1)}, bf16[1024,128]{1,0:T(8,128)(2,1)}) custom-call(f32[256,256]{1,0:T(8,128)S(1)} %shard_map.99.product, s32[1,1]{1,0:T(1,128)S(6)} %copy.10.choice, bf16[1024,128]{1,0:T(8,128)(2,1)S(1)} %get-tuple-element.62.keep, bf16[1024,128]{1,0:T(8,128)(2,1)S(1)} %collective-permute-done.5.received), custom_call_target="tpu_custom_call" | custom-call | flops 1073741824 | bytes 2097152 | tf_op jit(solution)/shard_map/pallas_call | solution.py:554
Async XLA Ops:
  0.6 16.6 %collective-permute-start.1 = (bf16[1024,128]{1,0:T(8,128)(2,1)}, bf16[1024,128]{1,0:T(8,128)(2,1)S(1)}, u32[]{:S(2)}, u32[]{:S(2)}) collective-permute-start(bf16[1024,128]{1,0:T(8,128)(2,1)} %bitcast.11), channel_id=1, source_target_pairs={{0,2},{2,4},{4,6},{6,8},{8,10},{10,12},{12,14},{14,0},{1,3},{3,5},... | collective-permute-start | bytes 786440 | tf_op jit(solution)/shard_map/ppermute | solution.py:575
  3.6 13.7 %collective-permute-start.2 = (bf16[1024,128]{1,0:T(8,128)(2,1)}, bf16[1024,128]{1,0:T(8,128)(2,1)S(1)}, u32[]{:S(2)}, u32[]{:S(2)}) collective-permute-start(bf16[1024,128]{1,0:T(8,128)(2,1)} %bitcast.12), channel_id=1, source_target_pairs={{0,14},{2,0},{4,2},{6,4},{8,6},{10,8},{12,10},{14,12},{1,15},{3,1}... | collective-permute-start | bytes 786440 | tf_op jit(solution)/shard_map/ppermute | solution.py:575
  14.2 1.2 %collective-permute-start = (bf16[1,4096]{1,0:T(2,128)(2,1)S(1)}, bf16[1,4096]{1,0:T(2,128)(2,1)S(1)}, u32[]{:S(2)}, u32[]{:S(2)}) collective-permute-start(bf16[1,4096]{1,0:T(2,128)(2,1)S(1)} %get-tuple-element.37), channel_id=1, source_target_pairs={{0,1},{1,0},{2,3},{3,2},{4,5},{5,4},{6,7},{7,6},{8,9},{9,8},{10,11... | collective-permute-start | bytes 24584 | tf_op jit(solution)/shard_map/ppermute | solution.py:579
  17.3 2.7 %collective-permute-start.3 = (bf16[1024,128]{1,0:T(8,128)(2,1)S(1)}, bf16[1024,128]{1,0:T(8,128)(2,1)S(1)}, u32[]{:S(2)}, u32[]{:S(2)}) collective-permute-start(bf16[1024,128]{1,0:T(8,128)(2,1)S(1)} %collective-permute-done.1.western), channel_id=1, source_target_pairs={{0,1},{1,0},{2,3},{3,2},{4,5},{5,4},{6,7},{7,6},{8,9},{9,8},{10,11... | collective-permute-start | bytes 786440 | tf_op jit(solution)/shard_map/ppermute | solution.py:579
  17.5 2.5 %collective-permute-start.4 = (bf16[1024,128]{1,0:T(8,128)(2,1)S(1)}, bf16[1024,128]{1,0:T(8,128)(2,1)S(1)}, u32[]{:S(2)}, u32[]{:S(2)}) collective-permute-start(bf16[1024,128]{1,0:T(8,128)(2,1)S(1)} %collective-permute-done.2.eastern), channel_id=1, source_target_pairs={{0,1},{1,0},{2,3},{3,2},{4,5},{5,4},{6,7},{7,6},{8,9},{9,8},{10,11... | collective-permute-start | bytes 786440 | tf_op jit(solution)/shard_map/ppermute | solution.py:579
  20.0 7.8 %collective-permute-start.6 = (bf16[1024,128]{1,0:T(8,128)(2,1)S(1)}, bf16[1024,128]{1,0:T(8,128)(2,1)S(1)}, u32[]{:S(2)}, u32[]{:S(2)}) collective-permute-start(bf16[1024,128]{1,0:T(8,128)(2,1)S(1)} %get-tuple-element.60), channel_id=1, source_target_pairs={{0,1},{1,0},{2,3},{3,2},{4,5},{5,4},{6,7},{7,6},{8,9},{9,8},{10,11... | collective-permute-start | bytes 786440 | tf_op jit(solution)/shard_map/ppermute | solution.py:579
  27.4 1.8 %collective-permute-start.5 = (bf16[1024,128]{1,0:T(8,128)(2,1)S(1)}, bf16[1024,128]{1,0:T(8,128)(2,1)S(1)}, u32[]{:S(2)}, u32[]{:S(2)}) collective-permute-start(bf16[1024,128]{1,0:T(8,128)(2,1)S(1)} %get-tuple-element.57), channel_id=1, source_target_pairs={{0,1},{1,0},{2,3},{3,2},{4,5},{5,4},{6,7},{7,6},{8,9},{9,8},{10,11... | collective-permute-start | bytes 786440 | tf_op jit(solution)/shard_map/ppermute | solution.py:579

commit v7 on v6

--- a/solution.py
+++ b/solution.py
@@ -445,7 +445,6 @@
     stacked = nn(sketched[...], rows_0[...])
     range_t = jnp.concatenate([stacked[blocks[d], :] for d in range(bond)], axis=1)
     high, low = split(range_t)
-    gram = nt(high, high) + (nt(high, low) + nt(low, high))
 
     def ready_lanes():
         for j in range(bond):
@@ -468,7 +467,12 @@
         + kron_steps(woven_1, edge, x_next, True)
         + absorb_steps(kron_1, x_next, closed, chi)
     )
-    (inverse,) = chol_inverse([gram], 2, beside)
+    for step in beside[:3]:
+        step()
+    gram = nt(high, high) + (nt(high, low) + nt(low, high))
+    for step in beside[3:6]:
+        step()
+    (inverse,) = chol_inverse([gram], 2, beside[6:])
     inverse_high, inverse_low = split(inverse)
     ortho = nn(inverse_high, high) + (nn(inverse_high, low) + nn(inverse_low, high))
     closing = ortho.astype(BF16)

time: 30.9 us -> 31 us (level)
  no operation moved by 1% of the time
where the time goes in v7:
time: 31 us; the launch traced here: 30.8 us
  Pallas kernels  21.4 us (69%)
  starting transfers between devices  7.37 us (24%)
  between operations  1.54 us (5%)
  waiting for transfers between devices  0.49 us (2%)
    pallas_call x7, Pallas kernels, call(): pl.pallas_call(kernel, out_shape=[jax.ShapeDtypeStruct(s, t) for s, t in...  21.4 us
    ppermute x2, starting transfers between devices, shifted(): lax.ppermute(block, axis, [(i, (i + steps) % count) for i in range(count)])  6.09 us
    ppermute x5, starting transfers between devices, exchanged(): return lax.ppermute(block, axis, [(0, 1), (1, 0)])  1.28 us
  transfers between devices with their start and end apart: 7, of which 1 were waited for; matrix products, arithmetic and copies ran while one was open for 0% of the time, Pallas kernels for 65%

profile of v7, /device:TPU:0, one launch (start us, length us, event | category | flops | bytes accessed | tf_op | source)
XLA Modules:
  0.0 30.8 jit_solution(3836768150616596207)
XLA Ops:
  0.6 3.0 %collective-permute-start.1 = (bf16[1024,128]{1,0:T(8,128)(2,1)}, bf16[1024,128]{1,0:T(8,128)(2,1)S(1)}, u32[]{:S(2)}, u32[]{:S(2)}) collective-permute-start(bf16[1024,128]{1,0:T(8,128)(2,1)} %bitcast.11), channel_id=1, source_target_pairs={{0,2},{2,4},{4,6},{6,8},{8,10},{10,12},{12,14},{14,0},{1,3},{3,5},... | collective-permute-start | bytes 786440 | tf_op jit(solution)/shard_map/ppermute | solution.py:579
  3.6 3.1 %collective-permute-start.2 = (bf16[1024,128]{1,0:T(8,128)(2,1)}, bf16[1024,128]{1,0:T(8,128)(2,1)S(1)}, u32[]{:S(2)}, u32[]{:S(2)}) collective-permute-start(bf16[1024,128]{1,0:T(8,128)(2,1)} %bitcast.12), channel_id=1, source_target_pairs={{0,14},{2,0},{4,2},{6,4},{8,6},{10,8},{12,10},{14,12},{1,15},{3,1}... | collective-permute-start | bytes 786440 | tf_op jit(solution)/shard_map/ppermute | solution.py:579
  7.4 6.8 %shard_map.94 = (bf16[1024,128]{1,0:T(8,128)(2,1)S(1)}, bf16[128,1024]{1,0:T(8,128)(2,1)S(1)}, bf16[1024,128]{1,0:T(8,128)(2,1)S(1)}, bf16[1024,128]{1,0:T(8,128...) custom-call(bf16[1024,128]{1,0:T(8,128)(2,1)} %bitcast.8, ...), custom_call_target="tpu_custom_call" | custom-call | flops 16777216 | bytes 2097152 | tf_op jit(solution)/shard_map/pallas_call | solution.py:558
  14.2 0.1 collective-permute-start
  14.2 0.7 %shard_map.95.x = bf16[256,4096]{1,0:T(8,128)(2,1)S(1)} custom-call(bf16[128,1024]{1,0:T(8,128)(2,1)S(1)} %get-tuple-element.38.basis_lanes, bf16[1024,128]{1,0:T(8,128)(2,1)S(1)} %get-tuple-element.39.sketch_t), custom_call_target="tpu_custom_call" | custom-call | flops 16777216 | bytes 2097152 | tf_op jit(solution)/shard_map/pallas_call | solution.py:558
  14.9 0.5 %collective-permute-done.site_other = bf16[1,4096]{1,0:T(2,128)(2,1)S(1)} collective-permute-done((bf16[1,4096]{1,0:T(2,128)(2,1)S(1)}, bf16[1,4096]{1,0:T(2,128)(2,1)S(1)}, u32[]{:S(2)}, u32[]{:S(2)}) %collective-permute-start) | collective-permute-done | bytes 8224 | tf_op jit(solution)/shard_map/ppermute | solution.py:583
  15.4 1.8 %shard_map.96 = (bf16[256,256]{1,0:T(8,128)(2,1)S(1)}, bf16[256,256]{1,0:T(8,128)(2,1)S(1)}, bf16[1024,1024]{1,0:T(8,128)(2,1)S(1)}) custom-call(bf16[256,4096]{1,0:T(8,128)(2,1)S(1)} %shard_map.95.x, bf16[1,4096]{1,0:T(2,128)(2,1)S(1)} %collective-permute-done.site_other, bf16[256,64]{1,0:T(8,128)(2,1)S(1)} %get-tuple-element.42.own_upper, ...), custom_call_target="tpu_custom_call" | custom-call | flops 16777216 | bytes 2097152 | tf_op jit(solution)/shard_map/pallas_call | solution.py:558
  17.3 0.0 collective-permute-done.1.western
  17.3 0.0 collective-permute-done.2.eastern
  17.3 0.2 collective-permute-start.3
  17.5 0.3 %collective-permute-start.4 = (bf16[1024,128]{1,0:T(8,128)(2,1)S(1)}, bf16[1024,128]{1,0:T(8,128)(2,1)S(1)}, u32[]{:S(2)}, u32[]{:S(2)}) collective-permute-start(bf16[1024,128]{1,0:T(8,128)(2,1)S(1)} %collective-permute-done.2.eastern), channel_id=1, source_target_pairs={{0,1},{1,0},{2,3},{3,2},{4,5},{5,4},{6,7},{7,6},{8,9},{9,8},{10,11... | collective-permute-start | bytes 786440 | tf_op jit(solution)/shard_map/ppermute | solution.py:583
  17.9 2.1 %shard_map.97 = (bf16[256,4096]{1,0:T(8,128)(2,1)S(1)}, bf16[1024,128]{1,0:T(8,128)(2,1)S(1)}, bf16[1024,128]{1,0:T(8,128)(2,1)S(1)}) custom-call(bf16[1024,128]{1,0:T(8,128)(2,1)S(1)} %get-tuple-element.47.first, bf16[1024,128]{1,0:T(8,128)(2,1)S(1)} %collective-permute-done.1.western, bf16[1024,128]{1,0:T(8,128)(2,1)S(1)} %collective-permute-done.2.eastern, ...), custom_call_target="tpu_custom_call" | custom-call | flops 4294967296 | bytes 2097152 | tf_op jit(solution)/shard_map/pallas_call | solution.py:558
  20.0 0.0 collective-permute-done.3.western_other
  20.0 0.0 collective-permute-done.4.eastern_other
  20.0 0.2 collective-permute-start.6
  20.3 7.2 %shard_map.98 = (bf16[1024,128]{1,0:T(8,128)(2,1)S(1)}, bf16[1024,128]{1,0:T(8,128)(2,1)S(1)}) custom-call(bf16[1024,128]{1,0:T(8,128)(2,1)S(1)} %get-tuple-element.35.basis, bf16[1024,128]{1,0:T(8,128)(2,1)S(1)} %get-tuple-element.36.edge, bf16[1024,1024]{1,0:T(8,128)(2,1)S(1)} %get-tuple-element.52.sketched, ...), custom_call_target="tpu_custom_call" | custom-call | flops 8589934592 | bytes 2097152 | tf_op jit(solution)/shard_map/pallas_call | solution.py:558
  27.4 0.4 %collective-permute-start.5 = (bf16[1024,128]{1,0:T(8,128)(2,1)S(1)}, bf16[1024,128]{1,0:T(8,128)(2,1)S(1)}, u32[]{:S(2)}, u32[]{:S(2)}) collective-permute-start(bf16[1024,128]{1,0:T(8,128)(2,1)S(1)} %get-tuple-element.57), channel_id=1, source_target_pairs={{0,1},{1,0},{2,3},{3,2},{4,5},{5,4},{6,7},{7,6},{8,9},{9,8},{10,11... | collective-permute-start | bytes 786440 | tf_op jit(solution)/shard_map/ppermute | solution.py:583
  27.8 0.0 collective-permute-done.6.carried
  27.8 1.4 %shard_map.99.product = f32[256,256]{1,0:T(8,128)S(1)} custom-call(bf16[256,4096]{1,0:T(8,128)(2,1)S(1)} %get-tuple-element.58.x_first, bf16[1024,128]{1,0:T(8,128)(2,1)S(1)} %get-tuple-element.59.back, bf16[1024,128]{1,0:T(8,128)(2,1)S(1)} %collective-permute-done.6.carried), custom_call_target="tpu_custom_call" | custom-call | flops 2147483648 | bytes 2097152 | tf_op jit(solution)/shard_map/pallas_call | solution.py:558
  29.3 0.0 collective-permute-done.5.received
  29.3 1.3 %shard_map.100 = (f32[2,4096]{1,0:T(2,128)}, bf16[1024,128]{1,0:T(8,128)(2,1)}, bf16[1024,128]{1,0:T(8,128)(2,1)}) custom-call(f32[256,256]{1,0:T(8,128)S(1)} %shard_map.99.product, s32[1,1]{1,0:T(1,128)S(6)} %copy.10.choice, bf16[1024,128]{1,0:T(8,128)(2,1)S(1)} %get-tuple-element.62.keep, bf16[1024,128]{1,0:T(8,128)(2,1)S(1)} %collective-permute-done.5.received), custom_call_target="tpu_custom_call" | custom-call | flops 1073741824 | bytes 2097152 | tf_op jit(solution)/shard_map/pallas_call | solution.py:558
Async XLA Ops:
  0.6 16.6 %collective-permute-start.1 = (bf16[1024,128]{1,0:T(8,128)(2,1)}, bf16[1024,128]{1,0:T(8,128)(2,1)S(1)}, u32[]{:S(2)}, u32[]{:S(2)}) collective-permute-start(bf16[1024,128]{1,0:T(8,128)(2,1)} %bitcast.11), channel_id=1, source_target_pairs={{0,2},{2,4},{4,6},{6,8},{8,10},{10,12},{12,14},{14,0},{1,3},{3,5},... | collective-permute-start | bytes 786440 | tf_op jit(solution)/shard_map/ppermute | solution.py:579
  3.6 13.7 %collective-permute-start.2 = (bf16[1024,128]{1,0:T(8,128)(2,1)}, bf16[1024,128]{1,0:T(8,128)(2,1)S(1)}, u32[]{:S(2)}, u32[]{:S(2)}) collective-permute-start(bf16[1024,128]{1,0:T(8,128)(2,1)} %bitcast.12), channel_id=1, source_target_pairs={{0,14},{2,0},{4,2},{6,4},{8,6},{10,8},{12,10},{14,12},{1,15},{3,1}... | collective-permute-start | bytes 786440 | tf_op jit(solution)/shard_map/ppermute | solution.py:579
  14.2 1.2 %collective-permute-start = (bf16[1,4096]{1,0:T(2,128)(2,1)S(1)}, bf16[1,4096]{1,0:T(2,128)(2,1)S(1)}, u32[]{:S(2)}, u32[]{:S(2)}) collective-permute-start(bf16[1,4096]{1,0:T(2,128)(2,1)S(1)} %get-tuple-element.37), channel_id=1, source_target_pairs={{0,1},{1,0},{2,3},{3,2},{4,5},{5,4},{6,7},{7,6},{8,9},{9,8},{10,11... | collective-permute-start | bytes 24584 | tf_op jit(solution)/shard_map/ppermute | solution.py:583
  17.3 2.7 %collective-permute-start.3 = (bf16[1024,128]{1,0:T(8,128)(2,1)S(1)}, bf16[1024,128]{1,0:T(8,128)(2,1)S(1)}, u32[]{:S(2)}, u32[]{:S(2)}) collective-permute-start(bf16[1024,128]{1,0:T(8,128)(2,1)S(1)} %collective-permute-done.1.western), channel_id=1, source_target_pairs={{0,1},{1,0},{2,3},{3,2},{4,5},{5,4},{6,7},{7,6},{8,9},{9,8},{10,11... | collective-permute-start | bytes 786440 | tf_op jit(solution)/shard_map/ppermute | solution.py:583
  17.5 2.5 %collective-permute-start.4 = (bf16[1024,128]{1,0:T(8,128)(2,1)S(1)}, bf16[1024,128]{1,0:T(8,128)(2,1)S(1)}, u32[]{:S(2)}, u32[]{:S(2)}) collective-permute-start(bf16[1024,128]{1,0:T(8,128)(2,1)S(1)} %collective-permute-done.2.eastern), channel_id=1, source_target_pairs={{0,1},{1,0},{2,3},{3,2},{4,5},{5,4},{6,7},{7,6},{8,9},{9,8},{10,11... | collective-permute-start | bytes 786440 | tf_op jit(solution)/shard_map/ppermute | solution.py:583
  20.0 7.8 %collective-permute-start.6 = (bf16[1024,128]{1,0:T(8,128)(2,1)S(1)}, bf16[1024,128]{1,0:T(8,128)(2,1)S(1)}, u32[]{:S(2)}, u32[]{:S(2)}) collective-permute-start(bf16[1024,128]{1,0:T(8,128)(2,1)S(1)} %get-tuple-element.60), channel_id=1, source_target_pairs={{0,1},{1,0},{2,3},{3,2},{4,5},{5,4},{6,7},{7,6},{8,9},{9,8},{10,11... | collective-permute-start | bytes 786440 | tf_op jit(solution)/shard_map/ppermute | solution.py:583
  27.4 1.8 %collective-permute-start.5 = (bf16[1024,128]{1,0:T(8,128)(2,1)S(1)}, bf16[1024,128]{1,0:T(8,128)(2,1)S(1)}, u32[]{:S(2)}, u32[]{:S(2)}) collective-permute-start(bf16[1024,128]{1,0:T(8,128)(2,1)S(1)} %get-tuple-element.57), channel_id=1, source_target_pairs={{0,1},{1,0},{2,3},{3,2},{4,5},{5,4},{6,7},{7,6},{8,9},{9,8},{10,11... | collective-permute-start | bytes 786440 | tf_op jit(solution)/shard_map/ppermute | solution.py:583
